TPU v7x, 32 devices: a whole 2x2x4 slice. The times are simulated.
32 devices in a mesh: batch: 8 (over z, y), head: 4 (over x, core).
Axes of the slice: x: 2, y: 2, z: 4, core: 2. Of those that a mesh axis runs over, the one named last changes fastest.
Arguments:
- post_stream: bfloat16 [32768, 512], P(('batch', 'head')), may hold values from -6 to 6
- dual_stream: float32 [32768, 512], P(('batch', 'head')), may hold values from -12 to 12
- post_cotangent: bfloat16 [32768, 512], P(('batch', 'head')), may hold values from -6 to 6
- dual_cotangent: bfloat16 [32768, 512], P(('batch', 'head')), may hold values from -6 to 6
- seq_lengths: int32 [32], P('batch'), may hold values from 64 to 1024, as said below
- owner_slots: int32 [8], replicated, may hold values from 0 to 7, each once
- weights: float32 [512, 6144], P('batch', 'head')
- first_moment: float32 [512, 6144], P('batch', 'head'), as said below
- second_moment: float32 [512, 6144], P('batch', 'head'), as said below
- norm_gain: float32 [2, 512], replicated, may hold values from 0.5 to 1.5
- norm_bias: float32 [2, 512], replicated, may hold values from -2 to 2
- norm_first: float32 [4, 512], replicated, may hold values from -80 to 80
- norm_second: float32 [4, 512], replicated, may hold values from 19.6608 to 78.6432
Outputs:
- post_out: bfloat16 [32768, 512], P(('batch', 'head'))
- dual_out: float32 [32768, 512], P(('batch', 'head'))
- post_grad: float32 [32768, 512], P(('batch', 'head'))
- new_first: float32 [512, 6144], P('batch', 'head')
- new_second: float32 [512, 6144], P('batch', 'head')
- new_weights: float32 [512, 6144], P('batch', 'head')
- norm_first_out: float32 [4, 512], replicated
- norm_second_out: float32 [4, 512], replicated
- norm_out: float32 [4, 512], replicated
Inputs may be any that keep to these rules, and one draw needn't show every extreme that they name: `seq_lengths`: in each aligned group of 4 sequences (those of one batch index) one sequence has all 1024 tokens valid. `owner_slots`: each row block owned by exactly one batch index. `first_moment`: entries of both signs. `second_moment`: entries positive.
All inputs are finite; a program needn't handle non-finite values.
Results may differ from a plain program's by a relative error of at most 0.023.
Values may be sent and summed in bfloat16 or wider, within the bound.
A program may use at most 192 MiB of HBM per device.

v0:
```python
import jax
import jax.numpy as jnp
from jax import lax
from jax.sharding import PartitionSpec as P

D = 512
FF = 2048
NHEADS = 8
DH = 64
SEQ_LEN = 1024
STEP = 10
GROUPW = 768


BETA_FIRST = 0.9
BETA_SECOND = 0.999
ADAM_EPSILON = 1e-08
WEIGHT_DECAY = 0.1
WEIGHT_RATE = 0.2
NORM_RATE = 0.2
NORM_EPSILON = 1e-05
MASK_VALUE = -1000000000.0


def layer_norm_parts(value, gain_row, bias_row):
    average = jnp.mean(value, axis=-1, keepdims=True)
    centred = value - average
    variance = jnp.mean(centred * centred, axis=-1, keepdims=True)
    reciprocal = lax.rsqrt(variance + NORM_EPSILON)
    normed = centred * reciprocal
    return (normed * gain_row + bias_row, normed, reciprocal)


def layer_norm_back(grad_out, normed, reciprocal, gain_row):
    grad_normed = grad_out * gain_row
    centre_term = jnp.mean(grad_normed, axis=-1, keepdims=True)
    slope_term = jnp.mean(grad_normed * normed, axis=-1, keepdims=True)
    grad_input = reciprocal * (grad_normed - centre_term - normed * slope_term)
    return (grad_input, jnp.sum(grad_out * normed, axis=0), jnp.sum(grad_out, axis=0))


def gelu_exact(value):
    return jax.nn.gelu(value, approximate=False)


def masked_scores(queries, key_rows, length):
    scores = jnp.einsum(
        "qgd,kgd->gqk", queries, key_rows, preferred_element_type=jnp.float32
    ) * DH ** (-0.5)
    kept_keys = jnp.arange(SEQ_LEN, dtype=jnp.int32) < length
    return jnp.where(kept_keys[None, None, :], scores, MASK_VALUE)


def attend_forward(sequence_block):
    queries, key_rows, value_rows, length = sequence_block
    scores = masked_scores(queries, key_rows, length)
    maximum = jnp.max(scores, axis=-1, keepdims=True)
    exponent = jnp.exp(scores - maximum)
    row_total = jnp.sum(exponent, axis=-1, keepdims=True)
    soft_weights = (exponent / row_total).astype(jnp.bfloat16)
    attended = jnp.einsum(
        "gqk,kgd->qgd", soft_weights, value_rows, preferred_element_type=jnp.float32
    )
    return (attended.astype(jnp.bfloat16), (maximum + jnp.log(row_total))[:, :, 0])


def attend_backward(sequence_block):
    queries, key_rows, value_rows, length, log_total, grad_attended = sequence_block
    scores = masked_scores(queries, key_rows, length)
    soft_weights = jnp.exp(scores - log_total[:, :, None])
    grad_soft = jnp.einsum(
        "qgd,kgd->gqk", grad_attended, value_rows, preferred_element_type=jnp.float32
    )
    grad_values = jnp.einsum(
        "gqk,qgd->kgd",
        soft_weights.astype(jnp.bfloat16),
        grad_attended,
        preferred_element_type=jnp.float32,
    )
    row_inner = jnp.sum(soft_weights * grad_soft, axis=-1, keepdims=True)
    grad_scores = (soft_weights * (grad_soft - row_inner)).astype(jnp.bfloat16)
    grad_queries = jnp.einsum(
        "gqk,kgd->qgd", grad_scores, key_rows, preferred_element_type=jnp.float32
    ) * DH ** (-0.5)
    grad_keys = jnp.einsum(
        "gqk,qgd->kgd", grad_scores, queries, preferred_element_type=jnp.float32
    ) * DH ** (-0.5)
    return jnp.concatenate([grad_queries, grad_keys, grad_values], axis=-1).astype(jnp.bfloat16)


def adam_update(param, grad, first, second, rate, decay):
    first_new = BETA_FIRST * first + (1.0 - BETA_FIRST) * grad
    second_new = BETA_SECOND * second + (1.0 - BETA_SECOND) * grad * grad
    first_hat = first_new / (1.0 - BETA_FIRST**STEP)
    second_hat = second_new / (1.0 - BETA_SECOND**STEP)
    param_new = param - rate * (first_hat / (jnp.sqrt(second_hat) + ADAM_EPSILON) + decay * param)
    return (first_new, second_new, param_new)


def shards(
    post_stream,
    dual_stream,
    post_cotangent,
    dual_cotangent,
    seq_lengths,
    owner_slots,
    weights,
    first_moment,
    second_moment,
    norm_gain,
    norm_bias,
    norm_first,
    norm_second,
):
    batches = lax.axis_size("batch")
    head_devices = lax.axis_size("head")
    tok_rows = post_stream.shape[0]
    row_block = D // batches
    groups_here = NHEADS // head_devices
    hidden_group = FF // NHEADS
    group_count = tok_rows * head_devices
    seq_count = seq_lengths.shape[0]
    slot_ids = jnp.arange(batches, dtype=jnp.int32)
    matches = owner_slots[None, :] == slot_ids[:, None]
    inverse = jnp.sum(jnp.where(matches, slot_ids[None, :], 0), axis=1)

    def to_slots(value):
        return jnp.take(value.reshape(value.shape[0], batches, row_block), owner_slots, axis=1)

    def from_slots(value):
        return jnp.take(value, inverse, axis=1).reshape(value.shape[0], D)

    local_block = weights.astype(jnp.bfloat16).reshape(row_block, groups_here, GROUPW)
    qkv_part = local_block[:, :, : 3 * DH]
    out_part = local_block[:, :, 3 * DH : 4 * DH]
    feed_part = local_block[:, :, 4 * DH :]
    feed_all = lax.all_gather(feed_part, ("batch", "head"), axis=0, tiled=True)
    qkv_all, out_all = (
        lax.all_gather(qkv_part, "batch", axis=0, tiled=True),
        lax.all_gather(out_part, "batch", axis=0, tiled=True),
    )
    out_all = out_all.reshape(batches, row_block, groups_here, DH)
    qkv_all = qkv_all.reshape(batches, row_block, groups_here, 3 * DH)
    feed_all = feed_all.reshape(batches, head_devices, row_block, groups_here, 2, hidden_group)
    w_up = feed_all[:, :, :, :, 0, :]
    w_down = feed_all[:, :, :, :, 1, :]
    group_tokens = lax.all_gather(post_stream, "head", axis=0, tiled=True)
    group_slots = to_slots(group_tokens)
    projected = jnp.einsum(
        "tbr,brgc->tgc", group_slots, qkv_all, preferred_element_type=jnp.float32
    ).astype(jnp.bfloat16)
    seq_shape = (seq_count, SEQ_LEN, groups_here, DH)
    queries = projected[:, :, :DH].reshape(seq_shape)
    key_rows = projected[:, :, DH : 2 * DH].reshape(seq_shape)
    value_rows = projected[:, :, 2 * DH :].reshape(seq_shape)
    attended, log_total = lax.map(attend_forward, (queries, key_rows, value_rows, seq_lengths))
    attended = attended.reshape(group_count, groups_here, DH)
    branch_part = from_slots(
        jnp.einsum("tgd,brgd->tbr", attended, out_all, preferred_element_type=jnp.float32)
    )
    branch = lax.psum_scatter(
        branch_part.astype(jnp.bfloat16), "head", scatter_dimension=0, tiled=True
    ).astype(jnp.float32)
    post_float = post_stream.astype(jnp.float32)
    middle, middle_normed, middle_recip = layer_norm_parts(
        post_float + branch, norm_gain[0], norm_bias[0]
    )
    dual_middle = dual_stream + branch
    middle_slots = to_slots(middle.astype(jnp.bfloat16))
    hidden_pre = jnp.einsum(
        "tbr,bhrgc->thgc", middle_slots, w_up, preferred_element_type=jnp.float32
    )
    hidden = gelu_exact(hidden_pre).astype(jnp.bfloat16)
    feed = from_slots(
        jnp.einsum("thgc,bhrgc->tbr", hidden, w_down, preferred_element_type=jnp.float32)
    )
    post_new, out_normed, out_recip = layer_norm_parts(middle + feed, norm_gain[1], norm_bias[1])
    dual_new = dual_middle + feed
    positions = lax.axis_index("head") * tok_rows + jnp.arange(tok_rows, dtype=jnp.int32)
    seq_of = positions // SEQ_LEN
    length_row = jnp.sum(
        jnp.where(
            seq_of[:, None] == jnp.arange(seq_count, dtype=jnp.int32)[None, :],
            seq_lengths[None, :],
            0,
        ),
        axis=1,
    )
    valid = (positions % SEQ_LEN < length_row).astype(jnp.float32)[:, None]
    grad_out = post_cotangent.astype(jnp.float32) * valid
    grad_dual = dual_cotangent.astype(jnp.float32) * valid
    grad_out_pre, gain_grad_two, bias_grad_two = layer_norm_back(
        grad_out, out_normed, out_recip, norm_gain[1]
    )
    grad_feed_slots = to_slots((grad_out_pre + grad_dual).astype(jnp.bfloat16))
    grad_down = jnp.einsum(
        "tbr,thgc->bhrgc", grad_feed_slots, hidden, preferred_element_type=jnp.float32
    )
    grad_hidden = jnp.einsum(
        "tbr,bhrgc->thgc", grad_feed_slots, w_down, preferred_element_type=jnp.float32
    )
    gelu_values, gelu_pullback = jax.vjp(gelu_exact, hidden_pre)
    grad_hidden_pre = gelu_pullback(grad_hidden)[0].astype(jnp.bfloat16)
    grad_up = jnp.einsum(
        "tbr,thgc->bhrgc", middle_slots, grad_hidden_pre, preferred_element_type=jnp.float32
    )
    grad_middle = grad_out_pre + from_slots(
        jnp.einsum("thgc,bhrgc->tbr", grad_hidden_pre, w_up, preferred_element_type=jnp.float32)
    )
    grad_mid_pre, gain_grad_one, bias_grad_one = layer_norm_back(
        grad_middle, middle_normed, middle_recip, norm_gain[0]
    )
    grad_branch = (grad_mid_pre + grad_dual).astype(jnp.bfloat16)
    branch_group = lax.all_gather(grad_branch, "head", axis=0, tiled=True)
    branch_slots = to_slots(branch_group)
    grad_out_proj = jnp.einsum(
        "tbr,tgd->brgd", branch_slots, attended, preferred_element_type=jnp.float32
    )
    grad_attended = jnp.einsum(
        "tbr,brgd->tgd", branch_slots, out_all, preferred_element_type=jnp.float32
    ).astype(jnp.bfloat16)
    grad_seq = grad_attended.reshape(seq_shape)
    grad_projected = lax.map(
        attend_backward, (queries, key_rows, value_rows, seq_lengths, log_total, grad_seq)
    )
    grad_projected = grad_projected.reshape(group_count, groups_here, 3 * DH)
    grad_qkv = jnp.einsum(
        "tbr,tgc->brgc", group_slots, grad_projected, preferred_element_type=jnp.float32
    )
    grad_group_in = from_slots(
        jnp.einsum("tgc,brgc->tbr", grad_projected, qkv_all, preferred_element_type=jnp.float32)
    )
    post_grad = grad_mid_pre + lax.psum_scatter(
        grad_group_in.astype(jnp.bfloat16), "head", scatter_dimension=0, tiled=True
    ).astype(jnp.float32)
    qkv_sum = lax.psum_scatter(
        grad_qkv.reshape(batches * row_block, groups_here, 3 * DH).astype(jnp.bfloat16),
        "batch",
        scatter_dimension=0,
        tiled=True,
    ).astype(jnp.float32)
    feed_grads = jnp.stack([grad_up, grad_down], axis=4).reshape(
        batches * head_devices * row_block, groups_here, 2 * hidden_group
    )
    feed_sum = lax.psum_scatter(feed_grads, ("batch", "head"), scatter_dimension=0, tiled=True)
    out_sum = lax.psum_scatter(
        grad_out_proj.reshape(batches * row_block, groups_here, DH).astype(jnp.bfloat16),
        "batch",
        scatter_dimension=0,
        tiled=True,
    ).astype(jnp.float32)
    weight_grad = jnp.concatenate([qkv_sum, out_sum, feed_sum], axis=2).reshape(
        row_block, groups_here * GROUPW
    )
    new_first, new_second, new_weights = adam_update(
        weights, weight_grad, first_moment, second_moment, WEIGHT_RATE, WEIGHT_DECAY
    )
    norm_local = jnp.stack([gain_grad_one, gain_grad_two, bias_grad_one, bias_grad_two], axis=0)
    norm_grads = lax.psum(norm_local, ("batch", "head"))
    norm_params = jnp.concatenate([norm_gain, norm_bias], axis=0)
    norm_first_out, norm_second_out, norm_out = adam_update(
        norm_params, norm_grads, norm_first, norm_second, NORM_RATE, 0.0
    )
    return (
        post_new.astype(jnp.bfloat16),
        dual_new,
        post_grad,
        new_first,
        new_second,
        new_weights,
        norm_first_out,
        norm_second_out,
        norm_out,
    )


def solution(mesh):
    in_specs = (
        P(("batch", "head"), None),
        P(("batch", "head"), None),
        P(("batch", "head"), None),
        P(("batch", "head"), None),
        P("batch"),
        P(),
        P("batch", "head"),
        P("batch", "head"),
        P("batch", "head"),
        P(),
        P(),
        P(),
        P(),
    )
    out_specs = (
        P(("batch", "head"), None),
        P(("batch", "head"), None),
        P(("batch", "head"), None),
        P("batch", "head"),
        P("batch", "head"),
        P("batch", "head"),
        P(),
        P(),
        P(),
    )
    return jax.shard_map(shards, mesh=mesh, in_specs=in_specs, out_specs=out_specs, check_vma=False)
```

profile of v0, /device:TPU:0, one launch (start us, length us, event | category | flops | bytes accessed | tf_op | source)
XLA Modules:
  0.0 671.9 jit_solution(4526344999371096587)
XLA Ops:
  7.2 2.3 copy.184
  11.9 33.1 %all_gather.16 = bf16[512,2,192]{2,1,0:T(2,128)(2,1)S(1)} all-gather(bf16[64,2,192]{2,1,0:T(2,128)(2,1)S(1)} %slice.66), channel_id=1, replica_groups=mesh['batch'=8,'head'=4] {'batch'}, dimensions={0}, use_global_device_ids=true | all-gather | bytes 442368 | tf_op jit(solution)/shard_map/all_gather | solution.py:139
  45.0 30.8 %all_gather.17 = bf16[512,2,64]{2,1,0:T(2,128)(2,1)S(1)} all-gather(bf16[64,2,64]{2,1,0:T(2,128)(2,1)S(1)} %slice.70), channel_id=1, replica_groups=mesh['batch'=8,'head'=4] {'batch'}, dimensions={0}, use_global_device_ids=true | all-gather | bytes 147456 | tf_op jit(solution)/shard_map/all_gather | solution.py:140
  75.9 5.0 gather_fusion
  80.9 2.7 broadcast_select_fusion.1
  86.5 34.9 %while.22 = (s32[]{:T(128)}, bf16[4,1024,2,64]{1,3,2,0:T(8,128)(2,1)}, f32[4,2,1024]{2,1,0:T(2,128)}, bf16[4,1024,2,64]{1,3,2,0:T(8,128)(2,1)S(1)}, s32[4]{0:T(1...) while((s32[]{:T(128)}, ...), condition=%wide.region_3.5_spmd, body=%wide.region_0.4_spmd.sunk | while | flops 562166784 | bytes 26286692 | solution.py:156
  89.4 2.3 fusion.161
  92.4 2.9 fusion.162
  98.1 2.3 fusion.161
  101.1 2.9 fusion.162
  106.8 2.3 fusion.161
  109.8 2.9 fusion.162
  115.5 2.3 fusion.161
  118.5 2.9 fusion.162
  121.4 3.8 copy.190
  125.2 2.6 reshape.365
  127.8 4.5 convolution_bitcast_fusion.1
  132.3 5.0 gather_fusion.1
  137.3 5.3 bitcast_convert_fusion.1
  147.4 2.3 copy.198
  149.9 11.8 %reshape.382 = bf16[8,4,64,2,2,256]{5,4,3,2,1,0:T(2,128)(2,1)} reshape(bf16[2048,2,512]{2,1,0:T(2,128)(2,1)} %all-gather.6.cloned.1.call-done) | data formatting | bytes 8388608 | tf_op jit(solution)/shard_map/reshape | solution.py:144
  161.7 10.3 %fusion.130 = (bf16[8,4,64,2,1,256]{5,4,3,2,1,0:T(2,128)(2,1)}, bf16[8,4,64,2,1,256]{5,4,3,2,1,0:T(2,128)(2,1)}) fusion(bf16[8,4,64,2,2,256]{5,4,3,2,1,0:T(2,128)(2,1)} %reshape.382), kind=kLoop, calls=%fused_computation.222 | loop fusion | bytes 8388608 | tf_op jit(solution)/shard_map/slice | solution.py:145
  172.0 16.4 %reduce-scatter.6.cloned.1.call-done = bf16[1024,512]{0,1:T(8,128)(2,1)} async-done(((bf16[4096,512]{0,1:T(8,128)(2,1)}), bf16[1024,512]{0,1:T(8,128)(2,1)}) %reduce-scatter.6.cloned.1.call-update) | async-done | bytes 1048592 | tf_op jit(solution)/shard_map/reduce_scatter | solution.py:161
  192.9 24.1 %multiply_convert_fusion.1 = (bf16[1024,4,2,256]{3,0,2,1:T(8,128)(2,1)S(1)}, f32[1024,4,2,256]{3,0,2,1:T(8,128)}, f32[1024,4,2,256,1]{3,0,4,2,1:T(8,128)}) fusion(bf16[8,4,64,2,1,256]{5,4,3,2,1,0:T(2,128)(2,1)} %get-tuple-element.284, bf16[8,1024,64]{1,2,0:T(8,128)(2,1)S(1)} %gather_fusion.2, pred[8]{0:T(512)(128)(4,1)S(1)} %compare_and_fusion.1), kind=kOutput, calls=%fused_computation.87 | convolution fusion | flops 2284322816 | bytes 24117256 | tf_op jit(solution)/shard_map/tbr,bhrgc->thgc/dot_general | solution.py:170
  219.1 3.7 fusion.99
  222.8 2.3 gather_fusion.3
  233.0 2.8 gather_fusion.4
  235.8 10.1 %fusion.60 = bf16[1024,4,2,256]{3,0,2,1:T(8,128)(2,1)S(1)} fusion(f32[1024,4,2,256]{3,0,2,1:T(8,128)} %get-tuple-element.279, f32[1024,4,2,256,1]{3,0,4,2,1:T(8,128)} %get-tuple-element.295, bf16[8,4,64,2,1,256]{5,4,3,2,1,0:T(2,128)(2,1)} %get-tuple-element.285, bf16[8,1024,64]{1,2,0:T(8,128)(2,1)} %gather_fusion.4, pred[8]{0:T(512)(128)(4,1)S(1)} %compare_and_fusion.1), kind=kOutput, calls=%fused_computation.81 | convolution fusion | flops 2177368064 | bytes 24117256 | tf_op jit(solution)/shard_map/tbr,bhrgc->thgc/dot_general | solution.py:199
  247.9 3.7 fusion.102
  251.6 3.6 gather_fusion.5
  257.4 4.0 multiply_reduce_fusion.2
  266.4 33.3 %all-gather.8.cloned.1.call-done = bf16[4096,512]{0,1:T(8,128)(2,1)} async-done(((bf16[1024,512]{0,1:T(8,128)(2,1)}), bf16[4096,512]{0,1:T(8,128)(2,1)}) %all-gather.8.cloned.1.call-update) | async-done | bytes 4194320 | tf_op jit(solution)/shard_map/all_gather | solution.py:214
  299.6 5.0 gather_fusion.6
  304.6 2.7 broadcast_select_fusion
  312.4 63.0 %while.23 = (s32[]{:T(128)}, bf16[4,1024,2,192]{1,3,2,0:T(8,128)(2,1)}, bf16[4,1024,2,64]{1,3,2,0:T(8,128)(2,1)S(1)}, s32[4]{0:T(128)S(1)}, bf16[4,1024,2,64]{1,...) while((s32[]{:T(128)}, ...), condition=%wide.region_17.22_spmd, body=%wide.region_15.21_spmd.sunk | while | flops 1376648192 | bytes 67172992 | solution.py:223
  315.7 3.5 multiply_reduce_fusion.9
  319.2 3.1 multiply_convert_fusion.3
  324.6 2.7 fusion.172
  331.5 3.5 multiply_reduce_fusion.9
  335.0 3.1 multiply_convert_fusion.3
  340.3 2.7 fusion.172
  347.2 3.5 multiply_reduce_fusion.9
  350.7 3.1 multiply_convert_fusion.3
  356.1 2.7 fusion.172
  362.9 3.5 multiply_reduce_fusion.9
  366.4 3.1 multiply_convert_fusion.3
  371.8 2.7 fusion.172
  375.4 4.3 copy.206
  379.7 4.0 copy.245
  383.7 4.2 reshape.377
  388.0 6.5 convolution_bitcast_fusion
  394.5 3.2 convolution_convert_fusion
  397.7 5.1 gather_fusion.7
  402.9 5.3 bitcast_convert_fusion
  409.4 4.9 fusion.83
  414.3 2.5 fusion.80
  418.0 8.0 %copy.208 = f32[8,4,64,2,2,256]{5,4,2,1,0,3:T(2,128)} copy(f32[8,4,64,2,2,256]{5,2,0,3,1,4:T(8,128)S(1)} %pad_maximum_fusion) | data formatting | bytes 16777216 | tf_op jit(solution)/shard_map/stack | solution.py:242
  426.0 11.6 %reshape.273 = f32[2048,2,512]{2,0,1:T(8,128)} reshape(f32[8,4,64,2,2,256]{5,4,2,1,0,3:T(2,128)} %copy.208) | data formatting | bytes 16777216 | tf_op jit(solution)/shard_map/reshape | solution.py:242
  440.1 2.9 copy.211
  443.1 39.6 %psum.7 = f32[4,512]{1,0:T(4,128)S(1)} all-reduce(f32[4,512]{1,0:T(4,128)S(1)} %pad_maximum_fusion.1), channel_id=1, replica_groups=mesh['batch'=8,'head'=4] {'batch','head'}, use_global_device_ids=true, to_apply=%region_26.31 | all-reduce | flops 2048 | bytes 16384 | tf_op jit(solution)/shard_map/psum | solution.py:259
  484.9 26.2 %reduce-scatter.8.cloned.1.call-done = bf16[1024,512]{0,1:T(8,128)(2,1)} async-done(((bf16[4096,512]{0,1:T(8,128)(2,1)}), bf16[1024,512]{0,1:T(8,128)(2,1)}) %reduce-scatter.8.cloned.1.call-update) | async-done | bytes 1048592 | tf_op jit(solution)/shard_map/reduce_scatter | solution.py:233
  511.1 4.2 convert_add_fusion.2
  515.3 3.0 copy.212
  518.3 144.0 %reduce-scatter.14.cloned.1.call-done = f32[64,2,512]{2,0,1:T(8,128)} async-done(((f32[2048,2,512]{2,0,1:T(8,128)}), f32[64,2,512]{2,0,1:T(8,128)}) %reduce-scatter.14.cloned.1.call-update) | async-done | bytes 262160 | tf_op jit(solution)/shard_map/reduce_scatter | solution.py:245
  (247 shorter events, 87.6 us)
Async XLA Ops:
  7.2 4.3 copy-start.58
  7.2 68.7 %all-gather.4.cloned.1.call-start = ((), (), s32[]{:S(2)}) async-start(), calls=%async_computation.5 | async-start | bytes 5242880 | tf_op jit(solution)/shard_map/all_gather | solution.py:147
  9.5 140.3 %all-gather.6.cloned.1.call-start = ((), (), s32[]{:S(2)}) async-start(), calls=%async_computation.7 | async-start | bytes 4325376 | tf_op jit(solution)/shard_map/all_gather | solution.py:137
  11.4 176.9 %reduce-scatter.6.cloned.1.call-start = ((), (), s32[]{:S(2)}) async-start(), calls=%async_computation.6 | async-start | bytes 5242880 | tf_op jit(solution)/shard_map/reduce_scatter | solution.py:161
  11.5 293.1 %copy-start.55 = (pred[8]{0:T(512)(128)(4,1)}, pred[8]{0:T(512)(128)(4,1)S(1)}, u32[]{:S(2)}) copy-start(pred[8]{0:T(512)(128)(4,1)S(1)} %compare_and_fusion.1) | copy-start | bytes 28
  11.8 243.4 %copy-start.47 = (pred[8]{0:T(512)(128)(4,1)}, pred[8]{0:T(512)(128)(4,1)S(1)}, u32[]{:S(2)}) copy-start(pred[8]{0:T(512)(128)(4,1)S(1)} %compare_and_fusion) | copy-start | bytes 28
  45.0 38.5 %copy-start.29 = (bf16[512,2,192]{2,0,1:T(8,128)(2,1)}, bf16[512,2,192]{2,0,1:T(8,128)(2,1)S(1)}, u32[]{:S(2)}) copy-start(bf16[512,2,192]{2,0,1:T(8,128)(2,1)S(1)} %copy.186) | copy-start | bytes 1179652
  75.9 175.8 %copy-start.46 = (s32[1024]{0:T(1024)}, s32[1024]{0:T(1024)S(1)}, u32[]{:S(2)}) copy-start(s32[1024]{0:T(1024)S(1)} %pad_clamp_fusion) | copy-start | bytes 12292
  83.6 2.0 copy-start.18
  121.4 10.9 %copy-start.6 = (bf16[4,1024,2,64]{1,3,2,0:T(8,128)(2,1)}, bf16[4,1024,2,64]{1,3,2,0:T(8,128)(2,1)S(1)}, u32[]{:S(2)}) copy-start(bf16[4,1024,2,64]{1,3,2,0:T(8,128)(2,1)S(1)} %get-tuple-element.462) | copy-start | bytes 3145732
  121.4 10.9 %copy-start.8 = (bf16[4,1024,2,64]{1,3,2,0:T(8,128)(2,1)}, bf16[4,1024,2,64]{1,3,2,0:T(8,128)(2,1)S(1)}, u32[]{:S(2)}) copy-start(bf16[4,1024,2,64]{1,3,2,0:T(8,128)(2,1)S(1)} %get-tuple-element.463) | copy-start | bytes 3145732
  121.4 10.9 %copy-start.16 = (bf16[4,1024,2,64]{1,3,2,0:T(8,128)(2,1)}, bf16[4,1024,2,64]{1,3,2,0:T(8,128)(2,1)S(1)}, u32[]{:S(2)}) copy-start(bf16[4,1024,2,64]{1,3,2,0:T(8,128)(2,1)S(1)} %get-tuple-element.470) | copy-start | bytes 3145732
  142.7 1.6 copy-start.26
  142.7 3.4 copy-start.28
  142.7 156.9 %all-gather.8.cloned.1.call-start = ((), (), s32[]{:S(2)}) async-start(), calls=%async_computation.8 | async-start | bytes 5242880 | tf_op jit(solution)/shard_map/all_gather | solution.py:214
  144.3 5.5 copy-start.42
  144.3 5.5 copy-start.44
  149.8 111.7 %copy-start.36 = (f32[1,512]{1,0:T(1,128)}, f32[1,512]{1,0:T(1,128)S(1)}, u32[]{:S(2)}) copy-start(f32[1,512]{1,0:T(1,128)S(1)} %get-tuple-element.292) | copy-start | bytes 6148
  161.7 26.7 %copy-start = (bf16[1024,512]{0,1:T(8,128)(2,1)S(1)}, bf16[1024,512]{0,1:T(8,128)(2,1)}, u32[]{:S(2)}) copy-start(bf16[1024,512]{0,1:T(8,128)(2,1)} %copy.184) | copy-start | bytes 3145732
  188.4 3.4 copy-start.2
  190.0 71.5 %copy-start.32 = (f32[1024]{0:T(1024)}, f32[1024]{0:T(1024)S(1)}, u32[]{:S(2)}) copy-start(f32[1024]{0:T(1024)S(1)} %broadcast_multiply_fusion.5) | copy-start | bytes 12292
  191.7 69.8 %copy-start.34 = (f32[1024]{0:T(1024)}, f32[1024]{0:T(1024)S(1)}, u32[]{:S(2)}) copy-start(f32[1024]{0:T(1024)S(1)} %add_rsqrt_fusion.1) | copy-start | bytes 12292
  192.9 24.2 %copy-start.20 = (bf16[8,1024,64]{1,2,0:T(8,128)(2,1)}, bf16[8,1024,64]{1,2,0:T(8,128)(2,1)S(1)}, u32[]{:S(2)}) copy-start(bf16[8,1024,64]{1,2,0:T(8,128)(2,1)S(1)} %gather_fusion.2) | copy-start | bytes 3145732
  192.9 26.2 %copy-start.24 = (bf16[8,4,64,2,1,256]{5,4,3,2,1,0:T(2,128)(2,1)S(1)}, bf16[8,4,64,2,1,256]{5,4,3,2,1,0:T(2,128)(2,1)}, u32[]{:S(2)}) copy-start(bf16[8,4,64,2,1,256]{5,4,3,2,1,0:T(2,128)(2,1)} %get-tuple-element.285) | copy-start | bytes 6291460
  217.1 2.0 copy-start.59
  225.1 1.9 copy-start.15
  227.0 2.4 copy-start.11
  229.1 1.9 copy-start.13
  235.8 12.1 %copy-start.23 = (bf16[8,4,64,2,1,256]{5,4,3,2,1,0:T(2,128)(2,1)S(1)}, bf16[8,4,64,2,1,256]{5,4,3,2,1,0:T(2,128)(2,1)}, u32[]{:S(2)}) copy-start(bf16[8,4,64,2,1,256]{5,4,3,2,1,0:T(2,128)(2,1)} %get-tuple-element.284) | copy-start | bytes 6291460
  246.0 2.0 copy-start.60
  255.3 2.0 copy-start.4
  255.3 2.2 copy-start.12
  257.4 5.4 copy-start.14
  261.5 4.8 copy-start.38
  261.5 4.8 copy-start.40
  265.0 218.3 %reduce-scatter.12.cloned.1.call-start = ((), (), s32[]{:S(2)}) async-start(), calls=%async_computation.11 | async-start | bytes 294912 | tf_op jit(solution)/shard_map/reduce_scatter | solution.py:246
  309.0 3.4 copy-start.7
  309.0 3.4 copy-start.9
  311.0 173.0 %reduce-scatter.10.cloned.1.call-start = ((), (), s32[]{:S(2)}) async-start(), calls=%async_computation.10 | async-start | bytes 589824 | tf_op jit(solution)/shard_map/reduce_scatter | solution.py:236
  388.0 6.6 copy-start.19
  388.0 6.5 copy-start.25
  397.7 5.2 copy-start.48
  402.8 108.3 %reduce-scatter.8.cloned.1.call-start = ((), (), s32[]{:S(2)}) async-start(), calls=%async_computation.9 | async-start | bytes 5242880 | tf_op jit(solution)/shard_map/reduce_scatter | solution.py:233
  408.2 6.1 copy-start.21
  408.2 254.1 %reduce-scatter.14.cloned.1.call-start = ((), (), s32[]{:S(2)}) async-start(), calls=%async_computation.12 | async-start | bytes 8650752 | tf_op jit(solution)/shard_map/reduce_scatter | solution.py:245
  409.4 4.9 copy-start.61
  437.6 5.4 copy-start.49
  437.6 5.4 copy-start.50
  437.6 5.4 copy-start.53
  437.6 5.4 copy-start.54
  437.6 45.0 %copy-start.43 = (f32[2,512]{1,0:T(2,128)S(1)}, f32[2,512]{1,0:T(2,128)}, u32[]{:S(2)}) copy-start(f32[2,512]{1,0:T(2,128)} %param.34) | copy-start | bytes 12292
  437.7 45.0 %copy-start.45 = (f32[2,512]{1,0:T(2,128)S(1)}, f32[2,512]{1,0:T(2,128)}, u32[]{:S(2)}) copy-start(f32[2,512]{1,0:T(2,128)} %param.35) | copy-start | bytes 12292
  437.7 44.9 %copy-start.51 = (f32[4,512]{1,0:T(4,128)S(1)}, f32[4,512]{1,0:T(4,128)}, u32[]{:S(2)}) copy-start(f32[4,512]{1,0:T(4,128)} %param.37) | copy-start | bytes 24580
  437.7 44.9 %copy-start.52 = (f32[4,512]{1,0:T(4,128)S(1)}, f32[4,512]{1,0:T(4,128)}, u32[]{:S(2)}) copy-start(f32[4,512]{1,0:T(4,128)} %param.36) | copy-start | bytes 24580
  437.7 73.4 %copy-start.1 = (bf16[1024,512]{0,1:T(8,128)(2,1)S(1)}, bf16[1024,512]{0,1:T(8,128)(2,1)}, u32[]{:S(2)}) copy-start(bf16[1024,512]{0,1:T(8,128)(2,1)} %copy.184) | copy-start | bytes 3145732
  437.7 73.4 %copy-start.5 = (bf16[1024,512]{0,1:T(8,128)(2,1)S(1)}, bf16[1024,512]{0,1:T(8,128)(2,1)}, u32[]{:S(2)}) copy-start(bf16[1024,512]{0,1:T(8,128)(2,1)} %reduce-scatter.6.cloned.1.call-done) | copy-start | bytes 3145732
  437.7 73.4 %copy-start.33 = (f32[1024]{0:T(1024)S(1)}, f32[1024]{0:T(1024)}, u32[]{:S(2)}) copy-start(f32[1024]{0:T(1024)} %copy-done.32) | copy-start | bytes 12292
  437.7 73.4 %copy-start.35 = (f32[1024]{0:T(1024)S(1)}, f32[1024]{0:T(1024)}, u32[]{:S(2)}) copy-start(f32[1024]{0:T(1024)} %copy-done.34) | copy-start | bytes 12292
  437.7 73.3 %copy-start.37 = (f32[1,512]{1,0:T(1,128)S(1)}, f32[1,512]{1,0:T(1,128)}, u32[]{:S(2)}) copy-start(f32[1,512]{1,0:T(1,128)} %copy-done.36) | copy-start | bytes 6148
  437.7 73.3 %copy-start.39 = (f32[1024]{0:T(1024)S(1)}, f32[1024]{0:T(1024)}, u32[]{:S(2)}) copy-start(f32[1024]{0:T(1024)} %copy-done.38) | copy-start | bytes 12292
  437.8 73.3 %copy-start.41 = (f32[1024]{0:T(1024)S(1)}, f32[1024]{0:T(1024)}, u32[]{:S(2)}) copy-start(f32[1024]{0:T(1024)} %copy-done.40) | copy-start | bytes 12292
  515.3 148.1 %copy-start.27 = (f32[64,1536]{1,0:T(8,128)S(1)}, f32[64,1536]{1,0:T(8,128)}, u32[]{:S(2)}) copy-start(f32[64,1536]{1,0:T(8,128)} %param.31) | copy-start | bytes 1179652
  515.3 148.1 %copy-start.30 = (f32[64,1536]{1,0:T(8,128)S(1)}, f32[64,1536]{1,0:T(8,128)}, u32[]{:S(2)}) copy-start(f32[64,1536]{1,0:T(8,128)} %param.33) | copy-start | bytes 1179652
  515.3 148.1 %copy-start.31 = (f32[64,1536]{1,0:T(8,128)S(1)}, f32[64,1536]{1,0:T(8,128)}, u32[]{:S(2)}) copy-start(f32[64,1536]{1,0:T(8,128)} %param.32) | copy-start | bytes 1179652
  (6 other events, 6.9 us)
Sparse Core Ops, SparseCore 0:
  9.7 37.1 all-gather.3
  50.3 62.1 all-gather.5
  142.8 45.5 reduce-scatter.5
  265.1 34.4 all-gather.7
  311.2 61.3 reduce-scatter.11
  402.9 62.1 reduce-scatter.9
  467.6 43.4 reduce-scatter.7
  513.5 148.8 reduce-scatter.13
where the time goes:
time: 683 us; the launch traced here: 672 us
  waiting for transfers between devices  220 us (32%)
  local copies, waits for them, and re-layouts  128 us (19%)
  matrix products  126 us (18%)
  blocking collectives  103 us (15%)
  other arithmetic  78.6 us (12%)
  between operations  15.4 us (2%)
    reduce_scatter x1, waiting for transfers between devices, shards(): lax.psum_scatter(feed_grads, ('batch', 'head'), scatter_dimension=0, tile...  144 us
    psum x1, blocking collectives, shards(): norm_grads = lax.psum(norm_local, ('batch', 'head'))  39.6 us
    all_gather x1, waiting for transfers between devices, shards(): branch_group = lax.all_gather(grad_branch, 'head', axis=0, tiled=True)  33.3 us
    all_gather x1, blocking collectives, shards(): lax.all_gather(qkv_part, 'batch', axis=0, tiled=True)  33.1 us
    all_gather x1, blocking collectives, shards(): lax.all_gather(out_part, 'batch', axis=0, tiled=True)  30.8 us
    reduce_scatter x1, waiting for transfers between devices, shards(): lax.psum_scatter(grad_group_in.astype(jnp.bfloat16), 'head', scatter_dime...  26.2 us
    unnamed x131, local copies, waits for them, and re-layouts  26 us
    dot_general x1, matrix products, shards(): jnp.einsum('tbr,bhrgc->thgc', middle_slots, w_up, preferred_element_type=...  24.1 us
  transfers between devices with their start and end apart: 8, of which 4 were waited for; matrix products, arithmetic and copies ran while one was open for 35% of the time, Pallas kernels for 0%

commit v1 on v0

v1 whole, which is shorter than its diff:
```python
import functools
import math

import jax
import jax.numpy as jnp
from jax import lax
from jax.experimental import pallas as pl
from jax.experimental.pallas import tpu as pltpu
from jax.sharding import PartitionSpec as P

D = 512
FF = 2048
NHEADS = 8
DH = 64
SEQ_LEN = 1024
STEP = 10
GROUPW = 768
PART = 256

BETA_FIRST = 0.9
BETA_SECOND = 0.999
ADAM_EPSILON = 1e-08
WEIGHT_DECAY = 0.1
WEIGHT_RATE = 0.2
NORM_RATE = 0.2
NORM_EPSILON = 1e-05
MASK_VALUE = -1000000000.0

MESH = pl.DeviceIdType.MESH
F32 = jnp.float32
BF = jnp.bfloat16
VMEM_BYTES = 60 << 20


def dot(a, b, ca, cb):
    return lax.dot_general(a, b, (((ca,), (cb,)), ((), ())), preferred_element_type=F32)


class Place:
    def __init__(self, batches, heads):
        self.X = self.Y = heads // 2
        self.Z = batches // self.Y
        self.batches, self.heads = batches, heads
        batch, head = lax.axis_index("batch"), lax.axis_index("head")
        self.j = batch
        self.z, self.y = batch // self.Y, batch % self.Y
        self.x, self.c = head // 2, head % 2
        self.xs = [lax.rem(self.x + d, self.X) for d in range(1, self.X)]
        self.ys = [lax.rem(self.y + d, self.Y) for d in range(1, self.Y)]
        self.zs = [lax.rem(self.z + d, self.Z) for d in range(1, self.Z)]

    def dev(self, z=None, y=None, x=None, c=None):
        z = self.z if z is None else z
        y = self.y if y is None else y
        x = self.x if x is None else x
        c = self.c if c is None else c
        return (z * self.Y + y, x * 2 + c)

    def greet(self, devices):
        barrier = pltpu.get_barrier_semaphore()
        for device in devices:
            pl.semaphore_signal(barrier, inc=1, device_id=device, device_id_type=MESH)
        pl.semaphore_wait(barrier, len(devices))

    def batch_peers(self):
        return [(lax.rem(self.j + d, self.batches), self.x * 2 + self.c) for d in range(1, self.batches)]


class Sends:
    def __init__(self, sems):
        self.sems, self.count, self.made = sems, 0, []

    def push(self, src, dst, recv, device, like, cond=None):
        copy = pltpu.make_async_remote_copy(
            src_ref=src, dst_ref=dst, send_sem=self.sems.at[self.count], recv_sem=recv,
            device_id=device, device_id_type=MESH,
        )
        if cond is None:
            copy.start()
        else:
            pl.when(cond())(lambda: copy.start())
        self.made.append((self.count, like, cond))
        self.count += 1

    def drain(self, place):
        for k, like, cond in self.made:
            sent = pltpu.make_async_remote_copy(
                src_ref=like(), dst_ref=like(), send_sem=self.sems.at[k], recv_sem=self.sems.at[k],
                device_id=place.dev(), device_id_type=MESH,
            )
            if cond is None:
                sent.wait_send()
            else:
                pl.when(cond())(lambda sent=sent: sent.wait_send())


def arrived(place, ref, recv, send):
    pltpu.make_async_remote_copy(
        src_ref=ref, dst_ref=ref, send_sem=send, recv_sem=recv, device_id=place.dev(), device_id_type=MESH
    ).wait_recv()


def forward_sends(X, Y, Z):
    part_a = (Z * Y - 1) + (X - 1) + 1 + (Z * Y - 1) * (X - 1 + 1) + (X - 1) * Z * Y
    part_b = (X - 1) + (Y - 1) + (Z - 1) + 1 + (Z - 1) * (X + Y - 1) + Z * (
        2 * (X - 1) * (Y - 1) + (X - 1) + (Y - 1) + (X - 1) * (Y - 1)
    )
    return part_a + part_b


def forward_kernel(
    batches, heads, owner_ref, length_ref, post_ref, weight_ref,
    qk_ref, vx_ref, p_ref, linv_ref, at_ref, xst_ref, ga_out, gb_ref,
    xs_ref, own_ref, ga_ref, recv_a, recv_b, send_sems, own_sem, out_sem,
):
    place = Place(batches, heads)
    groups, rows = NHEADS // heads, D // batches
    X, Y, Z = place.X, place.Y, place.Z
    step = pl.program_id(0)
    sends = Sends(send_sems)
    c, x, j = place.c, place.x, place.j
    dummy = send_sems.at[0]

    def got_a(cc, xx, jj):
        arrived(place, ga_ref.at[cc, xx, jj], recv_a.at[cc, xx, jj], dummy)

    def push_a(cc, xx, jj, device):
        ref = ga_ref.at[cc, xx, jj]
        sends.push(ref, ref, recv_a.at[cc, xx, jj], device, lambda: ga_ref.at[0, 0, 0])

    def got_b(block):
        cc, xx, jj = block
        arrived(place, gb_ref.at[cc, xx, jj], recv_b.at[cc, xx, jj], dummy)

    def push_b(block, device, cond=None, src=None):
        cc, xx, jj = block
        ref = gb_ref.at[cc, xx, jj]
        sends.push(ref if src is None else src, ref, recv_b.at[cc, xx, jj], device, lambda: gb_ref.at[0, 0, 0], cond)

    def at(z=None, y=None, x=None, c=None):
        jj, hh = place.dev(z, y, x, c)
        return (hh % 2, hh // 2, jj)

    def side(offset):
        zo = lax.rem(place.z + offset, Z)
        low = lambda: lax.rem(place.z + offset, Z) < (3 * Z) // 4
        for xx in place.xs:
            got_b(at(z=zo, x=xx))
            for yy in place.ys:
                push_b(at(z=zo, x=xx), place.dev(y=yy), low)
            push_b(at(z=zo, x=xx), place.dev(c=1 - c))
        for yy in place.ys:
            got_b(at(z=zo, y=yy))
            for xx in place.xs:
                push_b(at(z=zo, y=yy), place.dev(x=xx), lambda: jnp.logical_not(low()))
            push_b(at(z=zo, y=yy), place.dev(c=1 - c))

    def own_copy():
        return pltpu.make_async_copy(own_ref, gb_ref.at[c, x, j], own_sem)

    @pl.when(step == 0)
    def _():
        weight = weight_ref[...]
        for g in range(groups):
            ga_ref[c, x, j, g] = weight[:, g * GROUPW : g * GROUPW + PART].astype(BF)
        peers = place.batch_peers()
        place.greet(peers + [place.dev(x=xx) for xx in place.xs] + [place.dev(c=1 - c)])
        for peer in peers:
            push_a(c, x, j, peer)
        for xx in place.xs:
            push_a(c, x, j, place.dev(x=xx))
        push_a(c, x, j, place.dev(c=1 - c))
        for g in range(groups):
            for k in range(2):
                low = g * GROUPW + (k + 1) * PART
                own_ref[g, k] = weight[:, low : low + PART].astype(BF)
        own_copy().start()
        lane = lax.broadcasted_iota(jnp.int32, (1, D), 1)
        source = lane % rows
        for b in range(batches):
            source = jnp.where(lane // rows == b, source + owner_ref[b] * rows, source)
        pick = (lax.broadcasted_iota(jnp.int32, (D, D), 0) == source).astype(F32).astype(BF)
        ordered = dot(post_ref[...], pick, 1, 0).astype(BF)
        xs_ref[...] = ordered
        xst_ref[...] = ordered.T
        for jj, _ in peers:
            got_a(c, x, jj)
            for xx in place.xs:
                push_a(c, x, jj, place.dev(x=xx))
            push_a(c, x, jj, place.dev(c=1 - c))
        for xx in place.xs:
            push_b((c, x, j), place.dev(x=xx), src=own_ref)
        for yy in place.ys:
            push_b((c, x, j), place.dev(y=yy), src=own_ref)
        for zz in place.zs:
            push_b((c, x, j), place.dev(z=zz), src=own_ref)
        push_b((c, x, j), place.dev(c=1 - c), src=own_ref)

    for q in range(1, heads):

        @pl.when(step == q * groups)
        def _(q=q):
            xx = lax.rem(x + q // 2, X)
            for jj in range(batches):
                got_a((c + q) % 2, xx, jj)
            if q % 2 == 0:
                for jj in range(batches):
                    push_a(c, xx, jj, place.dev(c=1 - c))

    @pl.when(step == 3)
    def _():
        own_copy().wait()
        for zz in place.zs:
            got_b(at(z=zz))
            for xx in place.xs:
                push_b(at(z=zz), place.dev(x=xx))
            for yy in place.ys:
                push_b(at(z=zz), place.dev(y=yy))
            push_b(at(z=zz), place.dev(c=1 - c))
        side(0)

    @pl.when(step == 6)
    def _():
        for offset in range(1, Z):
            side(offset)

    @pl.when(step == NHEADS - 1)
    def _():
        pltpu.make_async_copy(ga_ref, ga_out, out_sem).start()

    q, g = step // groups, step % groups
    cc, xx = (c + q) % 2, lax.rem(x + q // 2, X)
    head = (xx * 2 + cc) * groups + g
    w = ga_ref[cc, xx, :, g].reshape(D, PART)
    proj = dot(xs_ref[...], w, 1, 0)
    lane = lax.broadcasted_iota(jnp.int32, (SEQ_LEN, 128), 1)
    qk = proj[:, :128].astype(BF)
    qk = jnp.where(lane < DH, qk * BF(DH**-0.5), qk)
    v = proj[:, 128:].astype(BF)
    vx = jnp.where(lane < DH, v, jnp.where(lane < DH + 2, BF(1), BF(0)))
    qk_ref[0] = qk
    vx_ref[0] = vx
    q_only = jnp.where(lane < DH, qk, BF(0))
    kq = jnp.concatenate([qk[:, DH:], qk[:, :DH]], axis=1)
    vxt = vx.T[: DH + 8]
    keep = lax.broadcasted_iota(jnp.int32, (SEQ_LEN, 1), 0) < length_ref[0]
    s = dot(kq, q_only, 1, 1)
    s = jnp.where(keep, s, F32(MASK_VALUE))
    m = jnp.max(s, axis=0, keepdims=True)
    p = jnp.exp(s - m).astype(BF)
    p_ref[0] = p
    o = dot(vxt, p, 1, 0)
    r = 1.0 / o[DH : DH + 1]
    linv_ref[head] = r
    at_ref[head] = (o[:DH] * r).astype(BF)

    @pl.when(step == NHEADS - 1)
    def _():
        pltpu.make_async_copy(ga_ref, ga_out, out_sem).wait()
        for zz in [place.z] + place.zs:
            for yy in place.ys:
                for xx in place.xs:
                    got_b(at(z=zz, y=yy, x=xx))
                    push_b(at(z=zz, y=yy, x=xx), place.dev(c=1 - c))
        for jj in range(batches):
            for xx in [x] + place.xs:
                got_b((1 - c, xx, jj))
        sends.drain(place)


def forward_call(owner, length, post, weights, batches, heads):
    groups, rows = NHEADS // heads, D // batches
    X, Y = heads // 2, heads // 2
    Z = batches // Y
    tokens = post.shape[0]
    whole = lambda shape: pl.BlockSpec(shape, lambda i: (0,) * len(shape), pipeline_mode=pl.Buffered(1))
    per_head = lambda *shape: pl.BlockSpec((1,) + shape, lambda i: (i, 0, 0))
    shapes = [
        ((NHEADS, tokens, 128), BF),
        ((NHEADS, tokens, 128), BF),
        ((NHEADS, tokens, tokens), BF),
        ((NHEADS, 1, tokens), F32),
        ((NHEADS, DH, tokens), BF),
        ((D, tokens), BF),
        ((2, X, batches, groups, rows, PART), BF),
        ((2, X, batches, groups, 2, rows, PART), BF),
    ]
    return pl.pallas_call(
        functools.partial(forward_kernel, batches, heads),
        grid=(NHEADS,),
        in_specs=[
            pl.BlockSpec(memory_space=pltpu.SMEM),
            pl.BlockSpec(memory_space=pltpu.SMEM),
            whole(post.shape),
            whole(weights.shape),
        ],
        out_specs=[
            per_head(tokens, 128),
            per_head(tokens, 128),
            per_head(tokens, tokens),
            whole(shapes[3][0]),
            whole(shapes[4][0]),
            whole(shapes[5][0]),
            pl.BlockSpec(memory_space=pl.ANY),
            pl.BlockSpec(memory_space=pl.ANY),
        ],
        out_shape=[jax.ShapeDtypeStruct(*s) for s in shapes],
        scratch_shapes=[
            pltpu.VMEM((tokens, D), BF),
            pltpu.VMEM((groups, 2, rows, PART), BF),
            pltpu.VMEM(shapes[6][0], BF),
            pltpu.SemaphoreType.DMA((2, X, batches)),
            pltpu.SemaphoreType.DMA((2, X, batches)),
            pltpu.SemaphoreType.DMA((forward_sends(X, Y, Z),)),
            pltpu.SemaphoreType.DMA,
            pltpu.SemaphoreType.DMA,
        ],
        name="attend_forward",
        compiler_params=pltpu.CompilerParams(
            collective_id=1, has_side_effects=True, vmem_limit_bytes=VMEM_BYTES
        ),
    )(owner, length, post, weights)


def norm_forward(u, gain, bias):
    centred = u - jnp.mean(u, axis=-1, keepdims=True)
    recip = lax.rsqrt(jnp.mean(centred * centred, axis=-1, keepdims=True) + NORM_EPSILON)
    normed = centred * recip
    return normed * gain + bias, normed, recip


def norm_back(grad, normed, recip, gain):
    e = grad * gain
    slope = jnp.mean(e * normed, axis=-1, keepdims=True)
    return recip * (e - jnp.mean(e, axis=-1, keepdims=True) - normed * slope)


def middle_kernel(
    batches, heads, block, owner_ref, length_ref, at_ref, post_ref, dual_ref, pc_ref, dc_ref, gain_ref, bias_ref,
    ga_ref, gb_ref, post_out, dual_out, dmid_ref, dat_ref, wq_ref, dff_ref, dwo_ref, norm_ref,
    wo, w1, w2, a1, a2, ao,
):
    groups, rows = NHEADS // heads, D // batches
    step = pl.program_id(0)

    def seat(h):
        return h % groups, (h // groups) // 2, (h // groups) % 2

    @pl.when(step == 0)
    def _():
        for j in range(batches):
            there = pl.ds(pl.multiple_of(owner_ref[j] * rows, rows), rows)
            for h in range(NHEADS):
                g, x, c = seat(h)
                held = ga_ref[c, x, j, g]
                wq_ref[there, h * PART : (h + 1) * PART] = held
                wo[there, h * DH : (h + 1) * DH] = held[:, 3 * DH :]
                w1[there, h * PART : (h + 1) * PART] = gb_ref[c, x, j, g, 0]
                w2[there, h * PART : (h + 1) * PART] = gb_ref[c, x, j, g, 1]
        a1[...] = jnp.zeros_like(a1)
        a2[...] = jnp.zeros_like(a2)
        ao[...] = jnp.zeros_like(ao)
        norm_ref[...] = jnp.zeros_like(norm_ref)

    at = at_ref[...].reshape(D, block)
    gain, bias = gain_ref[...], bias_ref[...]
    branch = dot(at, wo[...], 0, 1)
    middle, n1, r1 = norm_forward(post_ref[...].astype(F32) + branch, gain[0:1], bias[0:1])
    middle_low = middle.astype(BF)
    pre = dot(middle_low, w1[...], 1, 0)
    cdf = 0.5 + 0.5 * lax.erf(pre * F32(math.sqrt(0.5)))
    density = jnp.exp(pre * pre * F32(-0.5)) * F32(1.0 / math.sqrt(2.0 * math.pi))
    hidden = (pre * cdf).astype(BF)
    slope = cdf + pre * density
    feed = dot(hidden, w2[...], 1, 1)
    out, n2, r2 = norm_forward(middle + feed, gain[1:2], bias[1:2])
    post_out[...] = out.astype(BF)
    dual_out[...] = dual_ref[...] + branch + feed
    keep = step * block + lax.broadcasted_iota(jnp.int32, (block, 1), 0) < length_ref[0]
    d_out = jnp.where(keep, pc_ref[...].astype(F32), 0.0)
    d_dual = jnp.where(keep, dc_ref[...].astype(F32), 0.0)
    d_pre = norm_back(d_out, n2, r2, gain[1:2])
    d_feed = (d_pre + d_dual).astype(BF)
    a2[...] += dot(d_feed, hidden, 0, 0)
    d_hidden = dot(d_feed, w2[...], 1, 0)
    d_hidden_pre = (d_hidden * slope).astype(BF)
    a1[...] += dot(middle_low, d_hidden_pre, 0, 0)
    d_middle = d_pre + dot(d_hidden_pre, w1[...], 1, 1)
    d_mid = norm_back(d_middle, n1, r1, gain[0:1])
    dmid_ref[...] = d_mid
    d_branch = (d_mid + d_dual).astype(BF)
    ao[...] += dot(d_branch, at, 0, 1)
    dat_ref[...] = dot(wo[...], d_branch, 0, 1).astype(BF).reshape(NHEADS, DH, block)
    sums = [jnp.sum(v, axis=0, keepdims=True) for v in (d_middle * n1, d_out * n2, d_middle, d_out)]
    norm_ref[...] += jnp.concatenate(sums, axis=0)

    @pl.when(step == pl.num_programs(0) - 1)
    def _():
        empty = jnp.zeros((rows, DH), BF)
        for j in range(batches):
            there = pl.ds(pl.multiple_of(owner_ref[j] * rows, rows), rows)
            for h in range(NHEADS):
                g, x, c = seat(h)
                dff_ref[g * 2, c, x, j] = a1[there, h * PART : (h + 1) * PART].astype(BF)
                dff_ref[g * 2 + 1, c, x, j] = a2[there, h * PART : (h + 1) * PART].astype(BF)
                dwo = ao[there, h * DH : (h + 1) * DH].astype(BF)
                dwo_ref[h, j * rows : (j + 1) * rows] = jnp.concatenate([empty, dwo], axis=1)


def middle_call(owner, length, at, post, dual, pc, dc, gain, bias, ga, gb, batches, heads):
    groups, rows, X = NHEADS // heads, D // batches, heads // 2
    tokens, block = post.shape[0], 256
    whole = lambda shape: pl.BlockSpec(shape, lambda i, *_: (0,) * len(shape), pipeline_mode=pl.Buffered(1))
    token = pl.BlockSpec((block, D), lambda i, *_: (i, 0))
    across = pl.BlockSpec((NHEADS, DH, block), lambda i, *_: (0, 0, i))
    shapes = [
        ((tokens, D), BF),
        ((tokens, D), F32),
        ((tokens, D), F32),
        ((NHEADS, DH, tokens), BF),
        ((D, NHEADS * PART), BF),
        ((2 * groups, 2, X, batches, rows, PART), BF),
        ((NHEADS, D, 128), BF),
        ((4, D), F32),
    ]
    return pl.pallas_call(
        functools.partial(middle_kernel, batches, heads, block),
        grid_spec=pltpu.PrefetchScalarGridSpec(
            num_scalar_prefetch=2,
            grid=(tokens // block,),
            in_specs=[across, token, token, token, token]
            + [whole(a.shape) for a in (gain, bias, ga, gb)],
            out_specs=[token, token, token, across] + [whole(s[0]) for s in shapes[4:]],
            scratch_shapes=[
                pltpu.VMEM((D, D), BF),
                pltpu.VMEM((D, FF), BF),
                pltpu.VMEM((D, FF), BF),
                pltpu.VMEM((D, FF), F32),
                pltpu.VMEM((D, FF), F32),
                pltpu.VMEM((D, D), F32),
            ],
        ),
        out_shape=[jax.ShapeDtypeStruct(*s) for s in shapes],
        name="middle",
        compiler_params=pltpu.CompilerParams(vmem_limit_bytes=VMEM_BYTES),
    )(owner, length, at, post, dual, pc, dc, gain, bias, ga, gb)


def adam_update(param, grad, first, second, rate, decay):
    first_new = BETA_FIRST * first + (1.0 - BETA_FIRST) * grad
    second_new = BETA_SECOND * second + (1.0 - BETA_SECOND) * grad * grad
    first_hat = first_new * (1.0 / (1.0 - BETA_FIRST**STEP))
    second_hat = second_new * (1.0 / (1.0 - BETA_SECOND**STEP))
    param_new = param - rate * (first_hat / (jnp.sqrt(second_hat) + ADAM_EPSILON) + decay * param)
    return first_new, second_new, param_new


def bits(n):
    return [1 << k for k in range(n.bit_length() - 1)]


class Reduce:
    def __init__(self, place, piece, source, x_first, bufs, recv, sends):
        self.place, self.piece, self.source, self.x_first = place, piece, source, x_first
        self.r1, self.r2, self.r3, self.r4, self.s1, self.s2, self.s3, self.final = (
            b[0 if x_first else 1] if isinstance(b, tuple) else b for b in bufs
        )
        self.recv, self.sends = recv.at[piece], sends

    def got(self, ref, k):
        arrived(self.place, ref, self.recv.at[k], self.sends.sems.at[0])

    def across(self, axis):
        p = self.place
        return (p.X, p.x, lambda v: p.dev(x=v)) if axis == "x" else (p.Y, p.y, lambda v: p.dev(y=v))

    def hop0(self):
        p, k = self.place, self.piece
        self.sends.push(self.source.at[1 - p.c], self.r1.at[k], self.recv.at[0], p.dev(c=1 - p.c), lambda: self.r1.at[k])

    def hop1(self):
        p, k = self.place, self.piece
        self.got(self.r1.at[k], 0)
        self.s1[k] = (self.source[p.c].astype(F32) + self.r1[k].astype(F32)).astype(BF)
        size, me, dev = self.across("x" if self.x_first else "y")
        for d in range(1, size):
            to = lax.rem(me + d, size)
            src = self.s1.at[k, to] if self.x_first else self.s1.at[k, :, :, to]
            self.sends.push(src, self.r2.at[k, d - 1], self.recv.at[d], dev(to), lambda: self.r2.at[k, 0])

    def hop2(self):
        p, k = self.place, self.piece
        size, me, _ = self.across("x" if self.x_first else "y")
        own = self.s1[k, me] if self.x_first else self.s1[k, :, :, me]
        total = own.astype(F32)
        for d in range(1, size):
            self.got(self.r2.at[k, d - 1], d)
            total = total + self.r2[k, d - 1].astype(F32)
        self.s2[k] = total.astype(BF)
        size, me, dev = self.across("y" if self.x_first else "x")
        for d in range(1, size):
            to = lax.rem(me + d, size)
            src = self.s2.at[k, :, to] if self.x_first else self.s2.at[k, to]
            self.sends.push(src, self.r3.at[k, d - 1], self.recv.at[p.X + d], dev(to), lambda: self.r3.at[k, 0])

    def hop3(self):
        p, k = self.place, self.piece
        size, me, _ = self.across("y" if self.x_first else "x")
        own = self.s2[k, :, me] if self.x_first else self.s2[k, me]
        total = own.astype(F32)
        for d in range(1, size):
            self.got(self.r3.at[k, d - 1], p.X + d)
            total = total + self.r3[k, d - 1].astype(F32)
        self.s3[k] = total.astype(BF)
        for d in range(1, p.Z):
            to = lax.rem(p.z + d, p.Z)
            self.sends.push(self.s3.at[k, to], self.r4.at[k, d - 1], self.recv.at[2 * p.X + d], p.dev(z=to), lambda: self.r4.at[k, 0])

    def hop4(self):
        p, k = self.place, self.piece
        total = self.s3[k, p.z].astype(F32)
        for d in range(1, p.Z):
            self.got(self.r4.at[k, d - 1], 2 * p.X + d)
            total = total + self.r4[k, d - 1].astype(F32)
        self.final[k] = total


def backward_kernel(
    batches, heads, qk_ref, vx_ref, p_ref, linv_ref, at_ref, dat_ref, xst_ref, wq_ref, dmid_ref, dff_ref, dwo_ref,
    norm_ref, weight_ref, first_ref, second_ref, nparam_ref, nfirst_ref, nsecond_ref,
    grad_ref, first_out, second_out, weight_out, nfirst_out, nsecond_out, nparam_out,
    dp_ref, dqkv_ref, r1, r2x, r2y, r3, r4, s1, s2x, s2y, s3, final, norm_send, norm_recv, recv_sems, norm_sems, send_sems,
):
    place = Place(batches, heads)
    groups = NHEADS // heads
    X, Y, Z = place.X, place.Y, place.Z
    c, x = place.c, place.x
    step = pl.program_id(0)
    sends = Sends(send_sems)
    bufs = (r1, (r2x, r2y), r3, r4, s1, (s2x, s2y), s3, final)
    pieces = [Reduce(place, k, dff_ref.at[k], k % 2 == 0, bufs, recv_sems, sends) for k in range(2 * groups)]
    pieces += [
        Reduce(place, 2 * groups + g, dqkv_ref.at[g], g % 2 == 0, bufs, recv_sems, sends) for g in range(groups)
    ]
    partners = [place.dev(c=1 - c)]
    flip = lambda v, b: v + b - 2 * b * ((v // b) % 2)
    partners += [place.dev(x=flip(x, b)) for b in bits(X)]
    partners += [place.dev(y=flip(place.y, b)) for b in bits(Y)]
    partners += [place.dev(z=flip(place.z, b)) for b in bits(Z)]

    def norm_push(k):
        sends.push(norm_send.at[k], norm_recv.at[k], norm_sems.at[k], partners[k], lambda: norm_send.at[0])

    def norm_pull(k):
        arrived(place, norm_recv.at[k], norm_sems.at[k], send_sems.at[0])
        norm_send[k + 1] = norm_send[k] + norm_recv[k]

    @pl.when(step == 0)
    def _():
        norm_send[0] = norm_ref[...]
        place.greet(
            [place.dev(c=1 - c)]
            + [place.dev(x=v) for v in place.xs]
            + [place.dev(y=v) for v in place.ys]
            + [place.dev(z=v) for v in place.zs]
        )
        for k in range(2 * groups):
            pieces[k].hop0()
        norm_push(0)

    q, g = step % heads, step // heads
    cc, xx = (c + q) % 2, lax.rem(x + q // 2, X)
    head = (xx * 2 + cc) * groups + g
    lane = lax.broadcasted_iota(jnp.int32, (SEQ_LEN, 128), 1)
    row = lax.broadcasted_iota(jnp.int32, (DH, SEQ_LEN), 0)
    qk, vx = qk_ref[0], vx_ref[0]
    do = dat_ref[head].astype(F32) * linv_ref[head]
    inner = -jnp.sum(do * at_ref[head].astype(F32), axis=0, keepdims=True)
    coarse = inner.astype(BF).astype(F32)
    tail = jnp.where(row == 0, coarse, jnp.where(row == 1, inner - coarse, 0.0))
    et = jnp.concatenate([do, tail], axis=0).astype(BF)
    e = et.T
    kt = qk.T[DH:]
    kq = jnp.concatenate([qk[:, DH:], qk[:, :DH]], axis=1)
    dk = jnp.zeros((SEQ_LEN, 128), F32)
    dv = jnp.zeros((SEQ_LEN, 128), F32)
    dqs = []
    for b in range(2):
        sl = slice(b * (SEQ_LEN // 2), (b + 1) * (SEQ_LEN // 2))
        p = p_ref[0, :, sl]
        ds = (p.astype(F32) * dot(vx, et[:, sl], 1, 0)).astype(BF)
        dv = dv + dot(p, e[sl], 1, 0)
        dk = dk + dot(ds, kq[sl], 1, 0)
        dqs.append(dot(kt, ds, 1, 0))
    dqt = jnp.concatenate(dqs, axis=1) * F32(DH**-0.5)
    dq = jnp.concatenate([dqt, jnp.zeros_like(dqt)], axis=0).T
    d_proj = jnp.concatenate([jnp.where(lane < DH, dq, dk), jnp.where(lane < DH, dv, 0.0)], axis=1).astype(BF)
    dp_ref[head] = d_proj
    dw = dot(xst_ref[...], d_proj, 1, 0)
    dw = jnp.concatenate([dw[:, :128], dw[:, 128:] + dwo_ref[head].astype(F32)], axis=1).astype(BF)
    dqkv_ref[g, cc, xx] = dw.reshape(dqkv_ref.shape[3:])

    def at_step(k):
        return pl.when(step == k)

    half = len(pieces[: 2 * groups]) // 2
    early, late = pieces[:half], pieces[half : 2 * groups]

    for t, todo in enumerate(
        [
            [p.hop1 for p in early] + [lambda: norm_pull(0), lambda: norm_push(1)],
            [p.hop2 for p in early] + [lambda: norm_pull(1), lambda: norm_push(2)],
            [p.hop1 for p in late] + [p.hop3 for p in early],
            ([pieces[2 * groups].hop0] if groups > 1 else [])
            + [p.hop4 for p in early]
            + [p.hop2 for p in late]
            + [lambda: norm_pull(2), lambda: norm_push(3)],
            [p.hop3 for p in late] + ([pieces[2 * groups].hop1] if groups > 1 else []),
            [p.hop4 for p in late] + [lambda: norm_pull(3), lambda: norm_push(4)],
            ([pieces[2 * groups].hop2] if groups > 1 else []),
        ]
    ):

        @at_step(t)
        def _(todo=todo):
            for act in todo:
                act()

    @at_step(NHEADS - 1)
    def _():
        last = pieces[2 * groups + groups - 1]
        last.hop0()
        if groups > 1:
            pieces[2 * groups].hop3()
        for k in range(4, len(partners)):
            norm_pull(k)
            if k + 1 < len(partners):
                norm_push(k + 1)
        last.hop1()
        if groups > 1:
            pieces[2 * groups].hop4()
        total = dmid_ref[...]
        for h in range(NHEADS):
            total = total + dot(dp_ref[h], wq_ref[:, h * PART : (h + 1) * PART], 1, 1)
        grad_ref[...] = total
        last.hop2()
        last.hop3()
        norm_new = adam_update(
            nparam_ref[...], norm_send[len(partners)], nfirst_ref[...], nsecond_ref[...], NORM_RATE, 0.0
        )
        nfirst_out[...], nsecond_out[...], nparam_out[...] = norm_new

        def update(lo, grad):
            cols = slice(lo, lo + PART)
            new = adam_update(
                weight_ref[:, cols], grad, first_ref[:, cols], second_ref[:, cols], WEIGHT_RATE, WEIGHT_DECAY
            )
            first_out[:, cols], second_out[:, cols], weight_out[:, cols] = new

        for k in range(groups):
            update(k * GROUPW + PART, final[2 * k])
            update(k * GROUPW + 2 * PART, final[2 * k + 1])
            if k < groups - 1:
                update(k * GROUPW, final[2 * groups + k])
        last.hop4()
        update((groups - 1) * GROUPW, final[3 * groups - 1])
        sends.drain(place)


def backward_call(
    qk, vx, probs, linv, at, dat, xst, wq, dmid, dff, dwo, norm_grads, weights, first, second, nparam, nfirst, nsecond,
    batches, heads,
):
    groups, rows = NHEADS // heads, D // batches
    X = Y = heads // 2
    Z = batches // Y
    tokens = dmid.shape[0]
    whole = lambda shape: pl.BlockSpec(shape, lambda i: (0,) * len(shape), pipeline_mode=pl.Buffered(1))
    spot = lambda i: ((i % heads) * groups + i // heads, 0, 0)
    per_head = lambda *shape: pl.BlockSpec((1,) + shape, spot)
    dff = dff.reshape(2 * groups, 2, X, Z, Y, rows, PART)
    inputs = (linv, at, dat, xst, wq, dmid, dff, dwo, norm_grads, weights, first, second, nparam, nfirst, nsecond)
    shapes = [((tokens, D), F32)] + [(weights.shape, F32)] * 3 + [((4, D), F32)] * 3
    n = 3 * groups
    stages = 1 + sum(len(bits(v)) for v in (X, Y, Z))
    return pl.pallas_call(
        functools.partial(backward_kernel, batches, heads),
        grid=(NHEADS,),
        in_specs=[per_head(tokens, 128), per_head(tokens, 128), per_head(tokens, tokens)]
        + [whole(a.shape) for a in inputs],
        out_specs=[whole(s[0]) for s in shapes],
        out_shape=[jax.ShapeDtypeStruct(*s) for s in shapes],
        scratch_shapes=[
            pltpu.VMEM((NHEADS, tokens, PART), BF),
            pltpu.VMEM((groups, 2, X, Z, Y, rows, PART), BF),
            pltpu.VMEM((n, X, Z, Y, rows, PART), BF),
            pltpu.VMEM((n, X - 1, Z, Y, rows, PART), BF),
            pltpu.VMEM((n, Y - 1, X, Z, rows, PART), BF),
            pltpu.VMEM((n, X - 1, Z, rows, PART), BF),
            pltpu.VMEM((n, Z - 1, rows, PART), BF),
            pltpu.VMEM((n, X, Z, Y, rows, PART), BF),
            pltpu.VMEM((n, Z, Y, rows, PART), BF),
            pltpu.VMEM((n, X, Z, rows, PART), BF),
            pltpu.VMEM((n, Z, rows, PART), BF),
            pltpu.VMEM((n, rows, PART), F32),
            pltpu.VMEM((stages + 1, 4, D), F32),
            pltpu.VMEM((stages, 4, D), F32),
            pltpu.SemaphoreType.DMA((n, 2 * X + Z)),
            pltpu.SemaphoreType.DMA((stages,)),
            pltpu.SemaphoreType.DMA((n * (1 + 2 * (X - 1) + Z - 1) + stages,)),
        ],
        name="attend_backward",
        compiler_params=pltpu.CompilerParams(
            collective_id=2, has_side_effects=True, vmem_limit_bytes=VMEM_BYTES
        ),
    )(qk, vx, probs, *inputs)


def shards(
    post_stream,
    dual_stream,
    post_cotangent,
    dual_cotangent,
    seq_lengths,
    owner_slots,
    weights,
    first_moment,
    second_moment,
    norm_gain,
    norm_bias,
    norm_first,
    norm_second,
):
    batches, heads = lax.axis_size("batch"), lax.axis_size("head")
    length = lax.dynamic_slice(seq_lengths, (lax.axis_index("head"),), (1,))
    qk, vx, probs, linv, at, xst, ga, gb = forward_call(owner_slots, length, post_stream, weights, batches, heads)
    post_out, dual_out, dmid, dat, wq, dff, dwo, norm_grads = middle_call(
        owner_slots, length, at, post_stream, dual_stream, post_cotangent, dual_cotangent, norm_gain, norm_bias,
        ga, gb, batches, heads,
    )
    norm_params = jnp.concatenate([norm_gain, norm_bias], axis=0)
    rest = backward_call(
        qk, vx, probs, linv, at, dat, xst, wq, dmid, dff, dwo, norm_grads,
        weights, first_moment, second_moment, norm_params, norm_first, norm_second, batches, heads,
    )
    return (post_out, dual_out, *rest)


def solution(mesh):
    tokens, table, copied = P(("batch", "head"), None), P("batch", "head"), P()
    in_specs = (tokens,) * 4 + (P("batch"), copied) + (table,) * 3 + (copied,) * 4
    out_specs = (tokens,) * 3 + (table,) * 3 + (copied,) * 3
    return jax.shard_map(shards, mesh=mesh, in_specs=in_specs, out_specs=out_specs, check_vma=False)
```

time: 683 us -> 167 us (0.24); the launches traced: 672 us -> 166 us
  waiting for transfers between devices: 220 us -> 0 us
  Pallas kernels: 0 us -> 157 us
  matrix products: 126 us -> 0 us
  local copies, waits for them, and re-layouts: 128 us -> 8.48 us
  blocking collectives: 103 us -> 0 us
  other arithmetic: 78.6 us -> 0.61 us
  between operations: 15.4 us -> 0.74 us
    reduce_scatter x5 -> x0, waiting for transfers between devices: 187 us -> none  [the longest x1 144 us: shards(): lax.psum_scatter(feed_grads, ('batch', 'head'), scatter_dimension=0, tile...]
    pallas_call x0 -> x3, Pallas kernels: none -> 157 us  [the longest x1 70 us: backward_call(): pl.pallas_call(functools.partial(backward_kernel, batches, heads), grid=(...]
    dot_general x40 -> x0, matrix products: 126 us -> none  [the longest x1 24.1 us: shards(): jnp.einsum('tbr,bhrgc->thgc', middle_slots, w_up, preferred_element_type=...]
    all_gather x2 -> x0, blocking collectives: 63.9 us -> none  [the longest x1 33.1 us: shards(): lax.all_gather(qkv_part, 'batch', axis=0, tiled=True)]
    psum x1 -> x0, blocking collectives: 39.6 us -> none  [shards(): norm_grads = lax.psum(norm_local, ('batch', 'head'))]
    reshape x10 -> x0, local copies, waits for them, and re-layouts: 37 us -> none  [the longest x1 11.8 us: shards(): feed_all.reshape(batches, head_devices, row_block, groups_here, 2, hidden...]
    all_gather x3 -> x0, waiting for transfers between devices: 33.3 us -> none  [the longest x1 33.3 us: shards(): branch_group = lax.all_gather(grad_branch, 'head', axis=0, tiled=True)]
    convert_element_type x13 -> x0, other arithmetic: 30.3 us -> none  [the longest x4 12.4 us: attend_backward(): grad_scores = (soft_weights * (grad_soft - row_inner)).astype(jnp.bfloat16)]
  transfers between devices with their start and end apart: 8 -> 0, of which waited for: 4 -> 0; matrix products, arithmetic and copies ran while one was open for 35% -> 0% of each run, Pallas kernels for 0% -> 0%
where the time goes in v1:
time: 167 us; the launch traced here: 166 us
  Pallas kernels  157 us (94%)
  local copies, waits for them, and re-layouts  8.48 us (5%)
    pallas_call x1, Pallas kernels, backward_call(): pl.pallas_call(functools.partial(backward_kernel, batches, heads), grid=(...  70 us
    pallas_call x1, Pallas kernels, forward_call(): pl.pallas_call(functools.partial(forward_kernel, batches, heads), grid=(N...  53.9 us
    pallas_call x1, Pallas kernels, middle_call(): pl.pallas_call(functools.partial(middle_kernel, batches, heads, block), g...  32.7 us
    unnamed x23, local copies, waits for them, and re-layouts  7.24 us

profile of v1, /device:TPU:0, one launch (start us, length us, event | category | flops | bytes accessed | tf_op | source)
XLA Modules:
  0.0 166.4 jit_solution(1964928991270050679)
XLA Ops:
  0.6 1.2 dynamic_slice.3.length_ref
  1.9 53.9 %attend_forward.1 = (bf16[8,1024,128]{2,1,0:T(8,128)(2,1)}, bf16[8,1024,128]{2,1,0:T(8,128)(2,1)}, bf16[8,1024,1024]{2,1,0:T(8,128)(2,1)}, f32[8,1,1024]{2,1,0:T...) custom-call(s32[8]{0:T(128)} %owner_ref.3, ...), custom_call_target="tpu_custom_call" | custom-call | tf_op jit(solution)/shard_map/attend_forward/pallas_call | solution.py:288
  55.8 0.0 copy-start.3
  55.8 0.0 copy-start.4
  55.8 32.7 %middle.1 = (bf16[1024,512]{1,0:T(8,128)(2,1)}, f32[1024,512]{1,0:T(8,128)}, f32[1024,512]{1,0:T(8,128)}, bf16[8,64,1024]{2,1,0:T(8,128)(2,1)}, bf16[512,2048]{1...) custom-call(s32[8]{0:T(128)} %owner_ref.3, ...), custom_call_target="tpu_custom_call" | custom-call | tf_op jit(solution)/shard_map/middle/pallas_call | solution.py:426
  88.5 0.0 copy-done.3
  88.5 0.0 copy-done.4
  88.5 0.6 pad_maximum_fusion.nparam_ref
  89.1 70.0 %attend_backward.1 = (f32[1024,512]{1,0:T(8,128)}, f32[64,1536]{1,0:T(8,128)}, f32[64,1536]{1,0:T(8,128)}, f32[64,1536]{1,0:T(8,128)}, f32[4,512]{1,0:T(4,128)}, /*index=5*/f32[4,512]{1,0:T(4,128)}, f32[4,512]{1,0:T(4,128)}) custom-call(bf16[8,1024,128]{2,1,0:T(8,128)(2,1)} %get-tuple-element.37.qk_ref, bf16[8,1024,128]{2,1,0:T(8,128)(2,1)} %get-tuple-element.38.vx_ref, ...), custom_call_target="tpu_custom_call" | custom-call | tf_op jit(solution)/shard_map/attend_backward/pallas_call | solution.py:686
  159.1 0.0 copy-start.2
  159.1 0.0 copy-start.1
  159.1 0.0 copy-start
  159.1 3.2 %copy.29 = f32[1024,512]{1,0:T(8,128)} copy(f32[1024,512]{1,0:T(8,128)} %get-tuple-element.66) | data formatting | bytes 4194304
  162.3 0.0 copy-done.2
  162.3 0.0 copy-start.7
  162.3 0.0 copy-start.6
  162.3 0.0 copy-start.5
  162.3 0.7 copy.30
  163.1 0.0 copy-done.1
  163.1 0.7 copy.31
  163.8 0.0 copy-done
  163.8 0.7 copy.32
  164.6 0.0 copy-done.7
  164.6 0.6 copy.33
  165.2 0.0 copy-done.6
  165.2 0.6 copy.34
  165.8 0.0 copy-done.5
  165.8 0.6 copy.35
Async XLA Ops:
  55.8 32.7 %copy-start.3 = (f32[2,512]{1,0:T(2,128)S(1)}, f32[2,512]{1,0:T(2,128)}, u32[]{:S(2)}) copy-start(f32[2,512]{1,0:T(2,128)} %gain_ref.1) | copy-start | bytes 12292
  55.8 32.7 %copy-start.4 = (f32[2,512]{1,0:T(2,128)S(1)}, f32[2,512]{1,0:T(2,128)}, u32[]{:S(2)}) copy-start(f32[2,512]{1,0:T(2,128)} %bias_ref.1) | copy-start | bytes 12292
  159.1 3.2 %copy-start.2 = (f32[64,1536]{1,0:T(8,128)S(1)}, f32[64,1536]{1,0:T(8,128)}, u32[]{:S(2)}) copy-start(f32[64,1536]{1,0:T(8,128)} %get-tuple-element.67) | copy-start | bytes 1179652
  159.1 4.0 %copy-start.1 = (f32[64,1536]{1,0:T(8,128)S(1)}, f32[64,1536]{1,0:T(8,128)}, u32[]{:S(2)}) copy-start(f32[64,1536]{1,0:T(8,128)} %get-tuple-element.68) | copy-start | bytes 1179652
  159.1 4.7 %copy-start = (f32[64,1536]{1,0:T(8,128)S(1)}, f32[64,1536]{1,0:T(8,128)}, u32[]{:S(2)}) copy-start(f32[64,1536]{1,0:T(8,128)} %get-tuple-element.69) | copy-start | bytes 1179652
  162.3 2.3 %copy-start.7 = (f32[4,512]{1,0:T(4,128)S(1)}, f32[4,512]{1,0:T(4,128)}, u32[]{:S(2)}) copy-start(f32[4,512]{1,0:T(4,128)} %get-tuple-element.70) | copy-start | bytes 24580
  162.3 2.9 %copy-start.6 = (f32[4,512]{1,0:T(4,128)S(1)}, f32[4,512]{1,0:T(4,128)}, u32[]{:S(2)}) copy-start(f32[4,512]{1,0:T(4,128)} %get-tuple-element.71) | copy-start | bytes 24580
  162.3 3.5 %copy-start.5 = (f32[4,512]{1,0:T(4,128)S(1)}, f32[4,512]{1,0:T(4,128)}, u32[]{:S(2)}) copy-start(f32[4,512]{1,0:T(4,128)} %get-tuple-element.72) | copy-start | bytes 24580

commit v2 on v1

v2 whole, which is shorter than its diff:
```python
import functools
import math

import jax
import jax.numpy as jnp
from jax import lax
from jax.experimental import pallas as pl
from jax.experimental.pallas import tpu as pltpu
from jax.sharding import PartitionSpec as P

D = 512
FF = 2048
NHEADS = 8
DH = 64
SEQ_LEN = 1024
STEP = 10
GROUPW = 768
PART = 256

BETA_FIRST = 0.9
BETA_SECOND = 0.999
ADAM_EPSILON = 1e-08
WEIGHT_DECAY = 0.1
WEIGHT_RATE = 0.2
NORM_RATE = 0.2
NORM_EPSILON = 1e-05
MASK_VALUE = -1000000000.0

MESH = pl.DeviceIdType.MESH
F32 = jnp.float32
BF = jnp.bfloat16
VMEM_BYTES = 60 << 20
B_STEPS = (3, 6)


def dot(a, b, ca, cb):
    return lax.dot_general(a, b, (((ca,), (cb,)), ((), ())), preferred_element_type=F32)


class Place:
    def __init__(self, batches, heads):
        self.X = self.Y = heads // 2
        self.Z = batches // self.Y
        self.batches, self.heads = batches, heads
        batch, head = lax.axis_index("batch"), lax.axis_index("head")
        self.j = batch
        self.z, self.y = batch // self.Y, batch % self.Y
        self.x, self.c = head // 2, head % 2
        self.xs = [lax.rem(self.x + d, self.X) for d in range(1, self.X)]
        self.ys = [lax.rem(self.y + d, self.Y) for d in range(1, self.Y)]
        self.zs = [lax.rem(self.z + d, self.Z) for d in range(1, self.Z)]

    def dev(self, z=None, y=None, x=None, c=None):
        z = self.z if z is None else z
        y = self.y if y is None else y
        x = self.x if x is None else x
        c = self.c if c is None else c
        return (z * self.Y + y, x * 2 + c)

    def greet(self, devices):
        barrier = pltpu.get_barrier_semaphore()
        for device in devices:
            pl.semaphore_signal(barrier, inc=1, device_id=device, device_id_type=MESH)
        pl.semaphore_wait(barrier, len(devices))

    def plane(self):
        return [(x, y) for x in [self.x] + self.xs for y in [self.y] + self.ys][1:]


class Sends:
    def __init__(self, sems):
        self.sems, self.count, self.made = sems, 0, []

    def push(self, src, dst, recv, device, like, cond=None):
        copy = pltpu.make_async_remote_copy(
            src_ref=src, dst_ref=dst, send_sem=self.sems.at[self.count], recv_sem=recv,
            device_id=device, device_id_type=MESH,
        )
        if cond is None:
            copy.start()
        else:
            pl.when(cond())(lambda: copy.start())
        self.made.append((self.count, like, cond))
        self.count += 1

    def drain(self, place):
        for k, like, cond in self.made:
            sent = pltpu.make_async_remote_copy(
                src_ref=like(), dst_ref=like(), send_sem=self.sems.at[k], recv_sem=self.sems.at[k],
                device_id=place.dev(), device_id_type=MESH,
            )
            if cond is None:
                sent.wait_send()
            else:
                pl.when(cond())(lambda sent=sent: sent.wait_send())


def arrived(place, ref, recv, send):
    pltpu.make_async_remote_copy(
        src_ref=ref, dst_ref=ref, send_sem=send, recv_sem=recv, device_id=place.dev(), device_id_type=MESH
    ).wait_recv()


def forward_sends(X, Y, Z, groups):
    part_a = groups * (Z - 1 + Y - 1) + (X - 1) * (1 + Z - 1 + Y - 1) + X
    part_b = (X - 1) + (Y - 1) + (Z - 1) + 1 + (Z - 1) * (X + Y - 1)
    part_b += Z * (2 * (X - 1) * (Y - 1) + (X - 1) + (Y - 1) + (X - 1) * (Y - 1))
    return part_a + part_b


def forward_kernel(
    batches, heads, owner_ref, length_ref, post_ref, weight_ref,
    qk_ref, vx_ref, p_ref, linv_ref, at_ref, xst_ref, ga_out, gb_ref,
    xs_ref, own_ref, ga_ref, recv_z, recv_y, recv_x, core_a, recv_b, send_sems, own_sem, out_sem,
):
    place = Place(batches, heads)
    groups, rows = NHEADS // heads, D // batches
    X, Y, Z = place.X, place.Y, place.Z
    step = pl.program_id(0)
    sends = Sends(send_sems)
    c, x, y, z = place.c, place.x, place.y, place.z
    dummy = send_sems.at[0]

    def core_push_a(xx):
        ref = ga_ref.at[c, xx]
        sends.push(ref, ref, core_a.at[xx], place.dev(c=1 - c), lambda: ga_ref.at[0, 0])

    def own_copy():
        return pltpu.make_async_copy(own_ref, gb_ref.at[c, x, z, y], own_sem)

    def got_b(cc, xx, zz, yy):
        arrived(place, gb_ref.at[cc, xx, zz, yy], recv_b.at[cc, xx, zz, yy], dummy)

    def push_b(xx, zz, yy, device, cond=None, src=None):
        ref = gb_ref.at[c, xx, zz, yy]
        sends.push(
            ref if src is None else src, ref, recv_b.at[c, xx, zz, yy], device, lambda: gb_ref.at[0, 0, 0, 0], cond
        )

    def side(offset):
        zo = lax.rem(z + offset, Z)
        low = lambda: lax.rem(place.z + offset, Z) < (3 * Z) // 4
        for xx in place.xs:
            got_b(c, xx, zo, y)
            for yy in place.ys:
                push_b(xx, zo, y, place.dev(y=yy), low)
            push_b(xx, zo, y, place.dev(c=1 - c))
        for yy in place.ys:
            got_b(c, x, zo, yy)
            for xx in place.xs:
                push_b(x, zo, yy, place.dev(x=xx), lambda: jnp.logical_not(low()))
            push_b(x, zo, yy, place.dev(c=1 - c))

    @pl.when(step == 0)
    def _():
        weight = weight_ref[...]
        for g in range(groups):
            ga_ref[c, x, z, y, g] = weight[:, g * GROUPW : g * GROUPW + PART].astype(BF)
        place.greet([place.dev(**{k: v}) for k in "xyz" for v in getattr(place, k + "s")] + [place.dev(c=1 - c)])
        for g in range(groups):
            own = ga_ref.at[c, x, z, y, g]
            for zz in place.zs:
                sends.push(own, own, recv_z.at[g, z], place.dev(z=zz), lambda: ga_ref.at[0, 0, 0, 0, 0])
        own = ga_ref.at[c, x, z, y]
        for xx in place.xs:
            sends.push(own, own, recv_x.at[x, z], place.dev(x=xx), lambda: ga_ref.at[0, 0, 0, 0])
        for g in range(groups):
            for k in range(2):
                low = g * GROUPW + (k + 1) * PART
                own_ref[k, g] = weight[:, low : low + PART].astype(BF)
        for yy in place.ys:
            push_b(x, z, y, place.dev(y=yy), src=own_ref)
        for xx in place.xs:
            push_b(x, z, y, place.dev(x=xx), src=own_ref)
        own_copy().start()
        lane = lax.broadcasted_iota(jnp.int32, (1, D), 1)
        source = lane % rows
        for b in range(batches):
            source = jnp.where(lane // rows == b, source + owner_ref[b] * rows, source)
        pick = (lax.broadcasted_iota(jnp.int32, (D, D), 0) == source).astype(F32).astype(BF)
        ordered = dot(post_ref[...], pick, 1, 0).astype(BF)
        xs_ref[...] = ordered
        xst_ref[...] = ordered.T
        for g in range(groups):
            for zz in place.zs:
                arrived(place, ga_ref.at[c, x, zz, y, g], recv_z.at[g, zz], dummy)
            column = ga_ref.at[c, x, :, y, g]
            for yy in place.ys:
                sends.push(column, column, recv_y.at[g, y], place.dev(y=yy), lambda: ga_ref.at[0, 0, :, 0, 0])
        for zz in place.zs:
            push_b(x, z, y, place.dev(z=zz), src=own_ref)
        for xx in place.xs:
            for zz in place.zs:
                block = ga_ref.at[c, x, zz, y]
                sends.push(block, block, recv_x.at[x, zz], place.dev(x=xx), lambda: ga_ref.at[0, 0, 0, 0])
        push_b(x, z, y, place.dev(c=1 - c), src=own_ref)

    for g in range(groups):

        @pl.when(step == g)
        def _(g=g):
            for yy in place.ys:
                arrived(place, ga_ref.at[c, x, :, yy, g], recv_y.at[g, yy], dummy)
            if g == groups - 1:
                for yy in place.ys:
                    column = ga_ref.at[c, x, :, yy]
                    for xx in place.xs:
                        sends.push(
                            column, column, recv_x.at[x, Z + yy], place.dev(x=xx), lambda: ga_ref.at[0, 0, :, 0]
                        )
                core_push_a(x)

    for k in range(1, heads):

        @pl.when(step == k * groups)
        def _(k=k):
            xx = lax.rem(x + k // 2, X)
            if k % 2 == 0:
                for zz in [z] + place.zs:
                    arrived(place, ga_ref.at[c, xx, zz, y], recv_x.at[xx, zz], dummy)
                for yy in place.ys:
                    arrived(place, ga_ref.at[c, xx, :, yy], recv_x.at[xx, Z + yy], dummy)
                core_push_a(xx)
            else:
                arrived(place, ga_ref.at[1 - c, xx], core_a.at[xx], dummy)

    @pl.when(step == B_STEPS[0])
    def _():
        for zz in place.zs:
            got_b(c, x, zz, y)
            for xx in place.xs:
                push_b(x, zz, y, place.dev(x=xx))
            for yy in place.ys:
                push_b(x, zz, y, place.dev(y=yy))
            push_b(x, zz, y, place.dev(c=1 - c))
        side(0)

    @pl.when(step == B_STEPS[1])
    def _():
        for offset in range(1, Z):
            side(offset)

    @pl.when(step == NHEADS - 1)
    def _():
        pltpu.make_async_copy(ga_ref, ga_out, out_sem).start()

    q, g = step // groups, step % groups
    cc, xx = (c + q) % 2, lax.rem(x + q // 2, X)
    head = (xx * 2 + cc) * groups + g
    w = ga_ref[cc, xx, :, :, g].reshape(D, PART)
    proj = dot(xs_ref[...], w, 1, 0)
    lane = lax.broadcasted_iota(jnp.int32, (SEQ_LEN, 128), 1)
    qk = proj[:, :128].astype(BF)
    qk = jnp.where(lane < DH, qk * BF(DH**-0.5), qk)
    v = proj[:, 128:].astype(BF)
    vx = jnp.where(lane < DH, v, jnp.where(lane < DH + 2, BF(1), BF(0)))
    qk_ref[0] = qk
    vx_ref[0] = vx
    q_only = jnp.where(lane < DH, qk, BF(0))
    kq = jnp.concatenate([qk[:, DH:], qk[:, :DH]], axis=1)
    vxt = vx.T[: DH + 8]
    keep = lax.broadcasted_iota(jnp.int32, (SEQ_LEN, 1), 0) < length_ref[0]
    s = dot(kq, q_only, 1, 1)
    s = jnp.where(keep, s, F32(MASK_VALUE))
    m = jnp.max(s, axis=0, keepdims=True)
    p = jnp.exp(s - m).astype(BF)
    p_ref[0] = p
    o = dot(vxt, p, 1, 0)
    r = 1.0 / o[DH : DH + 1]
    linv_ref[head] = r
    at_ref[head] = (o[:DH] * r).astype(BF)

    @pl.when(step == NHEADS - 1)
    def _():
        pltpu.make_async_copy(ga_ref, ga_out, out_sem).wait()
        own_copy().wait()
        for offset in range(Z):
            zz = lax.rem(z + offset, Z)
            for yy in place.ys:
                for xx in place.xs:
                    got_b(c, xx, zz, yy)
                    push_b(xx, zz, yy, place.dev(c=1 - c))
        for xx in range(X):
            for zz in range(Z):
                for yy in range(Y):
                    got_b(1 - c, xx, zz, yy)
        sends.drain(place)


def forward_call(owner, length, post, weights, batches, heads):
    groups, rows = NHEADS // heads, D // batches
    X, Y = heads // 2, heads // 2
    Z = batches // Y
    tokens = post.shape[0]
    whole = lambda shape: pl.BlockSpec(shape, lambda i: (0,) * len(shape), pipeline_mode=pl.Buffered(1))
    per_head = lambda *shape: pl.BlockSpec((1,) + shape, lambda i: (i, 0, 0))
    shapes = [
        ((NHEADS, tokens, 128), BF),
        ((NHEADS, tokens, 128), BF),
        ((NHEADS, tokens, tokens), BF),
        ((NHEADS, 1, tokens), F32),
        ((NHEADS, DH, tokens), BF),
        ((D, tokens), BF),
        ((2, X, Z, Y, groups, rows, PART), BF),
        ((2, X, Z, Y, 2, groups, rows, PART), BF),
    ]
    return pl.pallas_call(
        functools.partial(forward_kernel, batches, heads),
        grid=(NHEADS,),
        in_specs=[
            pl.BlockSpec(memory_space=pltpu.SMEM),
            pl.BlockSpec(memory_space=pltpu.SMEM),
            whole(post.shape),
            whole(weights.shape),
        ],
        out_specs=[
            per_head(tokens, 128),
            per_head(tokens, 128),
            per_head(tokens, tokens),
            whole(shapes[3][0]),
            whole(shapes[4][0]),
            whole(shapes[5][0]),
            pl.BlockSpec(memory_space=pl.ANY),
            pl.BlockSpec(memory_space=pl.ANY),
        ],
        out_shape=[jax.ShapeDtypeStruct(*s) for s in shapes],
        scratch_shapes=[
            pltpu.VMEM((tokens, D), BF),
            pltpu.VMEM((2, groups, rows, PART), BF),
            pltpu.VMEM(shapes[6][0], BF),
            pltpu.SemaphoreType.DMA((groups, Z)),
            pltpu.SemaphoreType.DMA((groups, Y)),
            pltpu.SemaphoreType.DMA((X, Z + Y)),
            pltpu.SemaphoreType.DMA((X,)),
            pltpu.SemaphoreType.DMA((2, X, Z, Y)),
            pltpu.SemaphoreType.DMA((forward_sends(X, Y, Z, groups),)),
            pltpu.SemaphoreType.DMA,
            pltpu.SemaphoreType.DMA,
        ],
        name="attend_forward",
        compiler_params=pltpu.CompilerParams(
            collective_id=1, has_side_effects=True, vmem_limit_bytes=VMEM_BYTES
        ),
    )(owner, length, post, weights)


def norm_forward(u, gain, bias):
    centred = u - jnp.mean(u, axis=-1, keepdims=True)
    recip = lax.rsqrt(jnp.mean(centred * centred, axis=-1, keepdims=True) + NORM_EPSILON)
    normed = centred * recip
    return normed * gain + bias, normed, recip


def norm_back(grad, normed, recip, gain):
    e = grad * gain
    slope = jnp.mean(e * normed, axis=-1, keepdims=True)
    return recip * (e - jnp.mean(e, axis=-1, keepdims=True) - normed * slope)


def middle_kernel(
    batches, heads, block, owner_ref, length_ref, at_ref, post_ref, dual_ref, pc_ref, dc_ref, gain_ref, bias_ref,
    ga_ref, gb_ref, post_out, dual_out, dmid_ref, dat_ref, wq_ref, dff_ref, dwo_ref, norm_ref,
    wo, w1, w2, a1, a2, ao,
):
    groups, rows, Y = NHEADS // heads, D // batches, heads // 2
    step = pl.program_id(0)

    def seat(h):
        return h % groups, (h // groups) // 2, (h // groups) % 2

    @pl.when(step == 0)
    def _():
        for j in range(batches):
            there = pl.ds(pl.multiple_of(owner_ref[j] * rows, rows), rows)
            for h in range(NHEADS):
                g, x, c = seat(h)
                held = ga_ref[c, x, j // Y, j % Y, g]
                wq_ref[there, h * PART : (h + 1) * PART] = held
                wo[there, h * DH : (h + 1) * DH] = held[:, 3 * DH :]
                w1[there, h * PART : (h + 1) * PART] = gb_ref[c, x, j // Y, j % Y, 0, g]
                w2[there, h * PART : (h + 1) * PART] = gb_ref[c, x, j // Y, j % Y, 1, g]
        a1[...] = jnp.zeros_like(a1)
        a2[...] = jnp.zeros_like(a2)
        ao[...] = jnp.zeros_like(ao)
        norm_ref[...] = jnp.zeros_like(norm_ref)

    at = at_ref[...].reshape(D, block)
    gain, bias = gain_ref[...], bias_ref[...]
    branch = dot(at, wo[...], 0, 1)
    middle, n1, r1 = norm_forward(post_ref[...].astype(F32) + branch, gain[0:1], bias[0:1])
    middle_low = middle.astype(BF)
    pre = dot(middle_low, w1[...], 1, 0)
    cdf = 0.5 + 0.5 * lax.erf(pre * F32(math.sqrt(0.5)))
    density = jnp.exp(pre * pre * F32(-0.5)) * F32(1.0 / math.sqrt(2.0 * math.pi))
    hidden = (pre * cdf).astype(BF)
    slope = cdf + pre * density
    feed = dot(hidden, w2[...], 1, 1)
    out, n2, r2 = norm_forward(middle + feed, gain[1:2], bias[1:2])
    post_out[...] = out.astype(BF)
    dual_out[...] = dual_ref[...] + branch + feed
    keep = step * block + lax.broadcasted_iota(jnp.int32, (block, 1), 0) < length_ref[0]
    d_out = jnp.where(keep, pc_ref[...].astype(F32), 0.0)
    d_dual = jnp.where(keep, dc_ref[...].astype(F32), 0.0)
    d_pre = norm_back(d_out, n2, r2, gain[1:2])
    d_feed = (d_pre + d_dual).astype(BF)
    a2[...] += dot(d_feed, hidden, 0, 0)
    d_hidden = dot(d_feed, w2[...], 1, 0)
    d_hidden_pre = (d_hidden * slope).astype(BF)
    a1[...] += dot(middle_low, d_hidden_pre, 0, 0)
    d_middle = d_pre + dot(d_hidden_pre, w1[...], 1, 1)
    d_mid = norm_back(d_middle, n1, r1, gain[0:1])
    dmid_ref[...] = d_mid
    d_branch = (d_mid + d_dual).astype(BF)
    ao[...] += dot(d_branch, at, 0, 1)
    dat_ref[...] = dot(wo[...], d_branch, 0, 1).astype(BF).reshape(NHEADS, DH, block)
    sums = [jnp.sum(v, axis=0, keepdims=True) for v in (d_middle * n1, d_out * n2, d_middle, d_out)]
    norm_ref[...] += jnp.concatenate(sums, axis=0)

    @pl.when(step == pl.num_programs(0) - 1)
    def _():
        empty = jnp.zeros((rows, DH), BF)
        for j in range(batches):
            there = pl.ds(pl.multiple_of(owner_ref[j] * rows, rows), rows)
            for h in range(NHEADS):
                g, x, c = seat(h)
                dff_ref[g * 2, c, x, j // Y, j % Y] = a1[there, h * PART : (h + 1) * PART].astype(BF)
                dff_ref[g * 2 + 1, c, x, j // Y, j % Y] = a2[there, h * PART : (h + 1) * PART].astype(BF)
                dwo = ao[there, h * DH : (h + 1) * DH].astype(BF)
                dwo_ref[h, j * rows : (j + 1) * rows] = jnp.concatenate([empty, dwo], axis=1)


def middle_call(owner, length, at, post, dual, pc, dc, gain, bias, ga, gb, batches, heads):
    groups, rows, X = NHEADS // heads, D // batches, heads // 2
    tokens, block = post.shape[0], 256
    whole = lambda shape: pl.BlockSpec(shape, lambda i, *_: (0,) * len(shape), pipeline_mode=pl.Buffered(1))
    token = pl.BlockSpec((block, D), lambda i, *_: (i, 0))
    across = pl.BlockSpec((NHEADS, DH, block), lambda i, *_: (0, 0, i))
    shapes = [
        ((tokens, D), BF),
        ((tokens, D), F32),
        ((tokens, D), F32),
        ((NHEADS, DH, tokens), BF),
        ((D, NHEADS * PART), BF),
        ((2 * groups, 2, X, batches // X, X, rows, PART), BF),
        ((NHEADS, D, 128), BF),
        ((4, D), F32),
    ]
    return pl.pallas_call(
        functools.partial(middle_kernel, batches, heads, block),
        grid_spec=pltpu.PrefetchScalarGridSpec(
            num_scalar_prefetch=2,
            grid=(tokens // block,),
            in_specs=[across, token, token, token, token]
            + [whole(a.shape) for a in (gain, bias, ga, gb)],
            out_specs=[token, token, token, across] + [whole(s[0]) for s in shapes[4:]],
            scratch_shapes=[
                pltpu.VMEM((D, D), BF),
                pltpu.VMEM((D, FF), BF),
                pltpu.VMEM((D, FF), BF),
                pltpu.VMEM((D, FF), F32),
                pltpu.VMEM((D, FF), F32),
                pltpu.VMEM((D, D), F32),
            ],
        ),
        out_shape=[jax.ShapeDtypeStruct(*s) for s in shapes],
        name="middle",
        compiler_params=pltpu.CompilerParams(vmem_limit_bytes=VMEM_BYTES),
    )(owner, length, at, post, dual, pc, dc, gain, bias, ga, gb)


def adam_update(param, grad, first, second, rate, decay):
    first_new = BETA_FIRST * first + (1.0 - BETA_FIRST) * grad
    second_new = BETA_SECOND * second + (1.0 - BETA_SECOND) * grad * grad
    first_hat = first_new * (1.0 / (1.0 - BETA_FIRST**STEP))
    second_hat = second_new * (1.0 / (1.0 - BETA_SECOND**STEP))
    param_new = param - rate * (first_hat / (jnp.sqrt(second_hat) + ADAM_EPSILON) + decay * param)
    return first_new, second_new, param_new


class Piece:
    def __init__(self, place, k, source, x_first, bufs, recv, sends):
        self.place, self.source, self.x_first, self.sends = place, source, x_first, sends
        bufs = [b[0 if x_first else 1] if isinstance(b, tuple) else b for b in bufs]
        self.r1, self.s1, self.r2, self.s2, self.r3, self.s3, self.r4, self.final = (b.at[k] for b in bufs)
        self.recv = recv.at[k]

    def axis(self, x):
        p = self.place
        return (p.X, p.x, lambda v: p.dev(x=v)) if x else (p.Y, p.y, lambda v: p.dev(y=v))

    def send(self, axis, cut, buf, base):
        size, me, dev = axis
        for d in range(1, size):
            to = lax.rem(me + d, size)
            self.sends.push(cut(to), buf.at[d - 1], self.recv.at[base + d], dev(to), lambda: buf.at[0])

    def add(self, axis, own, buf, base):
        total = own.astype(F32)
        for d in range(1, axis[0]):
            arrived(self.place, buf.at[d - 1], self.recv.at[base + d], self.sends.sems.at[0])
            total = total + buf[d - 1].astype(F32)
        return total

    def hop0(self):
        p = self.place
        self.sends.push(self.source.at[1 - p.c], self.r1, self.recv.at[0], p.dev(c=1 - p.c), lambda: self.r1)

    def hop1(self):
        p = self.place
        arrived(p, self.r1, self.recv.at[0], self.sends.sems.at[0])
        self.s1[...] = (self.source[p.c].astype(F32) + self.r1[...].astype(F32)).astype(BF)
        cut = lambda to: self.s1.at[to] if self.x_first else self.s1.at[:, :, to]
        self.send(self.axis(self.x_first), cut, self.r2, 0)

    def hop2(self):
        p = self.place
        own = self.s1[p.x] if self.x_first else self.s1[:, :, p.y]
        self.s2[...] = self.add(self.axis(self.x_first), own, self.r2, 0).astype(BF)
        cut = lambda to: self.s2.at[:, to] if self.x_first else self.s2.at[to]
        self.send(self.axis(not self.x_first), cut, self.r3, p.X)

    def hop3(self):
        p = self.place
        own = self.s2[:, p.y] if self.x_first else self.s2[p.x]
        self.s3[...] = self.add(self.axis(not self.x_first), own, self.r3, p.X).astype(BF)
        self.send((p.Z, p.z, lambda v: p.dev(z=v)), lambda to: self.s3.at[to], self.r4, 2 * p.X)

    def hop4(self):
        p = self.place
        self.final[...] = self.add((p.Z, p.z, None), self.s3[p.z], self.r4, 2 * p.X)


class Chunk:
    def __init__(self, place, g, dx, source, bufs, recv, sends):
        self.place, self.dx, self.sends = place, dx, sends
        r1, s1, rx, s2, r2 = bufs
        self.source, self.r1, self.s1, self.rx, self.s2, self.r2 = (
            source.at[g], r1.at[g, dx], s1.at[g, dx], rx.at[g], s2.at[g], r2.at[g]
        )
        self.recv = recv.at[g]

    def hop0(self):
        p = self.place
        x = lax.rem(p.x + self.dx, p.X)
        self.sends.push(self.source.at[1 - p.c, x], self.r1, self.recv.at[self.dx], p.dev(c=1 - p.c), lambda: self.r1)

    def hop1(self):
        p = self.place
        x = lax.rem(p.x + self.dx, p.X)
        arrived(p, self.r1, self.recv.at[self.dx], self.sends.sems.at[0])
        total = self.source[p.c, x].astype(F32) + self.r1[...].astype(F32)
        if self.dx:
            self.s1[...] = total.astype(BF)
            self.sends.push(
                self.s1, self.rx.at[self.dx - 1], self.recv.at[p.X + self.dx], p.dev(x=x), lambda: self.s1
            )
            return
        for d in range(1, p.X):
            arrived(p, self.rx.at[d - 1], self.recv.at[p.X + d], self.sends.sems.at[0])
            total = total + self.rx[d - 1].astype(F32)
        self.s2[...] = total.astype(BF)
        for d in range(1, p.batches):
            j = lax.rem(p.j + d, p.batches)
            self.sends.push(
                self.s2.at[j], self.r2.at[d - 1], self.recv.at[2 * p.X + d], (j, p.x * 2 + p.c), lambda: self.r2.at[0]
            )

    def collect(self):
        p = self.place
        total = self.s2[p.j].astype(F32)
        for d in range(1, p.batches):
            arrived(p, self.r2.at[d - 1], self.recv.at[2 * p.X + d], self.sends.sems.at[0])
            total = total + self.r2[d - 1].astype(F32)
        return total


def bits(n):
    return [1 << k for k in range(n.bit_length() - 1)]


def backward_kernel(
    batches, heads, qk_ref, vx_ref, p_ref, linv_ref, at_ref, dat_ref, xst_ref, wq_ref, dff_ref, dwo_ref, norm_ref,
    partial_ref, grad_ref, norm_out,
    dp_ref, dqkv_ref, r1, s1, xr2, yr2, xs2, ys2, r3, s3, r4, final, qr1, qs1, qrx, qs2, qr2,
    norm_send, norm_recv, recv_f, recv_q, norm_sems, send_sems,
):
    place = Place(batches, heads)
    groups = NHEADS // heads
    X, Y, Z = place.X, place.Y, place.Z
    c, x = place.c, place.x
    step = pl.program_id(0)
    sends = Sends(send_sems)
    bufs = (r1, s1, (xr2, yr2), (xs2, ys2), r3, s3, r4, final)
    pieces = [Piece(place, k, dff_ref.at[k], k == 0, bufs, recv_f, sends) for k in range(2 * groups)]
    chunks = [
        Chunk(place, g, dx, dqkv_ref, (qr1, qs1, qrx, qs2, qr2), recv_q, sends)
        for g in range(groups)
        for dx in reversed(range(X))
    ]
    partners = [place.dev(c=1 - c)]
    flip = lambda v, b: v + b - 2 * b * ((v // b) % 2)
    partners += [place.dev(x=flip(x, b)) for b in bits(X)]
    partners += [place.dev(y=flip(place.y, b)) for b in bits(Y)]
    partners += [place.dev(z=flip(place.z, b)) for b in bits(Z)]

    def norm_push(k):
        sends.push(norm_send.at[k], norm_recv.at[k], norm_sems.at[k], partners[k], lambda: norm_send.at[0])

    def norm_pull(k):
        arrived(place, norm_recv.at[k], norm_sems.at[k], send_sems.at[0])
        norm_send[k + 1] = norm_send[k] + norm_recv[k]

    @pl.when(step == 0)
    def _():
        norm_send[0] = norm_ref[...]
        others = [(dx, dj) for dx in range(X) for dj in range(batches) if dx or dj]
        place.greet(
            [(lax.rem(place.j + dj, batches), lax.rem(x + dx, X) * 2 + c) for dx, dj in others] + [place.dev(c=1 - c)]
        )
        for piece in pieces:
            piece.hop0()
        norm_push(0)

    g, r = step // heads, step % heads
    cc, xx = (c + r) % 2, lax.rem(x + X - 1 - r // 2, X)
    head = (xx * 2 + cc) * groups + g
    lane = lax.broadcasted_iota(jnp.int32, (SEQ_LEN, 128), 1)
    row = lax.broadcasted_iota(jnp.int32, (DH, SEQ_LEN), 0)
    qk, vx = qk_ref[0], vx_ref[0]
    do = dat_ref[head].astype(F32) * linv_ref[head]
    inner = -jnp.sum(do * at_ref[head].astype(F32), axis=0, keepdims=True)
    coarse = inner.astype(BF).astype(F32)
    tail = jnp.where(row == 0, coarse, jnp.where(row == 1, inner - coarse, 0.0))
    et = jnp.concatenate([do, tail], axis=0).astype(BF)
    e = et.T
    kt = qk.T[DH:]
    kq = jnp.concatenate([qk[:, DH:], qk[:, :DH]], axis=1)
    dk = jnp.zeros((SEQ_LEN, 128), F32)
    dv = jnp.zeros((SEQ_LEN, 128), F32)
    dqs = []
    for b in range(2):
        sl = slice(b * (SEQ_LEN // 2), (b + 1) * (SEQ_LEN // 2))
        p = p_ref[0, :, sl]
        ds = (p.astype(F32) * dot(vx, et[:, sl], 1, 0)).astype(BF)
        dv = dv + dot(p, e[sl], 1, 0)
        dk = dk + dot(ds, kq[sl], 1, 0)
        dqs.append(dot(kt, ds, 1, 0))
    dqt = jnp.concatenate(dqs, axis=1) * F32(DH**-0.5)
    dq = jnp.concatenate([dqt, jnp.zeros_like(dqt)], axis=0).T
    d_proj = jnp.concatenate([jnp.where(lane < DH, dq, dk), jnp.where(lane < DH, dv, 0.0)], axis=1).astype(BF)
    dp_ref[head] = d_proj
    dw = dot(xst_ref[...], d_proj, 1, 0)
    dw = jnp.concatenate([dw[:, :128], dw[:, 128:] + dwo_ref[head].astype(F32)], axis=1).astype(BF)
    dqkv_ref[g, cc, xx] = dw.reshape(dqkv_ref.shape[3:])

    early, late = pieces[:2], pieces[2:]
    todo = [[] for _ in range(NHEADS)]
    todo[0] += [p.hop1 for p in early] + [lambda: norm_pull(0), lambda: norm_push(1)]
    todo[1] += [p.hop1 for p in late]
    for n, chunk in enumerate(chunks):
        todo[2 * n + 1].append(chunk.hop0)
        if n + 1 < len(chunks):
            todo[2 * n + 2].append(chunk.hop1)
    todo[2] += [lambda: norm_pull(1), lambda: norm_push(2)]
    todo[3] += [p.hop2 for p in early]
    todo[4] += [p.hop2 for p in late] + [lambda: norm_pull(2), lambda: norm_push(3)]
    todo[5] += [p.hop3 for p in early]
    todo[6] += [p.hop3 for p in late] + [lambda: norm_pull(3), lambda: norm_push(4)]
    todo[7] += [p.hop4 for p in early]

    for t in range(NHEADS - 1):

        @pl.when(step == t)
        def _(t=t):
            for act in todo[t]:
                act()

    @pl.when(step == NHEADS - 1)
    def _():
        for act in todo[NHEADS - 1]:
            act()
        for k in range(4, len(partners)):
            norm_pull(k)
            if k + 1 < len(partners):
                norm_push(k + 1)
        norm_out[...] = norm_send[len(partners)]
        chunks[-1].hop1()
        partial = dot(dp_ref[0], wq_ref[:, :PART], 1, 1)
        for h in range(1, NHEADS):
            partial = partial + dot(dp_ref[h], wq_ref[:, h * PART : (h + 1) * PART], 1, 1)
        partial_ref[...] = partial.astype(BF)
        for p in late:
            p.hop4()
        for k in range(groups):
            for n in range(2):
                low = k * GROUPW + (n + 1) * PART
                grad_ref[:, low : low + PART] = final[2 * k + n]
            grad_ref[:, k * GROUPW : k * GROUPW + PART] = chunks[(k + 1) * X - 1].collect()
        sends.drain(place)


def backward_call(qk, vx, probs, linv, at, dat, xst, wq, dff, dwo, norm_grads, batches, heads):
    groups, rows = NHEADS // heads, D // batches
    X = Y = heads // 2
    Z = batches // Y
    tokens = xst.shape[1]
    whole = lambda shape: pl.BlockSpec(shape, lambda i: (0,) * len(shape), pipeline_mode=pl.Buffered(1))
    spot = lambda i: ((heads - 2 - 2 * ((i % heads) // 2) + i % 2) * groups + i // heads, 0, 0)
    per_head = lambda *shape: pl.BlockSpec((1,) + shape, spot)
    inputs = (linv, at, dat, xst, wq, dff, dwo, norm_grads)
    shapes = [((tokens, D), BF), ((rows, groups * GROUPW), F32), ((4, D), F32)]
    n = 2 * groups
    stages = 1 + sum(len(bits(v)) for v in (X, Y, Z))
    count = n * (1 + X - 1 + Y - 1 + Z - 1) + groups * (X + X - 1 + batches - 1) + stages
    return pl.pallas_call(
        functools.partial(backward_kernel, batches, heads),
        grid=(NHEADS,),
        in_specs=[per_head(tokens, 128), per_head(tokens, 128), per_head(tokens, tokens)]
        + [whole(a.shape) for a in inputs],
        out_specs=[whole(s[0]) for s in shapes],
        out_shape=[jax.ShapeDtypeStruct(*s) for s in shapes],
        scratch_shapes=[
            pltpu.VMEM((NHEADS, tokens, PART), BF),
            pltpu.VMEM((groups, 2, X, batches, rows, PART), BF),
            pltpu.VMEM((n, X, Z, Y, rows, PART), BF),
            pltpu.VMEM((n, X, Z, Y, rows, PART), BF),
            pltpu.VMEM((n, X - 1, Z, Y, rows, PART), BF),
            pltpu.VMEM((n, Y - 1, X, Z, rows, PART), BF),
            pltpu.VMEM((n, Z, Y, rows, PART), BF),
            pltpu.VMEM((n, X, Z, rows, PART), BF),
            pltpu.VMEM((n, X - 1, Z, rows, PART), BF),
            pltpu.VMEM((n, Z, rows, PART), BF),
            pltpu.VMEM((n, Z - 1, rows, PART), BF),
            pltpu.VMEM((n, rows, PART), F32),
            pltpu.VMEM((groups, X, batches, rows, PART), BF),
            pltpu.VMEM((groups, X, batches, rows, PART), BF),
            pltpu.VMEM((groups, X - 1, batches, rows, PART), BF),
            pltpu.VMEM((groups, batches, rows, PART), BF),
            pltpu.VMEM((groups, batches - 1, rows, PART), BF),
            pltpu.VMEM((stages + 1, 4, D), F32),
            pltpu.VMEM((stages, 4, D), F32),
            pltpu.SemaphoreType.DMA((n, 2 * X + Z)),
            pltpu.SemaphoreType.DMA((groups, 2 * X + batches)),
            pltpu.SemaphoreType.DMA((stages,)),
            pltpu.SemaphoreType.DMA((count,)),
        ],
        name="attend_backward",
        compiler_params=pltpu.CompilerParams(
            collective_id=2, has_side_effects=True, vmem_limit_bytes=VMEM_BYTES
        ),
    )(qk, vx, probs, *inputs)


def update_kernel(
    dmid_ref, partial_ref, grad_ref, weight_ref, first_ref, second_ref, ngrad_ref, nparam_ref, nfirst_ref, nsecond_ref,
    post_out, first_out, second_out, weight_out, nfirst_out, nsecond_out, nparam_out,
):
    post_out[...] = dmid_ref[...] + partial_ref[...].astype(F32)
    first_out[...], second_out[...], weight_out[...] = adam_update(
        weight_ref[...], grad_ref[...], first_ref[...], second_ref[...], WEIGHT_RATE, WEIGHT_DECAY
    )
    nfirst_out[...], nsecond_out[...], nparam_out[...] = adam_update(
        nparam_ref[...], ngrad_ref[...], nfirst_ref[...], nsecond_ref[...], NORM_RATE, 0.0
    )


def update_call(dmid, partial, grad, weights, first, second, ngrad, nparam, nfirst, nsecond):
    steps = 2
    cut = lambda a: pl.BlockSpec((a.shape[0] // steps, a.shape[1]), lambda i: (i, 0))
    same = lambda a: pl.BlockSpec(a.shape, lambda i: (0, 0))
    outs = [dmid, weights, weights, weights, nparam, nparam, nparam]
    return pl.pallas_call(
        update_kernel,
        grid=(steps,),
        in_specs=[cut(a) for a in (dmid, partial, grad, weights, first, second)]
        + [same(a) for a in (ngrad, nparam, nfirst, nsecond)],
        out_specs=[cut(a) for a in outs[:4]] + [same(a) for a in outs[4:]],
        out_shape=[jax.ShapeDtypeStruct(a.shape, F32) for a in outs],
        name="update",
        compiler_params=pltpu.CompilerParams(vmem_limit_bytes=VMEM_BYTES),
    )(dmid, partial, grad, weights, first, second, ngrad, nparam, nfirst, nsecond)


def shards(
    post_stream,
    dual_stream,
    post_cotangent,
    dual_cotangent,
    seq_lengths,
    owner_slots,
    weights,
    first_moment,
    second_moment,
    norm_gain,
    norm_bias,
    norm_first,
    norm_second,
):
    batches, heads = lax.axis_size("batch"), lax.axis_size("head")
    length = lax.dynamic_slice(seq_lengths, (lax.axis_index("head"),), (1,))
    qk, vx, probs, linv, at, xst, ga, gb = forward_call(owner_slots, length, post_stream, weights, batches, heads)
    post_out, dual_out, dmid, dat, wq, dff, dwo, norm_grads = middle_call(
        owner_slots, length, at, post_stream, dual_stream, post_cotangent, dual_cotangent, norm_gain, norm_bias,
        ga, gb, batches, heads,
    )
    partial, weight_grad, norm_grad = backward_call(
        qk, vx, probs, linv, at, dat, xst, wq, dff, dwo, norm_grads, batches, heads
    )
    norm_params = jnp.concatenate([norm_gain, norm_bias], axis=0)
    rest = update_call(
        dmid, partial, weight_grad, weights, first_moment, second_moment, norm_grad, norm_params, norm_first, norm_second
    )
    return (post_out, dual_out, *rest)


def solution(mesh):
    tokens, table, copied = P(("batch", "head"), None), P("batch", "head"), P()
    in_specs = (tokens,) * 4 + (P("batch"), copied) + (table,) * 3 + (copied,) * 4
    out_specs = (tokens,) * 3 + (table,) * 3 + (copied,) * 3
    return jax.shard_map(shards, mesh=mesh, in_specs=in_specs, out_specs=out_specs, check_vma=False)
```

time: 167 us -> 144 us (0.86)
  Pallas kernels: 157 us -> 141 us
  local copies, waits for them, and re-layouts: 8.48 us -> 1.25 us
    pallas_call x1, Pallas kernels: 70 us -> 57.9 us  [backward_call(): pl.pallas_call(functools.partial(backward_kernel, batches, heads), grid=(...]
    pallas_call x1, Pallas kernels: 53.9 us -> 46.6 us  [forward_call(): pl.pallas_call(functools.partial(forward_kernel, batches, heads), grid=(N...]
    unnamed x23 -> x4, local copies, waits for them, and re-layouts: 7.24 us -> 0.01 us
    pallas_call x0 -> x1, Pallas kernels: none -> 3.7 us  [update_call(): pl.pallas_call(update_kernel, grid=(steps,), in_specs=[cut(a) for a in (d...]
where the time goes in v2:
time: 144 us
  Pallas kernels  141 us (98%)
    pallas_call x1, Pallas kernels, backward_call(): pl.pallas_call(functools.partial(backward_kernel, batches, heads), grid=(...  57.9 us
    pallas_call x1, Pallas kernels, forward_call(): pl.pallas_call(functools.partial(forward_kernel, batches, heads), grid=(N...  46.6 us
    pallas_call x1, Pallas kernels, middle_call(): pl.pallas_call(functools.partial(middle_kernel, batches, heads, block), g...  32.7 us
    pallas_call x1, Pallas kernels, update_call(): pl.pallas_call(update_kernel, grid=(steps,), in_specs=[cut(a) for a in (d...  3.7 us

profile of v2, /device:TPU:0, one launch (start us, length us, event | category | flops | bytes accessed | tf_op | source)
XLA Modules:
  0.0 143.5 jit_solution(10361528045542023770)
XLA Ops:
  0.6 1.2 dynamic_slice.3.length_ref
  1.9 46.6 %attend_forward.1 = (bf16[8,1024,128]{2,1,0:T(8,128)(2,1)}, bf16[8,1024,128]{2,1,0:T(8,128)(2,1)}, bf16[8,1024,1024]{2,1,0:T(8,128)(2,1)}, f32[8,1,1024]{2,1,0:T...) custom-call(s32[8]{0:T(128)} %owner_ref.3, ...), custom_call_target="tpu_custom_call" | custom-call | tf_op jit(solution)/shard_map/attend_forward/pallas_call | solution.py:307
  48.5 32.7 %middle.1 = (bf16[1024,512]{1,0:T(8,128)(2,1)}, f32[1024,512]{1,0:T(8,128)}, f32[1024,512]{1,0:T(8,128)}, bf16[8,64,1024]{2,1,0:T(8,128)(2,1)}, bf16[512,2048]{1...) custom-call(s32[8]{0:T(128)} %owner_ref.3, ...), custom_call_target="tpu_custom_call" | custom-call | tf_op jit(solution)/shard_map/middle/pallas_call | solution.py:448
  81.2 0.0 copy-start
  81.2 0.0 copy-start.1
  81.2 57.9 %attend_backward.1 = (bf16[1024,512]{1,0:T(8,128)(2,1)}, f32[64,1536]{1,0:T(8,128)}, f32[4,512]{1,0:T(4,128)}) custom-call(bf16[8,1024,128]{2,1,0:T(8,128)(2,1)} %get-tuple-element.41.qk_ref, bf16[8,1024,128]{2,1,0:T(8,128)(2,1)} %get-tuple-element.42.vx_ref, bf16[8,1024,1024]{2,1,0:T(8,128)(2,1)} %get-tuple-element.43.p_ref, ...), custom_call_target="tpu_custom_call" | custom-call | tf_op jit(solution)/shard_map/attend_backward/pallas_call | solution.py:715
  139.1 0.0 copy-done
  139.1 0.0 copy-done.1
  139.1 0.6 pad_maximum_fusion.nparam_ref
  139.7 3.7 %update.1 = (f32[1024,512]{1,0:T(8,128)}, f32[64,1536]{1,0:T(8,128)}, f32[64,1536]{1,0:T(8,128)}, f32[64,1536]{1,0:T(8,128)}, f32[4,512]{1,0:T(4,128)}, /*index=5*/f32[4,512]{1,0:T(4,128)}, f32[4,512]{1,0:T(4,128)}) custom-call(f32[1024,512]{1,0:T(8,128)} %get-tuple-element.40.dmid_ref, bf16[1024,512]{1,0:T(8,128)(2,1)} %get-tuple-element.51.partial_ref, ...), custom_call_target="tpu_custom_call" | custom-call | tf_op jit(solution)/shard_map/update/pallas_call | solution.py:772
Async XLA Ops:
  81.2 57.9 %copy-start = (f32[2,512]{1,0:T(2,128)S(1)}, f32[2,512]{1,0:T(2,128)}, u32[]{:S(2)}) copy-start(f32[2,512]{1,0:T(2,128)} %gain_ref.1) | copy-start | bytes 12292
  81.2 57.9 %copy-start.1 = (f32[2,512]{1,0:T(2,128)S(1)}, f32[2,512]{1,0:T(2,128)}, u32[]{:S(2)}) copy-start(f32[2,512]{1,0:T(2,128)} %bias_ref.1) | copy-start | bytes 12292

commit v3 on v0

v3 whole, which is shorter than its diff:
```python
import functools
import math

import jax
import jax.numpy as jnp
from jax import lax
from jax.experimental import pallas as pl
from jax.experimental.pallas import tpu as pltpu
from jax.sharding import PartitionSpec as P

D = 512
FF = 2048
NHEADS = 8
DH = 64
SEQ_LEN = 1024
STEP = 10
GROUPW = 768
PART = 256

BETA_FIRST = 0.9
BETA_SECOND = 0.999
ADAM_EPSILON = 1e-08
WEIGHT_DECAY = 0.1
WEIGHT_RATE = 0.2
NORM_RATE = 0.2
NORM_EPSILON = 1e-05
MASK_VALUE = -1000000000.0

MESH = pl.DeviceIdType.MESH
F32 = jnp.float32
BF = jnp.bfloat16
VMEM_BYTES = 63 << 20
B_STEPS = (3, 6)
MID_STEPS = 4


def dot(a, b, ca, cb):
    return lax.dot_general(a, b, (((ca,), (cb,)), ((), ())), preferred_element_type=F32)


class Place:
    def __init__(self, batches, heads):
        self.X = self.Y = heads // 2
        self.Z = batches // self.Y
        self.batches, self.heads = batches, heads
        batch, head = lax.axis_index("batch"), lax.axis_index("head")
        self.j = batch
        self.z, self.y = batch // self.Y, batch % self.Y
        self.x, self.c = head // 2, head % 2
        self.xs = [lax.rem(self.x + d, self.X) for d in range(1, self.X)]
        self.ys = [lax.rem(self.y + d, self.Y) for d in range(1, self.Y)]
        self.zs = [lax.rem(self.z + d, self.Z) for d in range(1, self.Z)]

    def dev(self, z=None, y=None, x=None, c=None):
        z = self.z if z is None else z
        y = self.y if y is None else y
        x = self.x if x is None else x
        c = self.c if c is None else c
        return (z * self.Y + y, x * 2 + c)

    def greet(self, devices):
        barrier = pltpu.get_barrier_semaphore()
        for device in devices:
            pl.semaphore_signal(barrier, inc=1, device_id=device, device_id_type=MESH)
        pl.semaphore_wait(barrier, len(devices))

    def plane(self):
        return [(x, y) for x in [self.x] + self.xs for y in [self.y] + self.ys][1:]


class Sends:
    def __init__(self, sems):
        self.sems, self.count, self.made = sems, 0, []

    def push(self, src, dst, recv, device, like, cond=None):
        copy = pltpu.make_async_remote_copy(
            src_ref=src, dst_ref=dst, send_sem=self.sems.at[self.count], recv_sem=recv,
            device_id=device, device_id_type=MESH,
        )
        if cond is None:
            copy.start()
        else:
            pl.when(cond())(lambda: copy.start())
        self.made.append((self.count, like, cond))
        self.count += 1

    def drain(self, place):
        for k, like, cond in self.made:
            sent = pltpu.make_async_remote_copy(
                src_ref=like(), dst_ref=like(), send_sem=self.sems.at[k], recv_sem=self.sems.at[k],
                device_id=place.dev(), device_id_type=MESH,
            )
            if cond is None:
                sent.wait_send()
            else:
                pl.when(cond())(lambda sent=sent: sent.wait_send())


def arrived(place, ref, recv, send):
    pltpu.make_async_remote_copy(
        src_ref=ref, dst_ref=ref, send_sem=send, recv_sem=recv, device_id=place.dev(), device_id_type=MESH
    ).wait_recv()


def bits(n):
    return [1 << k for k in range(n.bit_length() - 1)]


def norm_forward(u, gain, bias):
    centred = u - jnp.mean(u, axis=-1, keepdims=True)
    recip = lax.rsqrt(jnp.mean(centred * centred, axis=-1, keepdims=True) + NORM_EPSILON)
    normed = centred * recip
    return normed * gain + bias, normed, recip


def norm_back(grad, normed, recip, gain):
    e = grad * gain
    slope = jnp.mean(e * normed, axis=-1, keepdims=True)
    return recip * (e - jnp.mean(e, axis=-1, keepdims=True) - normed * slope)


def adam_update(param, grad, first, second, rate, decay):
    first_new = BETA_FIRST * first + (1.0 - BETA_FIRST) * grad
    second_new = BETA_SECOND * second + (1.0 - BETA_SECOND) * grad * grad
    first_hat = first_new * (1.0 / (1.0 - BETA_FIRST**STEP))
    second_hat = second_new * (1.0 / (1.0 - BETA_SECOND**STEP))
    param_new = param - rate * (first_hat / (jnp.sqrt(second_hat) + ADAM_EPSILON) + decay * param)
    return first_new, second_new, param_new


class Piece:
    def __init__(self, place, source, x_first, bufs, recv, sends):
        self.place, self.source, self.x_first, self.sends = place, source, x_first, sends
        self.s1 = source.at[place.c]
        self.r1, self.r2, self.s2, self.r3, self.s3, self.r4, self.final = bufs
        self.recv = recv

    def axis(self, x):
        p = self.place
        return (p.X, p.x, lambda v: p.dev(x=v)) if x else (p.Y, p.y, lambda v: p.dev(y=v))

    def send(self, axis, cut, buf, base):
        size, me, dev = axis
        for d in range(1, size):
            to = lax.rem(me + d, size)
            self.sends.push(cut(to), buf.at[d - 1], self.recv.at[base + d], dev(to), lambda: buf.at[0])

    def add(self, axis, own, buf, base):
        total = own.astype(F32)
        for d in range(1, axis[0]):
            arrived(self.place, buf.at[d - 1], self.recv.at[base + d], self.sends.sems.at[0])
            total = total + buf[d - 1].astype(F32)
        return total

    def hop0(self):
        p = self.place
        self.sends.push(self.source.at[1 - p.c], self.r1, self.recv.at[0], p.dev(c=1 - p.c), lambda: self.r1)

    def hop1(self):
        p = self.place
        arrived(p, self.r1, self.recv.at[0], self.sends.sems.at[0])
        self.s1[...] = (self.s1[...].astype(F32) + self.r1[...].astype(F32)).astype(BF)
        cut = lambda to: self.s1.at[to] if self.x_first else self.s1.at[:, :, to]
        self.send(self.axis(self.x_first), cut, self.r2, 0)

    def hop2(self):
        p = self.place
        own = self.s1[p.x] if self.x_first else self.s1[:, :, p.y]
        self.s2[...] = self.add(self.axis(self.x_first), own, self.r2, 0).astype(BF)
        cut = lambda to: self.s2.at[:, to] if self.x_first else self.s2.at[to]
        self.send(self.axis(not self.x_first), cut, self.r3, p.X)

    def hop3(self):
        p = self.place
        own = self.s2[:, p.y] if self.x_first else self.s2[p.x]
        self.s3[...] = self.add(self.axis(not self.x_first), own, self.r3, p.X).astype(BF)
        self.send((p.Z, p.z, lambda v: p.dev(z=v)), lambda to: self.s3.at[to], self.r4, 2 * p.X)

    def hop4(self):
        p = self.place
        self.final[...] = self.add((p.Z, p.z, None), self.s3[p.z], self.r4, 2 * p.X)


class Chunk:
    def __init__(self, place, g, dx, source, bufs, recv, sends):
        self.place, self.dx, self.sends = place, dx, sends
        r1, rx, r2 = bufs
        self.source, self.r1, self.rx, self.r2 = source.at[g], r1.at[g, dx], rx.at[g], r2.at[g]
        self.recv = recv.at[g]

    def hop0(self):
        p = self.place
        x = lax.rem(p.x + self.dx, p.X)
        self.sends.push(self.source.at[1 - p.c, x], self.r1, self.recv.at[self.dx], p.dev(c=1 - p.c), lambda: self.r1)

    def hop1(self):
        p = self.place
        x = lax.rem(p.x + self.dx, p.X)
        arrived(p, self.r1, self.recv.at[self.dx], self.sends.sems.at[0])
        total = self.source[p.c, x].astype(F32) + self.r1[...].astype(F32)
        if self.dx:
            self.source[p.c, x] = total.astype(BF)
            self.sends.push(
                self.source.at[p.c, x], self.rx.at[self.dx - 1], self.recv.at[p.X + self.dx], p.dev(x=x), lambda: self.r1
            )
            return
        for d in range(1, p.X):
            arrived(p, self.rx.at[d - 1], self.recv.at[p.X + d], self.sends.sems.at[0])
            total = total + self.rx[d - 1].astype(F32)
        self.source[p.c, x] = total.astype(BF)
        for d in range(1, p.batches):
            j = lax.rem(p.j + d, p.batches)
            self.sends.push(
                self.source.at[p.c, x, j], self.r2.at[d - 1], self.recv.at[2 * p.X + d], (j, p.x * 2 + p.c), lambda: self.r2.at[0]
            )

    def collect(self):
        p = self.place
        total = self.source[p.c, p.x, p.j].astype(F32)
        for d in range(1, p.batches):
            arrived(p, self.r2.at[d - 1], self.recv.at[2 * p.X + d], self.sends.sems.at[0])
            total = total + self.r2[d - 1].astype(F32)
        return total


def forward_sends(X, Y, Z, groups):
    part_a = groups * (Z - 1 + Y - 1) + (X - 1) * (1 + Z - 1 + Y - 1) + X
    part_b = (X - 1) + (Y - 1) + (Z - 1) + 1 + (Z - 1) * (X + Y - 1)
    part_b += Z * (2 * (X - 1) * (Y - 1) + (X - 1) + (Y - 1) + (X - 1) * (Y - 1))
    return part_a + part_b


def backward_sends(X, Y, Z, groups):
    stages = 1 + sum(len(bits(v)) for v in (X, Y, Z))
    return 2 * groups * (X + Y + Z - 2) + groups * (X + X - 1 + Y * Z - 1) + stages


def layer_kernel(
    batches, heads, owner_ref, length_ref, post_ref, weight_ref, gain_ref, bias_ref, dual_ref, pc_ref, dc_ref,
    post_out, dual_out, dmid_ref, partial_ref, grad_ref, norm_out, p_hbm,
    pick_ref, xs_ref, xst_ref, ga_ref, gb_ref, qk_ref, vx_ref, wide_ref, linv_ref, at_ref, dat_ref,
    w12_ref, wo_ref, mbt_ref, dft_ref, dbt_ref, dwo_ref, dqkv_ref,
    r1, xr2, yr2, xs2, ys2, r3, s3, r4, final, qr1, qrx, qr2, norm_send, norm_recv,
    recv_z, recv_y, recv_x, core_a, recv_b, send_f, recv_f, recv_q, norm_sems, send_r, p_sems,
):
    place = Place(batches, heads)
    groups, rows = NHEADS // heads, D // batches
    parts = 2 * groups
    X, Y, Z = place.X, place.Y, place.Z
    c, x, y, z = place.c, place.x, place.y, place.z
    step = pl.program_id(0)
    mid_at, dw_at, back_at = NHEADS, NHEADS + MID_STEPS, NHEADS + MID_STEPS + parts
    last_at = back_at + NHEADS - 1
    sends = Sends(send_f)
    dummy = send_f.at[0]

    def at_step(k):
        return pl.when(step == k)

    def core_push_a(xx):
        ref = ga_ref.at[c, xx]
        sends.push(ref, ref, core_a.at[xx], place.dev(c=1 - c), lambda: ga_ref.at[0, 0])

    def got_b(cc, xx, zz, yy):
        arrived(place, gb_ref.at[:, cc, xx, zz, yy], recv_b.at[cc, xx, zz, yy], dummy)

    def push_b(xx, zz, yy, device, cond=None):
        ref = gb_ref.at[:, c, xx, zz, yy]
        sends.push(ref, ref, recv_b.at[c, xx, zz, yy], device, lambda: gb_ref.at[:, 0, 0, 0, 0], cond)

    def side(offset):
        zo = lax.rem(z + offset, Z)
        low = lambda: lax.rem(place.z + offset, Z) < (3 * Z) // 4
        for xx in place.xs:
            got_b(c, xx, zo, y)
            for yy in place.ys:
                push_b(xx, zo, y, place.dev(y=yy), low)
            push_b(xx, zo, y, place.dev(c=1 - c))
        for yy in place.ys:
            got_b(c, x, zo, yy)
            for xx in place.xs:
                push_b(x, zo, yy, place.dev(x=xx), lambda: jnp.logical_not(low()))
            push_b(x, zo, yy, place.dev(c=1 - c))

    @at_step(0)
    def _():
        weight = weight_ref[...]
        for g in range(groups):
            ga_ref[c, x, z, y, g] = weight[:, g * GROUPW : g * GROUPW + PART].astype(BF)
        peers = [place.dev(z=zz, y=yy) for zz in [z] + place.zs for yy in [y] + place.ys][1:]
        place.greet(peers + [place.dev(x=xx) for xx in place.xs] + [place.dev(c=1 - c)])
        for g in range(groups):
            own = ga_ref.at[c, x, z, y, g]
            for zz in place.zs:
                sends.push(own, own, recv_z.at[g, z], place.dev(z=zz), lambda: ga_ref.at[0, 0, 0, 0, 0])
        own = ga_ref.at[c, x, z, y]
        for xx in place.xs:
            sends.push(own, own, recv_x.at[x, z], place.dev(x=xx), lambda: ga_ref.at[0, 0, 0, 0])
        for k in range(parts):
            low = (k % groups) * GROUPW + (2 - k // groups) * PART
            gb_ref[k, c, x, z, y] = weight[:, low : low + PART].astype(BF)
        for yy in place.ys:
            push_b(x, z, y, place.dev(y=yy))
        for xx in place.xs:
            push_b(x, z, y, place.dev(x=xx))
        lane = lax.broadcasted_iota(jnp.int32, (1, D), 1)
        source = lane % rows
        for b in range(batches):
            source = jnp.where(lane // rows == b, source + owner_ref[b] * rows, source)
        pick = (lax.broadcasted_iota(jnp.int32, (D, D), 0) == source).astype(F32).astype(BF)
        pick_ref[...] = pick
        ordered = dot(post_ref[...], pick, 1, 0).astype(BF)
        xs_ref[...] = ordered
        xst_ref[...] = ordered.T
        for g in range(groups):
            for zz in place.zs:
                arrived(place, ga_ref.at[c, x, zz, y, g], recv_z.at[g, zz], dummy)
            column = ga_ref.at[c, x, :, y, g]
            for yy in place.ys:
                sends.push(column, column, recv_y.at[g, y], place.dev(y=yy), lambda: ga_ref.at[0, 0, :, 0, 0])
        for zz in place.zs:
            push_b(x, z, y, place.dev(z=zz))
        for xx in place.xs:
            for zz in place.zs:
                block = ga_ref.at[c, x, zz, y]
                sends.push(block, block, recv_x.at[x, zz], place.dev(x=xx), lambda: ga_ref.at[0, 0, 0, 0])
        push_b(x, z, y, place.dev(c=1 - c))

    for g in range(groups):

        @at_step(g)
        def _(g=g):
            for yy in place.ys:
                arrived(place, ga_ref.at[c, x, :, yy, g], recv_y.at[g, yy], dummy)
            if g == groups - 1:
                for yy in place.ys:
                    column = ga_ref.at[c, x, :, yy]
                    for xx in place.xs:
                        sends.push(
                            column, column, recv_x.at[x, Z + yy], place.dev(x=xx), lambda: ga_ref.at[0, 0, :, 0]
                        )
                core_push_a(x)

    for k in range(1, heads):

        @at_step(k * groups)
        def _(k=k):
            xx = lax.rem(x + k // 2, X)
            if k % 2 == 0:
                for zz in [z] + place.zs:
                    arrived(place, ga_ref.at[c, xx, zz, y], recv_x.at[xx, zz], dummy)
                for yy in place.ys:
                    arrived(place, ga_ref.at[c, xx, :, yy], recv_x.at[xx, Z + yy], dummy)
                core_push_a(xx)
            else:
                arrived(place, ga_ref.at[1 - c, xx], core_a.at[xx], dummy)

    @at_step(B_STEPS[0])
    def _():
        for zz in place.zs:
            got_b(c, x, zz, y)
            for xx in place.xs:
                push_b(x, zz, y, place.dev(x=xx))
            for yy in place.ys:
                push_b(x, zz, y, place.dev(y=yy))
            push_b(x, zz, y, place.dev(c=1 - c))
        side(0)

    @at_step(B_STEPS[1])
    def _():
        for offset in range(1, Z):
            side(offset)

    def p_store(i):
        slot = lax.rem(i, 4)
        return pltpu.make_async_copy(wide_ref.at[pl.ds(2 * slot, 2)], p_hbm.at[i], p_sems.at[slot])

    def p_fetch(i):
        g, r = i // heads, i % heads
        spot = (heads - 2 - 2 * (r // 2) + r % 2) * groups + g
        slot = lax.rem(i, 2)
        return pltpu.make_async_copy(p_hbm.at[spot], wide_ref.at[pl.ds(2 * slot, 2)], p_sems.at[slot])

    @pl.when(step < mid_at)
    def _():
        @pl.when(step >= 4)
        def _():
            p_store(step - 4).wait()

        q, g = step // groups, step % groups
        cc, xx = (c + q) % 2, lax.rem(x + q // 2, X)
        head = (xx * 2 + cc) * groups + g
        w = ga_ref[cc, xx, :, :, g].reshape(D, PART)
        proj = dot(xs_ref[...], w, 1, 0)
        lane = lax.broadcasted_iota(jnp.int32, (SEQ_LEN, 128), 1)
        qk = proj[:, :128].astype(BF)
        qk = jnp.where(lane < DH, qk * BF(DH**-0.5), qk)
        v = proj[:, 128:].astype(BF)
        vx = jnp.where(lane < DH, v, jnp.where(lane < DH + 2, BF(1), BF(0)))
        qk_ref[head] = qk
        vx_ref[head] = vx
        q_only = jnp.where(lane < DH, qk, BF(0))
        kq = jnp.concatenate([qk[:, DH:], qk[:, :DH]], axis=1)
        vxt = vx.T[: DH + 8]
        keep = lax.broadcasted_iota(jnp.int32, (SEQ_LEN, 1), 0) < length_ref[0]
        s = dot(kq, q_only, 1, 1)
        s = jnp.where(keep, s, F32(MASK_VALUE))
        m = jnp.max(s, axis=0, keepdims=True)
        p = jnp.exp(s - m).astype(BF)
        slot = lax.rem(step, 4)
        wide_ref[2 * slot] = p[:, : SEQ_LEN // 2]
        wide_ref[2 * slot + 1] = p[:, SEQ_LEN // 2 :]
        o = dot(vxt, p, 1, 0)
        r = 1.0 / o[DH : DH + 1]
        linv_ref[head] = r
        at_ref[head] = (o[:DH] * r).astype(BF)
        p_store(step).start()

    @at_step(mid_at)
    def _():
        for i in range(NHEADS - 4, NHEADS):
            p_store(i).wait()
        for offset in range(Z):
            zz = lax.rem(z + offset, Z)
            for yy in place.ys:
                for xx in place.xs:
                    got_b(c, xx, zz, yy)
                    push_b(xx, zz, yy, place.dev(c=1 - c))
        for xx in range(X):
            for zz in range(Z):
                for yy in range(Y):
                    got_b(1 - c, xx, zz, yy)
        held = []
        for b in range(batches):
            found = 0
            for j in range(1, batches):
                found = jnp.where(owner_ref[j] == b, j, found)
            held.append(found)
        for b in range(batches):
            there = slice(b * rows, (b + 1) * rows)
            for h in range(NHEADS):
                g, xx, cc = h % groups, (h // groups) // 2, (h // groups) % 2
                wo_ref[there, h * DH : (h + 1) * DH] = ga_ref[cc, xx, held[b] // Y, held[b] % Y, g][:, 3 * DH :]
                for k in range(2):
                    w12_ref[1 - k, there, h * PART : (h + 1) * PART] = gb_ref[
                        k * groups + g, cc, xx, held[b] // Y, held[b] % Y
                    ]
        norm_send[0] = jnp.zeros((4, D), F32)

    @pl.when(jnp.logical_and(step >= mid_at, step < dw_at))
    def _():
        t = step - mid_at
        block = SEQ_LEN // MID_STEPS
        here = pl.ds(pl.multiple_of(t * block, block), block)
        at = at_ref[:, :, here].reshape(D, block)
        gain, bias = gain_ref[...], bias_ref[...]
        w1, w2, wo, pick = w12_ref[0], w12_ref[1], wo_ref[...], pick_ref[...]
        branch = dot(at, wo, 0, 1)
        middle, n1, r1_ = norm_forward(post_ref[here, :].astype(F32) + branch, gain[0:1], bias[0:1])
        middle_low = middle.astype(BF)
        pre = dot(middle_low, w1, 1, 0)
        cdf = 0.5 + 0.5 * lax.erf(pre * F32(math.sqrt(0.5)))
        density = jnp.exp(pre * pre * F32(-0.5)) * F32(1.0 / math.sqrt(2.0 * math.pi))
        hidden = (pre * cdf).astype(BF)
        slope = cdf + pre * density
        feed = dot(hidden, w2, 1, 1)
        out, n2, r2_ = norm_forward(middle + feed, gain[1:2], bias[1:2])
        post_out[...] = out.astype(BF)
        dual_out[...] = dual_ref[...] + branch + feed
        keep = t * block + lax.broadcasted_iota(jnp.int32, (block, 1), 0) < length_ref[0]
        d_out = jnp.where(keep, pc_ref[...].astype(F32), 0.0)
        d_dual = jnp.where(keep, dc_ref[...].astype(F32), 0.0)
        d_pre = norm_back(d_out, n2, r2_, gain[1:2])
        d_feed = (d_pre + d_dual).astype(BF)
        d_hidden = dot(d_feed, w2, 1, 0)
        d_hidden_pre = (d_hidden * slope).astype(BF)
        for k in range(4):
            wide_ref[k, here, :] = hidden[:, k * 512 : (k + 1) * 512]
            wide_ref[4 + k, here, :] = d_hidden_pre[:, k * 512 : (k + 1) * 512]
        d_middle = d_pre + dot(d_hidden_pre, w1, 1, 1)
        d_mid = norm_back(d_middle, n1, r1_, gain[0:1])
        dmid_ref[...] = d_mid
        d_branch = (d_mid + d_dual).astype(BF)
        mbt_ref[:, here] = dot(pick, middle_low, 0, 1).astype(BF)
        dft_ref[:, here] = dot(pick, d_feed, 0, 1).astype(BF)
        dbt_ref[:, here] = dot(pick, d_branch, 0, 1).astype(BF)
        dat_ref[:, :, here] = dot(wo, d_branch, 0, 1).astype(BF).reshape(NHEADS, DH, block)
        sums = [jnp.sum(v, axis=0, keepdims=True) for v in (d_middle * n1, d_out * n2, d_middle, d_out)]
        norm_send[0] = norm_send[0] + jnp.concatenate(sums, axis=0)

    reduce_sends = Sends(send_r)
    pieces = []
    for k in range(parts):
        x_first = k == 0
        bufs = (r1.at[k], xr2.at[0], xs2.at[0]) if x_first else (r1.at[k], yr2.at[k - 1], ys2.at[k - 1])
        bufs += tuple(b.at[k] for b in (r3, s3, r4, final))
        pieces.append(Piece(place, gb_ref.at[k], x_first, bufs, recv_f.at[k], reduce_sends))
    chunks = [
        Chunk(place, g, dx, dqkv_ref, (qr1, qrx, qr2), recv_q, reduce_sends)
        for g in range(groups)
        for dx in reversed(range(X))
    ]
    partners = [place.dev(c=1 - c)]
    flip = lambda v, b: v + b - 2 * b * ((v // b) % 2)
    partners += [place.dev(x=flip(x, b)) for b in bits(X)]
    partners += [place.dev(y=flip(y, b)) for b in bits(Y)]
    partners += [place.dev(z=flip(z, b)) for b in bits(Z)]

    def norm_push(k):
        reduce_sends.push(norm_send.at[k], norm_recv.at[k], norm_sems.at[k], partners[k], lambda: norm_send.at[0])

    def norm_pull(k):
        arrived(place, norm_recv.at[k], norm_sems.at[k], send_r.at[0])
        norm_send[k + 1] = norm_send[k] + norm_recv[k]

    for k in range(parts):

        @at_step(dw_at + k)
        def _(k=k):
            if k == 0:
                sends.drain(place)
                norm_push(0)
                dwo = dot(dbt_ref[...], at_ref[...].reshape(D, SEQ_LEN), 1, 1).astype(BF)
                empty = jnp.zeros((D, DH), BF)
                for h in range(NHEADS):
                    dwo_ref[h] = jnp.concatenate([empty, dwo[:, h * DH : (h + 1) * DH]], axis=1)
            if k == groups:
                p_fetch(0).start()
                p_fetch(1).start()
            left = (dft_ref if k < groups else mbt_ref)[...]
            for device in range(heads):
                h = device * groups + k % groups
                held = wide_ref[4 * (k // groups) + h // 2, :, (h % 2) * PART : (h % 2 + 1) * PART]
                grad = dot(left, held, 1, 0).astype(BF)
                gb_ref[k, device % 2, device // 2] = grad.reshape(Z, Y, rows, PART)
            pieces[k].hop0()
            if k:
                pieces[k - 1].hop1()

    @pl.when(step >= back_at)
    def _():
        i = step - back_at
        p_fetch(i).wait()
        g, r = i // heads, i % heads
        cc, xx = (c + r) % 2, lax.rem(x + X - 1 - r // 2, X)
        head = (xx * 2 + cc) * groups + g
        lane = lax.broadcasted_iota(jnp.int32, (SEQ_LEN, 128), 1)
        row = lax.broadcasted_iota(jnp.int32, (DH, SEQ_LEN), 0)
        qk, vx = qk_ref[head], vx_ref[head]
        do = dat_ref[head].astype(F32) * linv_ref[head]
        inner = -jnp.sum(do * at_ref[head].astype(F32), axis=0, keepdims=True)
        coarse = inner.astype(BF).astype(F32)
        tail = jnp.where(row == 0, coarse, jnp.where(row == 1, inner - coarse, 0.0))
        et = jnp.concatenate([do, tail], axis=0).astype(BF)
        e = et.T
        kt = qk.T[DH:]
        kq = jnp.concatenate([qk[:, DH:], qk[:, :DH]], axis=1)
        dk = jnp.zeros((SEQ_LEN, 128), F32)
        dv = jnp.zeros((SEQ_LEN, 128), F32)
        dqs = []
        slot = lax.rem(i, 2)
        for b in range(2):
            sl = slice(b * (SEQ_LEN // 2), (b + 1) * (SEQ_LEN // 2))
            p = wide_ref[2 * slot + b]
            ds = (p.astype(F32) * dot(vx, et[:, sl], 1, 0)).astype(BF)
            dv = dv + dot(p, e[sl], 1, 0)
            dk = dk + dot(ds, kq[sl], 1, 0)
            dqs.append(dot(kt, ds, 1, 0))
        dqt = jnp.concatenate(dqs, axis=1) * F32(DH**-0.5)
        dq = jnp.concatenate([dqt, jnp.zeros_like(dqt)], axis=0).T
        d_proj = jnp.concatenate([jnp.where(lane < DH, dq, dk), jnp.where(lane < DH, dv, 0.0)], axis=1).astype(BF)
        cols = pl.ds(pl.multiple_of(head * PART, PART), PART)
        w12_ref[0, :, cols] = d_proj[: SEQ_LEN // 2]
        w12_ref[1, :, cols] = d_proj[SEQ_LEN // 2 :]
        dw = dot(xst_ref[...], d_proj, 1, 0)
        dw = jnp.concatenate([dw[:, :128], dw[:, 128:] + dwo_ref[head].astype(F32)], axis=1).astype(BF)
        dqkv_ref[g, cc, xx] = dw.reshape(dqkv_ref.shape[3:])

        @pl.when(i + 2 < NHEADS)
        def _():
            p_fetch(i + 2).start()

    todo = [[] for _ in range(NHEADS)]
    todo[0] += [pieces[-1].hop1, lambda: norm_pull(0), lambda: norm_push(1)]
    for n, chunk in enumerate(chunks):
        todo[2 * n + 1].append(chunk.hop0)
        if n + 1 < len(chunks):
            todo[2 * n + 2].append(chunk.hop1)
    half = parts // 2
    todo[1] += [p.hop2 for p in pieces[:half]]
    todo[2] += [lambda: norm_pull(1), lambda: norm_push(2)]
    todo[3] += [p.hop2 for p in pieces[half:]] + [p.hop3 for p in pieces[:half]]
    todo[4] += [lambda: norm_pull(2), lambda: norm_push(3)]
    todo[5] += [p.hop3 for p in pieces[half:]] + [p.hop4 for p in pieces[:half]]
    todo[6] += [lambda: norm_pull(3), lambda: norm_push(4)]
    todo[7] += [p.hop4 for p in pieces[half:]]

    for t in range(NHEADS):

        @at_step(back_at + t)
        def _(t=t):
            for act in todo[t]:
                act()

    @at_step(last_at)
    def _():
        for k in range(4, len(partners)):
            norm_pull(k)
            if k + 1 < len(partners):
                norm_push(k + 1)
        norm_out[...] = norm_send[len(partners)]
        chunks[-1].hop1()
        table = []
        for h in range(NHEADS):
            g, xx, cc = h % groups, (h // groups) // 2, (h // groups) % 2
            table.append(ga_ref[cc, xx, :, :, g].reshape(D, PART))
        table = jnp.concatenate(table, axis=1)
        for k in range(2):
            ordered = dot(w12_ref[k], table, 1, 1).astype(BF)
            partial_ref[k * (SEQ_LEN // 2) : (k + 1) * (SEQ_LEN // 2)] = dot(ordered, pick_ref[...], 1, 1).astype(BF)
        for g in range(groups):
            low = g * GROUPW
            grad_ref[:, low + PART : low + 2 * PART] = final[groups + g]
            grad_ref[:, low + 2 * PART : low + 3 * PART] = final[g]
            grad_ref[:, low : low + PART] = chunks[(g + 1) * X - 1].collect()
        reduce_sends.drain(place)


def layer_call(owner, length, post, weights, gain, bias, dual, pc, dc, batches, heads):
    groups, rows = NHEADS // heads, D // batches
    parts = 2 * groups
    X = Y = heads // 2
    Z = batches // Y
    tokens = post.shape[0]
    assert tokens == SEQ_LEN
    block = tokens // MID_STEPS
    stages = 1 + sum(len(bits(v)) for v in (X, Y, Z))
    scalar = pl.BlockSpec(memory_space=pltpu.SMEM)
    whole = lambda a: pl.BlockSpec(a.shape, lambda i: (0,) * len(a.shape), pipeline_mode=pl.Buffered(1))
    token = pl.BlockSpec((block, D), lambda i: (jnp.clip(i - NHEADS, 0, MID_STEPS - 1), 0))
    outs = [
        jax.ShapeDtypeStruct((tokens, D), BF),
        jax.ShapeDtypeStruct((tokens, D), F32),
        jax.ShapeDtypeStruct((tokens, D), F32),
        jax.ShapeDtypeStruct((tokens, D), BF),
        jax.ShapeDtypeStruct((rows, groups * GROUPW), F32),
        jax.ShapeDtypeStruct((4, D), F32),
        jax.ShapeDtypeStruct((NHEADS, 2, tokens, tokens // 2), BF),
    ]
    dma = pltpu.SemaphoreType.DMA
    return pl.pallas_call(
        functools.partial(layer_kernel, batches, heads),
        grid=(NHEADS + MID_STEPS + parts + NHEADS,),
        in_specs=[scalar, scalar, whole(post), whole(weights), whole(gain), whole(bias), token, token, token],
        out_specs=[token, token, token] + [whole(a) for a in outs[3:6]] + [pl.BlockSpec(memory_space=pl.ANY)],
        out_shape=outs,
        scratch_shapes=[
            pltpu.VMEM((D, D), BF),
            pltpu.VMEM((tokens, D), BF),
            pltpu.VMEM((D, tokens), BF),
            pltpu.VMEM((2, X, Z, Y, groups, rows, PART), BF),
            pltpu.VMEM((parts, 2, X, Z, Y, rows, PART), BF),
            pltpu.VMEM((NHEADS, tokens, 128), BF),
            pltpu.VMEM((NHEADS, tokens, 128), BF),
            pltpu.VMEM((8, tokens, tokens // 2), BF),
            pltpu.VMEM((NHEADS, 1, tokens), F32),
            pltpu.VMEM((NHEADS, DH, tokens), BF),
            pltpu.VMEM((NHEADS, DH, tokens), BF),
            pltpu.VMEM((2, D, FF), BF),
            pltpu.VMEM((D, D), BF),
            pltpu.VMEM((D, tokens), BF),
            pltpu.VMEM((D, tokens), BF),
            pltpu.VMEM((D, tokens), BF),
            pltpu.VMEM((NHEADS, D, 128), BF),
            pltpu.VMEM((groups, 2, X, batches, rows, PART), BF),
            pltpu.VMEM((parts, X, Z, Y, rows, PART), BF),
            pltpu.VMEM((1, X - 1, Z, Y, rows, PART), BF),
            pltpu.VMEM((parts - 1, Y - 1, X, Z, rows, PART), BF),
            pltpu.VMEM((1, Z, Y, rows, PART), BF),
            pltpu.VMEM((parts - 1, X, Z, rows, PART), BF),
            pltpu.VMEM((parts, X - 1, Z, rows, PART), BF),
            pltpu.VMEM((parts, Z, rows, PART), BF),
            pltpu.VMEM((parts, Z - 1, rows, PART), BF),
            pltpu.VMEM((parts, rows, PART), F32),
            pltpu.VMEM((groups, X, batches, rows, PART), BF),
            pltpu.VMEM((groups, X - 1, batches, rows, PART), BF),
            pltpu.VMEM((groups, batches - 1, rows, PART), BF),
            pltpu.VMEM((stages + 1, 4, D), F32),
            pltpu.VMEM((stages, 4, D), F32),
            dma((groups, Z)),
            dma((groups, Y)),
            dma((X, Z + Y)),
            dma((X,)),
            dma((2, X, Z, Y)),
            dma((forward_sends(X, Y, Z, groups),)),
            dma((parts, 2 * X + Z)),
            dma((groups, 2 * X + batches)),
            dma((stages,)),
            dma((backward_sends(X, Y, Z, groups),)),
            dma((4,)),
        ],
        name="layer",
        compiler_params=pltpu.CompilerParams(
            collective_id=1, has_side_effects=True, vmem_limit_bytes=VMEM_BYTES
        ),
    )(owner, length, post, weights, gain, bias, dual, pc, dc)


def update_kernel(
    post_in, dual_in, dmid_ref, partial_ref, grad_ref, weight_ref, first_ref, second_ref,
    ngrad_ref, nparam_ref, nfirst_ref, nsecond_ref,
    post_out, dual_out, grad_out, first_out, second_out, weight_out, nfirst_out, nsecond_out, nparam_out,
):
    post_out[...] = post_in[...]
    dual_out[...] = dual_in[...]
    grad_out[...] = dmid_ref[...] + partial_ref[...].astype(F32)
    first_out[...], second_out[...], weight_out[...] = adam_update(
        weight_ref[...], grad_ref[...], first_ref[...], second_ref[...], WEIGHT_RATE, WEIGHT_DECAY
    )
    nfirst_out[...], nsecond_out[...], nparam_out[...] = adam_update(
        nparam_ref[...], ngrad_ref[...], nfirst_ref[...], nsecond_ref[...], NORM_RATE, 0.0
    )


def update_call(post, dual, dmid, partial, grad, weights, first, second, ngrad, nparam, nfirst, nsecond):
    steps = 2
    cut = lambda a: pl.BlockSpec((a.shape[0] // steps, a.shape[1]), lambda i: (i, 0))
    same = lambda a: pl.BlockSpec(a.shape, lambda i: (0, 0))
    outs = [post, dual, dmid, weights, weights, weights, nparam, nparam, nparam]
    return pl.pallas_call(
        update_kernel,
        grid=(steps,),
        in_specs=[cut(a) for a in (post, dual, dmid, partial, grad, weights, first, second)]
        + [same(a) for a in (ngrad, nparam, nfirst, nsecond)],
        out_specs=[cut(a) for a in outs[:6]] + [same(a) for a in outs[6:]],
        out_shape=[jax.ShapeDtypeStruct(a.shape, a.dtype) for a in outs],
        name="update",
        compiler_params=pltpu.CompilerParams(vmem_limit_bytes=VMEM_BYTES),
    )(post, dual, dmid, partial, grad, weights, first, second, ngrad, nparam, nfirst, nsecond)


def shards(
    post_stream,
    dual_stream,
    post_cotangent,
    dual_cotangent,
    seq_lengths,
    owner_slots,
    weights,
    first_moment,
    second_moment,
    norm_gain,
    norm_bias,
    norm_first,
    norm_second,
):
    batches, heads = lax.axis_size("batch"), lax.axis_size("head")
    length = lax.dynamic_slice(seq_lengths, (lax.axis_index("head"),), (1,))
    post, dual, dmid, partial, grad, norm_grad, _ = layer_call(
        owner_slots, length, post_stream, weights, norm_gain, norm_bias, dual_stream, post_cotangent, dual_cotangent,
        batches, heads,
    )
    norm_params = jnp.concatenate([norm_gain, norm_bias], axis=0)
    return update_call(
        post, dual, dmid, partial, grad, weights, first_moment, second_moment,
        norm_grad, norm_params, norm_first, norm_second,
    )


def solution(mesh):
    tokens, table, copied = P(("batch", "head"), None), P("batch", "head"), P()
    in_specs = (tokens,) * 4 + (P("batch"), copied) + (table,) * 3 + (copied,) * 4
    out_specs = (tokens,) * 3 + (table,) * 3 + (copied,) * 3
    return jax.shard_map(shards, mesh=mesh, in_specs=in_specs, out_specs=out_specs, check_vma=False)
```

time: 683 us -> 129 us (0.19); the launches traced: 672 us -> 128 us
  waiting for transfers between devices: 220 us -> 0 us
  local copies, waits for them, and re-layouts: 128 us -> 1.25 us
  matrix products: 126 us -> 0 us
  Pallas kernels: 0 us -> 126 us
  blocking collectives: 103 us -> 0 us
  other arithmetic: 78.6 us -> 0.6 us
  between operations: 15.4 us -> 0.67 us
    reduce_scatter x5 -> x0, waiting for transfers between devices: 187 us -> none  [the longest x1 144 us: shards(): lax.psum_scatter(feed_grads, ('batch', 'head'), scatter_dimension=0, tile...]
    pallas_call x0 -> x2, Pallas kernels: none -> 126 us  [the longest x1 121 us: layer_call(): pl.pallas_call(functools.partial(layer_kernel, batches, heads), grid=(NHE...]
    dot_general x40 -> x0, matrix products: 126 us -> none  [the longest x1 24.1 us: shards(): jnp.einsum('tbr,bhrgc->thgc', middle_slots, w_up, preferred_element_type=...]
    all_gather x2 -> x0, blocking collectives: 63.9 us -> none  [the longest x1 33.1 us: shards(): lax.all_gather(qkv_part, 'batch', axis=0, tiled=True)]
    psum x1 -> x0, blocking collectives: 39.6 us -> none  [shards(): norm_grads = lax.psum(norm_local, ('batch', 'head'))]
    reshape x10 -> x0, local copies, waits for them, and re-layouts: 37 us -> none  [the longest x1 11.8 us: shards(): feed_all.reshape(batches, head_devices, row_block, groups_here, 2, hidden...]
    all_gather x3 -> x0, waiting for transfers between devices: 33.3 us -> none  [the longest x1 33.3 us: shards(): branch_group = lax.all_gather(grad_branch, 'head', axis=0, tiled=True)]
    convert_element_type x13 -> x0, other arithmetic: 30.3 us -> none  [the longest x4 12.4 us: attend_backward(): grad_scores = (soft_weights * (grad_soft - row_inner)).astype(jnp.bfloat16)]
  transfers between devices with their start and end apart: 8 -> 0, of which waited for: 4 -> 0; matrix products, arithmetic and copies ran while one was open for 35% -> 0% of each run, Pallas kernels for 0% -> 0%
where the time goes in v3:
time: 129 us; the launch traced here: 128 us
  Pallas kernels  126 us (98%)
    pallas_call x1, Pallas kernels, layer_call(): pl.pallas_call(functools.partial(layer_kernel, batches, heads), grid=(NHE...  121 us
    pallas_call x1, Pallas kernels, update_call(): pl.pallas_call(update_kernel, grid=(steps,), in_specs=[cut(a) for a in (p...  5.41 us

profile of v3, /device:TPU:0, one launch (start us, length us, event | category | flops | bytes accessed | tf_op | source)
XLA Modules:
  0.0 128.4 jit_solution(16197457681641783078)
XLA Ops:
  0.6 1.2 dynamic_slice.3.length_ref
  1.9 0.0 copy-start
  1.9 0.0 copy-start.1
  1.9 120.5 %layer.1 = (bf16[1024,512]{1,0:T(8,128)(2,1)}, f32[1024,512]{1,0:T(8,128)}, f32[1024,512]{1,0:T(8,128)}, bf16[1024,512]{1,0:T(8,128)(2,1)}, f32[64,1536]{1,0:T(8...) custom-call(s32[8]{0:T(128)} %owner_ref.1, s32[1]{0:T(128)} %dynamic_slice.3.length_ref, ...), custom_call_target="tpu_custom_call" | custom-call | tf_op jit(solution)/shard_map/layer/pallas_call | solution.py:651
  122.4 0.0 copy-done
  122.4 0.0 copy-done.1
  122.4 0.6 pad_maximum_fusion.nparam_ref
  123.0 5.4 %update.1 = (bf16[1024,512]{1,0:T(8,128)(2,1)}, f32[1024,512]{1,0:T(8,128)}, f32[1024,512]{1,0:T(8,128)}, f32[64,1536]{1,0:T(8,128)}, f32[64,1536]{1,0:T(8,128)}...) custom-call(bf16[1024,512]{1,0:T(8,128)(2,1)} %get-tuple-element.15.post_in, ...), custom_call_target="tpu_custom_call" | custom-call | tf_op jit(solution)/shard_map/update/pallas_call | solution.py:730
Async XLA Ops:
  1.9 120.5 %copy-start = (f32[2,512]{1,0:T(2,128)S(1)}, f32[2,512]{1,0:T(2,128)}, u32[]{:S(2)}) copy-start(f32[2,512]{1,0:T(2,128)} %gain_ref.1) | copy-start | bytes 12292
  1.9 120.5 %copy-start.1 = (f32[2,512]{1,0:T(2,128)S(1)}, f32[2,512]{1,0:T(2,128)}, u32[]{:S(2)}) copy-start(f32[2,512]{1,0:T(2,128)} %bias_ref.1) | copy-start | bytes 12292

commit v4 on v3

v4 whole, which is shorter than its diff:
```python
import functools
import math

import jax
import jax.numpy as jnp
from jax import lax
from jax.experimental import pallas as pl
from jax.experimental.pallas import tpu as pltpu
from jax.sharding import PartitionSpec as P

D = 512
FF = 2048
NHEADS = 8
DH = 64
SEQ_LEN = 1024
STEP = 10
GROUPW = 768
PART = 256

BETA_FIRST = 0.9
BETA_SECOND = 0.999
ADAM_EPSILON = 1e-08
WEIGHT_DECAY = 0.1
WEIGHT_RATE = 0.2
NORM_RATE = 0.2
NORM_EPSILON = 1e-05
MASK_VALUE = -1000000000.0

MESH = pl.DeviceIdType.MESH
F32 = jnp.float32
BF = jnp.bfloat16
VMEM_BYTES = 63 << 20
B_PLAN = {'first': [], 'after': [('send', 1), ('send', 2), ('send', 3)], 0: [], 1: [], 2: [('side', 0)], 3: [('pass', 1), ('pass', 2), ('pass', 3)], 4: [], 5: [('side', 1)], 6: [('side', 2)], 7: [('side', 3)]}
MID_STEPS = 2
UNROLL = 2
X_FIRST = (0, 2)


def dot(a, b, ca, cb):
    return lax.dot_general(a, b, (((ca,), (cb,)), ((), ())), preferred_element_type=F32)


class Place:
    def __init__(self, batches, heads):
        self.X = self.Y = heads // 2
        self.Z = batches // self.Y
        self.batches, self.heads = batches, heads
        batch, head = lax.axis_index("batch"), lax.axis_index("head")
        self.j = batch
        self.z, self.y = batch // self.Y, batch % self.Y
        self.x, self.c = head // 2, head % 2
        self.xs = [lax.rem(self.x + d, self.X) for d in range(1, self.X)]
        self.ys = [lax.rem(self.y + d, self.Y) for d in range(1, self.Y)]
        self.zs = [lax.rem(self.z + d, self.Z) for d in range(1, self.Z)]

    def dev(self, z=None, y=None, x=None, c=None):
        z = self.z if z is None else z
        y = self.y if y is None else y
        x = self.x if x is None else x
        c = self.c if c is None else c
        return (z * self.Y + y, x * 2 + c)

    def greet(self, devices):
        barrier = pltpu.get_barrier_semaphore()
        for device in devices:
            pl.semaphore_signal(barrier, inc=1, device_id=device, device_id_type=MESH)
        pl.semaphore_wait(barrier, len(devices))

    def plane(self):
        return [(x, y) for x in [self.x] + self.xs for y in [self.y] + self.ys][1:]


class Sends:
    def __init__(self, sems):
        self.sems, self.count, self.made = sems, 0, []

    def push(self, src, dst, recv, device, like, cond=None, given=None):
        copy = pltpu.make_async_remote_copy(
            src_ref=src, dst_ref=dst, send_sem=self.sems.at[self.count], recv_sem=recv,
            device_id=device, device_id_type=MESH,
        )
        if cond is None:
            copy.start()
        else:
            pl.when(cond())(lambda: copy.start())
        self.made.append((self.count, like, cond or given))
        self.count += 1

    def drain(self, place):
        for k, like, cond in self.made:
            sent = pltpu.make_async_remote_copy(
                src_ref=like(), dst_ref=like(), send_sem=self.sems.at[k], recv_sem=self.sems.at[k],
                device_id=place.dev(), device_id_type=MESH,
            )
            if cond is None:
                sent.wait_send()
            else:
                pl.when(cond())(lambda sent=sent: sent.wait_send())


def arrived(place, ref, recv, send):
    pltpu.make_async_remote_copy(
        src_ref=ref, dst_ref=ref, send_sem=send, recv_sem=recv, device_id=place.dev(), device_id_type=MESH
    ).wait_recv()


def bits(n):
    return [1 << k for k in range(n.bit_length() - 1)]


def norm_forward(u, gain, bias):
    centred = u - jnp.mean(u, axis=-1, keepdims=True)
    recip = lax.rsqrt(jnp.mean(centred * centred, axis=-1, keepdims=True) + NORM_EPSILON)
    normed = centred * recip
    return normed * gain + bias, normed, recip


def norm_back(grad, normed, recip, gain):
    e = grad * gain
    slope = jnp.mean(e * normed, axis=-1, keepdims=True)
    return recip * (e - jnp.mean(e, axis=-1, keepdims=True) - normed * slope)


def adam_update(param, grad, first, second, rate, decay):
    first_new = BETA_FIRST * first + (1.0 - BETA_FIRST) * grad
    second_new = BETA_SECOND * second + (1.0 - BETA_SECOND) * grad * grad
    first_hat = first_new * (1.0 / (1.0 - BETA_FIRST**STEP))
    second_hat = second_new * (1.0 / (1.0 - BETA_SECOND**STEP))
    param_new = param - rate * (first_hat / (jnp.sqrt(second_hat) + ADAM_EPSILON) + decay * param)
    return first_new, second_new, param_new


class Piece:
    def __init__(self, place, source, x_first, bufs, recv, sends):
        self.place, self.source, self.x_first, self.sends = place, source, x_first, sends
        self.s1 = source.at[place.c]
        self.r1, self.r2, self.s2, self.r3, self.s3, self.r4, self.final = bufs
        self.recv = recv

    def axis(self, x):
        p = self.place
        return (p.X, p.x, lambda v: p.dev(x=v)) if x else (p.Y, p.y, lambda v: p.dev(y=v))

    def send(self, axis, cut, buf, base):
        size, me, dev = axis
        for d in range(1, size):
            to = lax.rem(me + d, size)
            self.sends.push(cut(to), buf.at[d - 1], self.recv.at[base + d], dev(to), lambda: buf.at[0])

    def add(self, axis, own, buf, base):
        total = own.astype(F32)
        for d in range(1, axis[0]):
            arrived(self.place, buf.at[d - 1], self.recv.at[base + d], self.sends.sems.at[0])
            total = total + buf[d - 1].astype(F32)
        return total

    def hop0(self):
        p = self.place
        self.sends.push(self.source.at[1 - p.c], self.r1, self.recv.at[0], p.dev(c=1 - p.c), lambda: self.r1)

    def hop1(self):
        p = self.place
        arrived(p, self.r1, self.recv.at[0], self.sends.sems.at[0])
        self.s1[...] = (self.s1[...].astype(F32) + self.r1[...].astype(F32)).astype(BF)
        cut = lambda to: self.s1.at[to] if self.x_first else self.s1.at[:, :, to]
        self.send(self.axis(self.x_first), cut, self.r2, 0)

    def hop2(self):
        p = self.place
        own = self.s1[p.x] if self.x_first else self.s1[:, :, p.y]
        self.s2[...] = self.add(self.axis(self.x_first), own, self.r2, 0).astype(BF)
        cut = lambda to: self.s2.at[:, to] if self.x_first else self.s2.at[to]
        self.send(self.axis(not self.x_first), cut, self.r3, p.X)

    def hop3(self):
        p = self.place
        own = self.s2[:, p.y] if self.x_first else self.s2[p.x]
        self.s3[...] = self.add(self.axis(not self.x_first), own, self.r3, p.X).astype(BF)
        self.send((p.Z, p.z, lambda v: p.dev(z=v)), lambda to: self.s3.at[to], self.r4, 2 * p.X)

    def hop4(self):
        p = self.place
        self.final[...] = self.add((p.Z, p.z, None), self.s3[p.z], self.r4, 2 * p.X)


class Chunk:
    def __init__(self, place, g, dx, cc, source, bufs, recv, sends):
        self.place, self.dx, self.cc, self.sends = place, dx, cc, sends
        r1, rx, r2 = bufs
        self.source, self.r1, self.rx, self.r2 = source.at[g], r1.at[g, dx], rx.at[g], r2.at[g]
        self.recv = recv.at[g]

    def mine(self):
        return self.place.c == self.cc

    def hop0(self):
        p = self.place
        x = lax.rem(p.x + self.dx, p.X)
        self.sends.push(
            self.source.at[self.cc, x], self.r1, self.recv.at[self.dx], p.dev(c=self.cc), lambda: self.r1,
            lambda: self.place.c != self.cc,
        )

    def hop1(self):
        pl.when(self.mine())(self.pass_on)

    def pass_on(self):
        p = self.place
        x = lax.rem(p.x + self.dx, p.X)
        arrived(p, self.r1, self.recv.at[self.dx], self.sends.sems.at[0])
        total = self.source[self.cc, x].astype(F32) + self.r1[...].astype(F32)
        if self.dx:
            self.source[self.cc, x] = total.astype(BF)
            self.sends.push(
                self.source.at[self.cc, x], self.rx.at[self.dx - 1], self.recv.at[p.X + self.dx], p.dev(x=x),
                lambda: self.r1, given=self.mine,
            )
            return
        for d in range(1, p.X):
            arrived(p, self.rx.at[d - 1], self.recv.at[p.X + d], self.sends.sems.at[0])
            total = total + self.rx[d - 1].astype(F32)
        self.source[self.cc, x] = total.astype(BF)
        for d in range(1, p.batches):
            j = lax.rem(p.j + d, p.batches)
            self.sends.push(
                self.source.at[self.cc, x, j], self.r2.at[d - 1], self.recv.at[2 * p.X + d], (j, p.x * 2 + p.c),
                lambda: self.r2.at[0], given=self.mine,
            )


def collect(place, source, r2, recv, dummy):
    total = source[place.c, place.x, place.j].astype(F32)
    for d in range(1, place.batches):
        arrived(place, r2.at[d - 1], recv.at[2 * place.X + d], dummy)
        total = total + r2[d - 1].astype(F32)
    return total


def forward_sends(X, Y, Z, groups):
    part_a = groups * (Z - 1 + Z * (Y - 1)) + (X - 1) * (1 + Z - 1 + Y - 1) + X
    part_b = (X - 1) + (Y - 1) + (Z - 1) + 1 + (Z - 1) * (X + Y - 1)
    part_b += Z * (2 * (X - 1) * (Y - 1) + (X - 1) + (Y - 1) + (X - 1) * (Y - 1))
    return part_a + part_b


def backward_sends(X, Y, Z, groups):
    stages = 1 + sum(len(bits(v)) for v in (X, Y, Z))
    return 2 * groups * (X + Y + Z - 2) + groups * 2 * (X + X - 1 + Y * Z - 1) + stages


def layer_kernel(
    batches, heads, owner_ref, lengths_ref, gain_ref, bias_ref, post_in, weight_in, dual_in, pc_in, dc_in,
    post_out, dual_out, dpost_out, grad_ref, norm_out, p_hbm,
    post_ref, weight_ref, dual_ref, pc_ref, dc_ref, dmid_ref, dpre_ref, recip_ref, pick_ref, xs_ref, xst_ref, ga_ref, gb_ref, qk_ref, vx_ref, wide_ref, linv_ref, at_ref, dat_ref,
    w12_ref, wo_ref, mbt_ref, dft_ref, dbt_ref, dwo_ref, dqkv_ref,
    r1, xr2, yr2, xs2, ys2, r3, s3, r4, final, qr1, qrx, qr2, norm_send, norm_recv,
    recv_z, recv_y, recv_x, core_a, recv_b, send_f, recv_f, recv_q, norm_sems, send_r, p_sems, in_sems, out_sems,
):
    place = Place(batches, heads)
    groups, rows = NHEADS // heads, D // batches
    parts = 2 * groups
    X, Y, Z = place.X, place.Y, place.Z
    c, x, y, z = place.c, place.x, place.y, place.z
    sends = Sends(send_f)
    dummy = send_f.at[0]
    length = lengths_ref[lax.axis_index("head")]
    ins = ((weight_in, weight_ref), (post_in, post_ref), (pc_in, pc_ref), (dc_in, dc_ref), (dual_in, dual_ref))

    def load(k):
        return pltpu.make_async_copy(*ins[k], in_sems.at[k])

    def core_push_a(xx):
        ref = ga_ref.at[c, xx]
        sends.push(ref, ref, core_a.at[xx], place.dev(c=1 - c), lambda: ga_ref.at[0, 0])

    def got_b(cc, xx, zz, yy):
        arrived(place, gb_ref.at[:, cc, xx, zz, yy], recv_b.at[cc, xx, zz, yy], dummy)

    def push_b(xx, zz, yy, device, cond=None):
        ref = gb_ref.at[:, c, xx, zz, yy]
        sends.push(ref, ref, recv_b.at[c, xx, zz, yy], device, lambda: gb_ref.at[:, 0, 0, 0, 0], cond)

    def side(offset):
        zo = lax.rem(z + offset, Z)
        low = lambda: lax.rem(place.z + offset, Z) < (3 * Z) // 4
        for xx in place.xs:
            got_b(c, xx, zo, y)
            for yy in place.ys:
                push_b(xx, zo, y, place.dev(y=yy), low)
            push_b(xx, zo, y, place.dev(c=1 - c))
        for yy in place.ys:
            got_b(c, x, zo, yy)
            for xx in place.xs:
                push_b(x, zo, yy, place.dev(x=xx), lambda: jnp.logical_not(low()))
            push_b(x, zo, yy, place.dev(c=1 - c))

    def spread(act, offset):
        for d in [d for d in range(Z) if d == offset or (offset == Z - 1 and d >= offset) or (offset == 1 and 0)]:
            zz = lax.rem(z + d, Z)
            if act == "send":
                push_b(x, z, y, place.dev(z=zz))
            elif act == "side":
                side(d)
            else:
                got_b(c, x, zz, y)
                for xx in place.xs:
                    push_b(x, zz, y, place.dev(x=xx))
                for yy in place.ys:
                    push_b(x, zz, y, place.dev(y=yy))
                push_b(x, zz, y, place.dev(c=1 - c))

    for n in range(len(ins)):
        load(n).start()
    load(0).wait()
    weight = weight_ref[...]
    for g in range(groups):
        ga_ref[c, x, z, y, g] = weight[:, g * GROUPW : g * GROUPW + PART].astype(BF)
    peers = [place.dev(z=zz, y=yy) for zz in [z] + place.zs for yy in [y] + place.ys][1:]
    place.greet(peers + [place.dev(x=xx) for xx in place.xs] + [place.dev(c=1 - c)])
    for g in range(groups):
        own = ga_ref.at[c, x, z, y, g]
        for zz in place.zs:
            sends.push(own, own, recv_z.at[g, z], place.dev(z=zz), lambda: ga_ref.at[0, 0, 0, 0, 0])
        for yy in place.ys:
            sends.push(own, own, recv_y.at[g, z, y], place.dev(y=yy), lambda: ga_ref.at[0, 0, 0, 0, 0])
    own = ga_ref.at[c, x, z, y]
    for xx in place.xs:
        sends.push(own, own, recv_x.at[x, z], place.dev(x=xx), lambda: ga_ref.at[0, 0, 0, 0])
    for k in range(parts):
        low = (k % groups) * GROUPW + (2 - k // groups) * PART
        gb_ref[k, c, x, z, y] = weight[:, low : low + PART].astype(BF)
    for act, offset in B_PLAN["first"]:
        spread(act, offset)
    for yy in place.ys:
        push_b(x, z, y, place.dev(y=yy))
    for xx in place.xs:
        push_b(x, z, y, place.dev(x=xx))
    load(1).wait()
    lane = lax.broadcasted_iota(jnp.int32, (1, D), 1)
    source = lane % rows
    for b in range(batches):
        source = jnp.where(lane // rows == b, source + owner_ref[b] * rows, source)
    pick = (lax.broadcasted_iota(jnp.int32, (D, D), 0) == source).astype(F32).astype(BF)
    pick_ref[...] = pick
    ordered = dot(post_ref[...], pick, 1, 0).astype(BF)
    xs_ref[...] = ordered
    xst_ref[...] = ordered.T
    for g in range(groups):
        for zz in place.zs:
            block = ga_ref.at[c, x, zz, y, g]
            arrived(place, block, recv_z.at[g, zz], dummy)
            for yy in place.ys:
                sends.push(block, block, recv_y.at[g, zz, y], place.dev(y=yy), lambda: ga_ref.at[0, 0, 0, 0, 0])
    for act, offset in B_PLAN["after"]:
        spread(act, offset)
    for xx in place.xs:
        for zz in place.zs:
            block = ga_ref.at[c, x, zz, y]
            sends.push(block, block, recv_x.at[x, zz], place.dev(x=xx), lambda: ga_ref.at[0, 0, 0, 0])
    push_b(x, z, y, place.dev(c=1 - c))


    def forward_transfers(t):
        if t < groups:
            for zz in range(Z):
                for yy in place.ys:
                    arrived(place, ga_ref.at[c, x, zz, yy, t], recv_y.at[t, zz, yy], dummy)
        if t == groups - 1:
            for yy in place.ys:
                column = ga_ref.at[c, x, :, yy]
                for xx in place.xs:
                    sends.push(column, column, recv_x.at[x, Z + yy], place.dev(x=xx), lambda: ga_ref.at[0, 0, :, 0])
            core_push_a(x)
        if t and t % groups == 0:
            k = t // groups
            xx = lax.rem(x + k // 2, X)
            if k % 2 == 0:
                for zz in [z] + place.zs:
                    arrived(place, ga_ref.at[c, xx, zz, y], recv_x.at[xx, zz], dummy)
                for yy in place.ys:
                    arrived(place, ga_ref.at[c, xx, :, yy], recv_x.at[xx, Z + yy], dummy)
                core_push_a(xx)
            else:
                arrived(place, ga_ref.at[1 - c, xx], core_a.at[xx], dummy)
        for act, offset in B_PLAN[t]:
            spread(act, offset)

    def p_store(i):
        slot = lax.rem(i, 4)
        return pltpu.make_async_copy(wide_ref.at[pl.ds(2 * slot, 2)], p_hbm.at[i], p_sems.at[slot])

    def p_fetch(i):
        g, r = i // heads, i % heads
        dx, cc = X - 1 - r // 2, r % 2
        spot = (2 * dx + (cc + c) % 2) * groups + g
        slot = lax.rem(i, 2)
        return pltpu.make_async_copy(p_hbm.at[spot], wide_ref.at[pl.ds(2 * slot, 2)], p_sems.at[slot])

    @pl.loop(0, NHEADS)
    def _(step):
        for t in range(NHEADS):
            pl.when(step == t)(functools.partial(forward_transfers, t))

        @pl.when(step >= 4)
        def _():
            p_store(step - 4).wait()

        q, g = step // groups, step % groups
        cc, xx = (c + q) % 2, lax.rem(x + q // 2, X)
        head = (xx * 2 + cc) * groups + g
        w = ga_ref[cc, xx, :, :, g].reshape(D, PART)
        proj = dot(xs_ref[...], w, 1, 0)
        lane = lax.broadcasted_iota(jnp.int32, (SEQ_LEN, 128), 1)
        qk = proj[:, :128].astype(BF)
        qk = jnp.where(lane < DH, qk * BF(DH**-0.5), qk)
        v = proj[:, 128:].astype(BF)
        vx = jnp.where(lane < DH, v, jnp.where(lane < DH + 2, BF(1), BF(0)))
        qk_ref[head] = qk
        vx_ref[head] = vx
        q_only = jnp.where(lane < DH, qk, BF(0))
        kq = jnp.concatenate([qk[:, DH:], qk[:, :DH]], axis=1)
        vxt = vx.T[: DH + 8]
        keep = lax.broadcasted_iota(jnp.int32, (SEQ_LEN, 1), 0) < length
        s = dot(kq, q_only, 1, 1)
        s = jnp.where(keep, s, F32(MASK_VALUE))
        m = jnp.max(s, axis=0, keepdims=True)
        p = jnp.exp(s - m).astype(BF)
        slot = lax.rem(step, 4)
        wide_ref[2 * slot] = p[:, : SEQ_LEN // 2]
        wide_ref[2 * slot + 1] = p[:, SEQ_LEN // 2 :]
        o = dot(vxt, p, 1, 0)
        r = 1.0 / o[DH : DH + 1]
        linv_ref[head] = r
        at_ref[head] = (o[:DH] * r).astype(BF)
        p_store(step).start()

    reduce_sends = Sends(send_r)
    pieces = []
    for k in range(parts):
        x_first = k in X_FIRST
        bufs = (r1.at[k], xr2.at[k], xs2.at[k]) if x_first else (r1.at[k], yr2.at[k], ys2.at[k])
        bufs += tuple(b.at[k] for b in (r3, s3, r4, final))
        pieces.append(Piece(place, gb_ref.at[k], x_first, bufs, recv_f.at[k], reduce_sends))
    chunks = [
        Chunk(place, g, dx, cc, dqkv_ref, (qr1, qrx, qr2), recv_q, reduce_sends)
        for g in range(groups)
        for dx in reversed(range(X))
        for cc in range(2)
    ]
    partners = [place.dev(c=1 - c)]
    flip = lambda v, b: v + b - 2 * b * ((v // b) % 2)
    partners += [place.dev(x=flip(x, b)) for b in bits(X)]
    partners += [place.dev(y=flip(y, b)) for b in bits(Y)]
    partners += [place.dev(z=flip(z, b)) for b in bits(Z)]

    def norm_push(k):
        reduce_sends.push(norm_send.at[k], norm_recv.at[k], norm_sems.at[k], partners[k], lambda: norm_send.at[0])

    def norm_pull(k):
        arrived(place, norm_recv.at[k], norm_sems.at[k], send_r.at[0])
        norm_send[k + 1] = norm_send[k] + norm_recv[k]

    for i in range(NHEADS - 4, NHEADS):
        p_store(i).wait()
    for n in range(2, len(ins)):
        load(n).wait()
    held = []
    for b in range(batches):
        found = 0
        for j in range(1, batches):
            found = jnp.where(owner_ref[j] == b, j, found)
        held.append(found)
    for b in range(batches):
        there = slice(b * rows, (b + 1) * rows)
        for h in range(NHEADS):
            g, xx, cc = h % groups, (h // groups) // 2, (h // groups) % 2
            wo_ref[there, h * DH : (h + 1) * DH] = ga_ref[cc, xx, held[b] // Y, held[b] % Y, g][:, 3 * DH :]
    norm_send[0] = jnp.zeros((4, D), F32)

    block = SEQ_LEN // MID_STEPS
    outs = ((pc_ref, post_out), (dual_ref, dual_out))

    def store(n, t):
        here = pl.ds(pl.multiple_of(t * block, block), block)
        return pltpu.make_async_copy(outs[n][0].at[here], outs[n][1].at[here], out_sems.at[n, t])

    def block_of(t):
        return pl.ds(pl.multiple_of(t * block, block), block)

    def kept(t):
        return t * block + lax.broadcasted_iota(jnp.int32, (block, 1), 0) < length

    gain, bias = gain_ref[...], bias_ref[...]
    zero = jnp.zeros((1, D), F32)

    def over_tokens(value):
        return jnp.sum(value, axis=0, keepdims=True)

    @pl.loop(0, MID_STEPS, unroll=UNROLL)
    def _(t):
        here = block_of(t)
        branch = dot(at_ref[:, :, here].reshape(D, block), wo_ref[...], 0, 1)
        middle, n1, recip = norm_forward(post_ref[here, :].astype(F32) + branch, gain[0:1], bias[0:1])
        dual_ref[here, :] = dual_ref[here, :] + branch
        dmid_ref[here, :] = n1
        recip_ref[here, :] = recip
        middle_low = middle.astype(BF)
        post_ref[here, :] = middle_low
        mbt_ref[:, here] = dot(pick_ref[...], middle_low, 0, 1).astype(BF)

    for offset in range(Z):
        zz = lax.rem(z + offset, Z)
        for yy in place.ys:
            for xx in place.xs:
                got_b(c, xx, zz, yy)
                push_b(xx, zz, yy, place.dev(c=1 - c))
    for xx in range(X):
        for zz in range(Z):
            for yy in range(Y):
                got_b(1 - c, xx, zz, yy)
    for b in range(batches):
        there = slice(b * rows, (b + 1) * rows)
        for h in range(NHEADS):
            g, xx, cc = h % groups, (h // groups) // 2, (h // groups) % 2
            for k in range(2):
                w12_ref[1 - k, there, h * PART : (h + 1) * PART] = gb_ref[
                    k * groups + g, cc, xx, held[b] // Y, held[b] % Y
                ]

    @pl.loop(0, MID_STEPS, unroll=UNROLL)
    def _(t):
        here = block_of(t)
        pre = dot(post_ref[here, :], w12_ref[0], 1, 0)
        cdf = 0.5 + 0.5 * lax.erf(pre * F32(math.sqrt(0.5)))
        density = jnp.exp(pre * pre * F32(-0.5)) * F32(1.0 / math.sqrt(2.0 * math.pi))
        hidden = (pre * cdf).astype(BF)
        slope = (cdf + pre * density).astype(BF)
        for k in range(4):
            wide_ref[k, here, :] = hidden[:, k * 512 : (k + 1) * 512]
            wide_ref[4 + k, here, :] = slope[:, k * 512 : (k + 1) * 512]

    @pl.loop(0, MID_STEPS, unroll=UNROLL)
    def _(t):
        here = block_of(t)
        hidden = jnp.concatenate([wide_ref[k, here, :] for k in range(4)], axis=1)
        feed = dot(hidden, w12_ref[1], 1, 1)
        out, n2, recip = norm_forward(dmid_ref[here, :] * gain[0:1] + bias[0:1] + feed, gain[1:2], bias[1:2])
        dual_ref[here, :] = dual_ref[here, :] + feed
        d_out = jnp.where(kept(t), pc_ref[here, :].astype(F32), 0.0)
        d_dual = jnp.where(kept(t), dc_ref[here, :].astype(F32), 0.0)
        pc_ref[here, :] = out.astype(BF)
        store(0, t).start()
        store(1, t).start()
        d_pre = norm_back(d_out, n2, recip, gain[1:2])
        dpre_ref[here, :] = d_pre
        d_feed = (d_pre + d_dual).astype(BF)
        post_ref[here, :] = d_feed
        dft_ref[:, here] = dot(pick_ref[...], d_feed, 0, 1).astype(BF)
        norm_send[0] = norm_send[0] + jnp.concatenate([zero, over_tokens(d_out * n2), zero, over_tokens(d_out)], axis=0)

    def weight_piece(k):
        left = (dft_ref if k < groups else mbt_ref)[...]
        for device in range(heads):
            h = device * groups + k % groups
            held = wide_ref[4 * (k // groups) + h // 2, :, (h % 2) * PART : (h % 2 + 1) * PART]
            grad = dot(left, held, 1, 0).astype(BF)
            gb_ref[k, device % 2, device // 2] = grad.reshape(Z, Y, rows, PART)
        pieces[k].hop0()

    sends.drain(place)
    for k in range(groups):
        weight_piece(k)
    p_fetch(0).start()
    p_fetch(1).start()

    @pl.loop(0, MID_STEPS, unroll=UNROLL)
    def _(t):
        here = block_of(t)
        d_hidden = dot(post_ref[here, :], w12_ref[1], 1, 0)
        slope = jnp.concatenate([wide_ref[4 + k, here, :] for k in range(4)], axis=1)
        d_hidden_pre = (d_hidden * slope.astype(F32)).astype(BF)
        for k in range(4):
            wide_ref[4 + k, here, :] = d_hidden_pre[:, k * 512 : (k + 1) * 512]
        d_middle = dpre_ref[here, :] + dot(d_hidden_pre, w12_ref[0], 1, 1)
        n1 = dmid_ref[here, :]
        d_mid = norm_back(d_middle, n1, recip_ref[here, :], gain[0:1])
        dmid_ref[here, :] = d_mid
        d_branch = (d_mid + jnp.where(kept(t), dc_ref[here, :].astype(F32), 0.0)).astype(BF)
        dbt_ref[:, here] = dot(pick_ref[...], d_branch, 0, 1).astype(BF)
        dat_ref[:, :, here] = dot(wo_ref[...], d_branch, 0, 1).astype(BF).reshape(NHEADS, DH, block)
        norm_send[0] = norm_send[0] + jnp.concatenate(
            [over_tokens(d_middle * n1), zero, over_tokens(d_middle), zero], axis=0
        )
        for k in range(groups):
            pl.when(t == k)(pieces[k].hop1)

    norm_push(0)
    for k in range(groups, parts):
        weight_piece(k)
    dwo = dot(dbt_ref[...], at_ref[...].reshape(D, SEQ_LEN), 1, 1).astype(BF)
    empty = jnp.zeros((D, DH), BF)
    for h in range(NHEADS):
        dwo_ref[h] = jnp.concatenate([empty, dwo[:, h * DH : (h + 1) * DH]], axis=1)

    half = parts // 2
    todo = [[] for _ in range(NHEADS)]
    for n, chunk in enumerate(chunks):
        todo[n].append(chunk.hop0)
        if n + 1 < len(chunks):
            todo[n + 1].append(chunk.hop1)
    early, late = pieces[:half], pieces[half:]
    todo[0] += [p.hop1 for p in late] + [lambda: norm_pull(0), lambda: norm_push(1)]
    todo[0] += [p.hop2 for p in early]
    todo[2] += [lambda: norm_pull(1), lambda: norm_push(2)]
    todo[2] += [p.hop3 for p in early]
    todo[3] += [p.hop2 for p in late]
    todo[4] += [p.hop4 for p in early] + [lambda: norm_pull(2), lambda: norm_push(3)]
    todo[5] += [p.hop3 for p in late]
    todo[6] += [lambda: norm_pull(3), lambda: norm_push(4)]

    def backward_transfers(t):
        for act in todo[t]:
            act()

    @pl.loop(0, NHEADS)
    def _(i):
        p_fetch(i).wait()
        g, r = i // heads, i % heads
        cc, xx = r % 2, lax.rem(x + X - 1 - r // 2, X)
        head = (xx * 2 + cc) * groups + g
        lane = lax.broadcasted_iota(jnp.int32, (SEQ_LEN, 128), 1)
        row = lax.broadcasted_iota(jnp.int32, (DH, SEQ_LEN), 0)
        qk, vx = qk_ref[head], vx_ref[head]
        do = dat_ref[head].astype(F32) * linv_ref[head]
        inner = -jnp.sum(do * at_ref[head].astype(F32), axis=0, keepdims=True)
        coarse = inner.astype(BF).astype(F32)
        tail = jnp.where(row == 0, coarse, jnp.where(row == 1, inner - coarse, 0.0))
        et = jnp.concatenate([do, tail], axis=0).astype(BF)
        e = et.T
        kt = qk.T[DH:]
        kq = jnp.concatenate([qk[:, DH:], qk[:, :DH]], axis=1)
        dk = jnp.zeros((SEQ_LEN, 128), F32)
        dv = jnp.zeros((SEQ_LEN, 128), F32)
        dqs = []
        slot = lax.rem(i, 2)
        for b in range(2):
            sl = slice(b * (SEQ_LEN // 2), (b + 1) * (SEQ_LEN // 2))
            p = wide_ref[2 * slot + b]
            ds = (p.astype(F32) * dot(vx, et[:, sl], 1, 0)).astype(BF)
            dv = dv + dot(p, e[sl], 1, 0)
            dk = dk + dot(ds, kq[sl], 1, 0)
            dqs.append(dot(kt, ds, 1, 0))
        dqt = jnp.concatenate(dqs, axis=1) * F32(DH**-0.5)
        dq = jnp.concatenate([dqt, jnp.zeros_like(dqt)], axis=0).T
        d_proj = jnp.concatenate([jnp.where(lane < DH, dq, dk), jnp.where(lane < DH, dv, 0.0)], axis=1).astype(BF)
        cols = pl.ds(pl.multiple_of(head * PART, PART), PART)
        w12_ref[0, :, cols] = d_proj[: SEQ_LEN // 2]
        w12_ref[1, :, cols] = d_proj[SEQ_LEN // 2 :]
        dw = dot(xst_ref[...], d_proj, 1, 0)
        dw = jnp.concatenate([dw[:, :128], dw[:, 128:] + dwo_ref[head].astype(F32)], axis=1).astype(BF)
        dqkv_ref[g, cc, xx] = dw.reshape(dqkv_ref.shape[3:])

        @pl.when(i + 2 < NHEADS)
        def _():
            p_fetch(i + 2).start()

        for t in range(NHEADS):
            pl.when(i == t)(functools.partial(backward_transfers, t))

    for k in range(4, len(partners)):
        norm_pull(k)
        if k + 1 < len(partners):
            norm_push(k + 1)
    norm_out[...] = norm_send[len(partners)]
    chunks[-1].hop1()
    table = []
    for h in range(NHEADS):
        g, xx, cc = h % groups, (h // groups) // 2, (h // groups) % 2
        table.append(ga_ref[cc, xx, :, :, g].reshape(D, PART))
    table = jnp.concatenate(table, axis=1)
    dpost = []
    for k in range(2):
        here = slice(k * (SEQ_LEN // 2), (k + 1) * (SEQ_LEN // 2))
        ordered = dot(w12_ref[k], table, 1, 1).astype(BF)
        dmid_ref[here, :] = dmid_ref[here, :] + dot(ordered, pick_ref[...], 1, 1)
        dpost.append(pltpu.make_async_copy(dmid_ref.at[here], dpost_out.at[here], in_sems.at[k]))
        dpost[k].start()
    for piece in pieces[len(pieces) // 2 :]:
        piece.hop4()
    for g in range(groups):
        low = g * GROUPW
        grad_ref[:, low + PART : low + 2 * PART] = final[groups + g]
        grad_ref[:, low + 2 * PART : low + 3 * PART] = final[g]
        grad_ref[:, low : low + PART] = collect(place, dqkv_ref.at[g], qr2.at[g], recv_q.at[g], send_r.at[0])
    for copy in dpost:
        copy.wait()
    for n in range(len(outs)):
        for t in range(MID_STEPS):
            store(n, t).wait()
    reduce_sends.drain(place)


def layer_call(owner, lengths, gain, bias, post, weights, dual, pc, dc, batches, heads):
    groups, rows = NHEADS // heads, D // batches
    parts = 2 * groups
    X = Y = heads // 2
    Z = batches // Y
    tokens = post.shape[0]
    assert tokens == SEQ_LEN
    stages = 1 + sum(len(bits(v)) for v in (X, Y, Z))
    smem, vmem = pl.BlockSpec(memory_space=pltpu.SMEM), pl.BlockSpec(memory_space=pltpu.VMEM)
    far = pl.BlockSpec(memory_space=pl.ANY)
    outs = [
        jax.ShapeDtypeStruct((tokens, D), BF),
        jax.ShapeDtypeStruct((tokens, D), F32),
        jax.ShapeDtypeStruct((tokens, D), F32),
        jax.ShapeDtypeStruct((rows, groups * GROUPW), F32),
        jax.ShapeDtypeStruct((4, D), F32),
        jax.ShapeDtypeStruct((NHEADS, 2, tokens, tokens // 2), BF),
    ]
    dma = pltpu.SemaphoreType.DMA
    return pl.pallas_call(
        functools.partial(layer_kernel, batches, heads),
        in_specs=[smem, smem, vmem, vmem] + [far] * 5,
        out_specs=[far, far, far, vmem, vmem, far],
        out_shape=outs,
        scratch_shapes=[
            pltpu.VMEM((tokens, D), BF),
            pltpu.VMEM(weights.shape, F32),
            pltpu.VMEM((tokens, D), F32),
            pltpu.VMEM((tokens, D), BF),
            pltpu.VMEM((tokens, D), BF),
            pltpu.VMEM((tokens, D), F32),
            pltpu.VMEM((tokens, D), F32),
            pltpu.VMEM((tokens, 1), F32),
            pltpu.VMEM((D, D), BF),
            pltpu.VMEM((tokens, D), BF),
            pltpu.VMEM((D, tokens), BF),
            pltpu.VMEM((2, X, Z, Y, groups, rows, PART), BF),
            pltpu.VMEM((parts, 2, X, Z, Y, rows, PART), BF),
            pltpu.VMEM((NHEADS, tokens, 128), BF),
            pltpu.VMEM((NHEADS, tokens, 128), BF),
            pltpu.VMEM((8, tokens, tokens // 2), BF),
            pltpu.VMEM((NHEADS, 1, tokens), F32),
            pltpu.VMEM((NHEADS, DH, tokens), BF),
            pltpu.VMEM((NHEADS, DH, tokens), BF),
            pltpu.VMEM((2, D, FF), BF),
            pltpu.VMEM((D, D), BF),
            pltpu.VMEM((D, tokens), BF),
            pltpu.VMEM((D, tokens), BF),
            pltpu.VMEM((D, tokens), BF),
            pltpu.VMEM((NHEADS, D, 128), BF),
            pltpu.VMEM((groups, 2, X, batches, rows, PART), BF),
            pltpu.VMEM((parts, X, Z, Y, rows, PART), BF),
            pltpu.VMEM((parts, X - 1, Z, Y, rows, PART), BF),
            pltpu.VMEM((parts, Y - 1, X, Z, rows, PART), BF),
            pltpu.VMEM((parts, Z, Y, rows, PART), BF),
            pltpu.VMEM((parts, X, Z, rows, PART), BF),
            pltpu.VMEM((parts, X - 1, Z, rows, PART), BF),
            pltpu.VMEM((parts, Z, rows, PART), BF),
            pltpu.VMEM((parts, Z - 1, rows, PART), BF),
            pltpu.VMEM((parts, rows, PART), F32),
            pltpu.VMEM((groups, X, batches, rows, PART), BF),
            pltpu.VMEM((groups, X - 1, batches, rows, PART), BF),
            pltpu.VMEM((groups, batches - 1, rows, PART), BF),
            pltpu.VMEM((stages + 1, 4, D), F32),
            pltpu.VMEM((stages, 4, D), F32),
            dma((groups, Z)),
            dma((groups, Z, Y)),
            dma((X, Z + Y)),
            dma((X,)),
            dma((2, X, Z, Y)),
            dma((forward_sends(X, Y, Z, groups),)),
            dma((parts, 2 * X + Z)),
            dma((groups, 2 * X + batches)),
            dma((stages,)),
            dma((backward_sends(X, Y, Z, groups),)),
            dma((4,)),
            dma((5,)),
            dma((2, MID_STEPS)),
        ],
        name="layer",
        compiler_params=pltpu.CompilerParams(
            collective_id=1, has_side_effects=True, vmem_limit_bytes=VMEM_BYTES
        ),
    )(owner, lengths, gain, bias, post, weights, dual, pc, dc)


def update_kernel(
    post_in, dual_in, dpost_in, grad_ref, weight_ref, first_ref, second_ref,
    ngrad_ref, gain_ref, bias_ref, nfirst_ref, nsecond_ref,
    post_out, dual_out, dpost_out, first_out, second_out, weight_out, nfirst_out, nsecond_out, nparam_out,
):
    post_out[...] = post_in[...]
    dual_out[...] = dual_in[...]
    dpost_out[...] = dpost_in[...]
    first_out[...], second_out[...], weight_out[...] = adam_update(
        weight_ref[...], grad_ref[...], first_ref[...], second_ref[...], WEIGHT_RATE, WEIGHT_DECAY
    )
    nparam = jnp.concatenate([gain_ref[...], bias_ref[...]], axis=0)
    nfirst_out[...], nsecond_out[...], nparam_out[...] = adam_update(
        nparam, ngrad_ref[...], nfirst_ref[...], nsecond_ref[...], NORM_RATE, 0.0
    )


def update_call(post, dual, dpost, grad, weights, first, second, ngrad, gain, bias, nfirst, nsecond):
    steps = 2
    cut = lambda a: pl.BlockSpec((a.shape[0] // steps, a.shape[1]), lambda i: (i, 0))
    same = lambda a: pl.BlockSpec(a.shape, lambda i: (0, 0))
    outs = [post, dual, dpost, weights, weights, weights, nfirst, nfirst, nfirst]
    return pl.pallas_call(
        update_kernel,
        grid=(steps,),
        in_specs=[cut(a) for a in (post, dual, dpost, grad, weights, first, second)]
        + [same(a) for a in (ngrad, gain, bias, nfirst, nsecond)],
        out_specs=[cut(a) for a in outs[:6]] + [same(a) for a in outs[6:]],
        out_shape=[jax.ShapeDtypeStruct(a.shape, a.dtype) for a in outs],
        name="update",
        compiler_params=pltpu.CompilerParams(vmem_limit_bytes=VMEM_BYTES),
    )(post, dual, dpost, grad, weights, first, second, ngrad, gain, bias, nfirst, nsecond)


def shards(
    post_stream,
    dual_stream,
    post_cotangent,
    dual_cotangent,
    seq_lengths,
    owner_slots,
    weights,
    first_moment,
    second_moment,
    norm_gain,
    norm_bias,
    norm_first,
    norm_second,
):
    batches, heads = lax.axis_size("batch"), lax.axis_size("head")
    post, dual, dpost, grad, norm_grad, _ = layer_call(
        owner_slots, seq_lengths, norm_gain, norm_bias, post_stream, weights, dual_stream, post_cotangent,
        dual_cotangent, batches, heads,
    )
    return update_call(
        post, dual, dpost, grad, weights, first_moment, second_moment,
        norm_grad, norm_gain, norm_bias, norm_first, norm_second,
    )


def solution(mesh):
    tokens, table, copied = P(("batch", "head"), None), P("batch", "head"), P()
    in_specs = (tokens,) * 4 + (P("batch"), copied) + (table,) * 3 + (copied,) * 4
    out_specs = (tokens,) * 3 + (table,) * 3 + (copied,) * 3
    return jax.shard_map(shards, mesh=mesh, in_specs=in_specs, out_specs=out_specs, check_vma=False)
```

time: 129 us -> 113 us (0.88)
  Pallas kernels: 126 us -> 111 us
    pallas_call x1, Pallas kernels: 121 us -> 106 us  [layer_call(): pl.pallas_call(functools.partial(layer_kernel, batches, heads), in_specs=...]
where the time goes in v4:
time: 113 us; the launch traced here: 112 us
  Pallas kernels  111 us (98%)
    pallas_call x1, Pallas kernels, layer_call(): pl.pallas_call(functools.partial(layer_kernel, batches, heads), in_specs=...  106 us
    pallas_call x1, Pallas kernels, update_call(): pl.pallas_call(update_kernel, grid=(steps,), in_specs=[cut(a) for a in (p...  5.15 us

profile of v4, /device:TPU:0, one launch (start us, length us, event | category | flops | bytes accessed | tf_op | source)
XLA Modules:
  0.0 111.6 jit_solution(16933861460448113253)
XLA Ops:
  0.6 105.6 %layer.1 = (bf16[1024,512]{1,0:T(8,128)(2,1)}, f32[1024,512]{1,0:T(8,128)}, f32[1024,512]{1,0:T(8,128)}, f32[64,1536]{1,0:T(8,128)}, f32[4,512]{1,0:T(4,128)}, /*index=5*/bf16[8,2,1024,512]{3,2,1,0:T(8,128)(2,1)}) custom-call(s32[8]{0:T(128)} %owner_ref.1, s32[4]{0:T(128)} %lengths_ref.1, f32[2,512]{1,0:T(2,128)} %gain_ref.3, f32[2,512]{1,0:T(2,128)} %bias_ref.3, ...), custom_call_target="tpu_custom_call" | custom-call | tf_op jit(solution)/shard_map/layer/pallas_call | solution.py:722
  106.2 5.1 %update.1 = (bf16[1024,512]{1,0:T(8,128)(2,1)}, f32[1024,512]{1,0:T(8,128)}, f32[1024,512]{1,0:T(8,128)}, f32[64,1536]{1,0:T(8,128)}, f32[64,1536]{1,0:T(8,128)}...) custom-call(bf16[1024,512]{1,0:T(8,128)(2,1)} %get-tuple-element.14.post_in, ...), custom_call_target="tpu_custom_call" | custom-call | tf_op jit(solution)/shard_map/update/pallas_call | solution.py:811

commit v5 on v4

--- a/solution.py
+++ b/solution.py
@@ -33,6 +33,7 @@
 B_PLAN = {'first': [], 'after': [('send', 1), ('send', 2), ('send', 3)], 0: [], 1: [], 2: [('side', 0)], 3: [('pass', 1), ('pass', 2), ('pass', 3)], 4: [], 5: [('side', 1)], 6: [('side', 2)], 7: [('side', 3)]}
 MID_STEPS = 2
 UNROLL = 2
+REDUCE_PLAN = ((0, 'hop1', 1), (0, 'hop2', 0), (2, 'hop3', 0), (3, 'hop2', 1), (4, 'hop4', 0), (5, 'hop3', 1))
 X_FIRST = (0, 2)
 
 
@@ -64,7 +65,9 @@
         barrier = pltpu.get_barrier_semaphore()
         for device in devices:
             pl.semaphore_signal(barrier, inc=1, device_id=device, device_id_type=MESH)
-        pl.semaphore_wait(barrier, len(devices))
+
+    def greeted(self, devices):
+        pl.semaphore_wait(pltpu.get_barrier_semaphore(), len(devices))
 
     def plane(self):
         return [(x, y) for x in [self.x] + self.xs for y in [self.y] + self.ys][1:]
@@ -251,7 +254,7 @@
 def layer_kernel(
     batches, heads, owner_ref, lengths_ref, gain_ref, bias_ref, post_in, weight_in, dual_in, pc_in, dc_in,
     post_out, dual_out, dpost_out, grad_ref, norm_out, p_hbm,
-    post_ref, weight_ref, dual_ref, pc_ref, dc_ref, dmid_ref, dpre_ref, recip_ref, pick_ref, xs_ref, xst_ref, ga_ref, gb_ref, qk_ref, vx_ref, wide_ref, linv_ref, at_ref, dat_ref,
+    post_ref, weight_ref, dual_ref, dc_ref, dmid_ref, dpre_ref, recip_ref, pick_ref, xs_ref, xst_ref, ga_ref, gb_ref, qk_ref, vx_ref, wide_ref, linv_ref, at_ref, dat_ref,
     w12_ref, wo_ref, mbt_ref, dft_ref, dbt_ref, dwo_ref, dqkv_ref,
     r1, xr2, yr2, xs2, ys2, r3, s3, r4, final, qr1, qrx, qr2, norm_send, norm_recv,
     recv_z, recv_y, recv_x, core_a, recv_b, send_f, recv_f, recv_q, norm_sems, send_r, p_sems, in_sems, out_sems,
@@ -264,7 +267,8 @@
     sends = Sends(send_f)
     dummy = send_f.at[0]
     length = lengths_ref[lax.axis_index("head")]
-    ins = ((weight_in, weight_ref), (post_in, post_ref), (pc_in, pc_ref), (dc_in, dc_ref), (dual_in, dual_ref))
+    pc_ref = xs_ref
+    ins = ((weight_in, weight_ref), (post_in, post_ref), (dc_in, dc_ref), (dual_in, dual_ref), (pc_in, pc_ref))
 
     def load(k):
         return pltpu.make_async_copy(*ins[k], in_sems.at[k])
@@ -309,32 +313,29 @@
                     push_b(x, zz, y, place.dev(y=yy))
                 push_b(x, zz, y, place.dev(c=1 - c))
 
-    for n in range(len(ins)):
+    peers = [place.dev(z=zz, y=yy) for zz in [z] + place.zs for yy in [y] + place.ys][1:]
+    peers += [place.dev(x=xx) for xx in place.xs] + [place.dev(c=1 - c)]
+    place.greet(peers)
+    for n in range(len(ins) - 1):
         load(n).start()
     load(0).wait()
     weight = weight_ref[...]
     for g in range(groups):
         ga_ref[c, x, z, y, g] = weight[:, g * GROUPW : g * GROUPW + PART].astype(BF)
-    peers = [place.dev(z=zz, y=yy) for zz in [z] + place.zs for yy in [y] + place.ys][1:]
-    place.greet(peers + [place.dev(x=xx) for xx in place.xs] + [place.dev(c=1 - c)])
-    for g in range(groups):
+    for k in range(parts):
+        low = (k % groups) * GROUPW + (2 - k // groups) * PART
+        gb_ref[k, c, x, z, y] = weight[:, low : low + PART].astype(BF)
+    place.greeted(peers)
+
+    def first_sends(g):
         own = ga_ref.at[c, x, z, y, g]
         for zz in place.zs:
             sends.push(own, own, recv_z.at[g, z], place.dev(z=zz), lambda: ga_ref.at[0, 0, 0, 0, 0])
         for yy in place.ys:
             sends.push(own, own, recv_y.at[g, z, y], place.dev(y=yy), lambda: ga_ref.at[0, 0, 0, 0, 0])
-    own = ga_ref.at[c, x, z, y]
-    for xx in place.xs:
-        sends.push(own, own, recv_x.at[x, z], place.dev(x=xx), lambda: ga_ref.at[0, 0, 0, 0])
-    for k in range(parts):
-        low = (k % groups) * GROUPW + (2 - k // groups) * PART
-        gb_ref[k, c, x, z, y] = weight[:, low : low + PART].astype(BF)
-    for act, offset in B_PLAN["first"]:
-        spread(act, offset)
-    for yy in place.ys:
-        push_b(x, z, y, place.dev(y=yy))
-    for xx in place.xs:
-        push_b(x, z, y, place.dev(x=xx))
+
+    for g in range(groups):
+        first_sends(g)
     load(1).wait()
     lane = lax.broadcasted_iota(jnp.int32, (1, D), 1)
     source = lane % rows
@@ -345,6 +346,15 @@
     ordered = dot(post_ref[...], pick, 1, 0).astype(BF)
     xs_ref[...] = ordered
     xst_ref[...] = ordered.T
+    own = ga_ref.at[c, x, z, y]
+    for xx in place.xs:
+        sends.push(own, own, recv_x.at[x, z], place.dev(x=xx), lambda: ga_ref.at[0, 0, 0, 0])
+    for act, offset in B_PLAN["first"]:
+        spread(act, offset)
+    for yy in place.ys:
+        push_b(x, z, y, place.dev(y=yy))
+    for xx in place.xs:
+        push_b(x, z, y, place.dev(x=xx))
     for g in range(groups):
         for zz in place.zs:
             block = ga_ref.at[c, x, zz, y, g]
@@ -438,7 +448,8 @@
     pieces = []
     for k in range(parts):
         x_first = k in X_FIRST
-        bufs = (r1.at[k], xr2.at[k], xs2.at[k]) if x_first else (r1.at[k], yr2.at[k], ys2.at[k])
+        order = sum((j in X_FIRST) == x_first for j in range(k))
+        bufs = (r1.at[k], xr2.at[order], xs2.at[order]) if x_first else (r1.at[k], yr2.at[order], ys2.at[order])
         bufs += tuple(b.at[k] for b in (r3, s3, r4, final))
         pieces.append(Piece(place, gb_ref.at[k], x_first, bufs, recv_f.at[k], reduce_sends))
     chunks = [
@@ -462,8 +473,9 @@
 
     for i in range(NHEADS - 4, NHEADS):
         p_store(i).wait()
-    for n in range(2, len(ins)):
-        load(n).wait()
+    load(4).start()
+    load(2).wait()
+    load(3).wait()
     held = []
     for b in range(batches):
         found = 0
@@ -506,7 +518,7 @@
         recip_ref[here, :] = recip
         middle_low = middle.astype(BF)
         post_ref[here, :] = middle_low
-        mbt_ref[:, here] = dot(pick_ref[...], middle_low, 0, 1).astype(BF)
+        mbt_ref[:, :, here] = middle_low.T.reshape(batches, rows, block)
 
     for offset in range(Z):
         zz = lax.rem(z + offset, Z)
@@ -539,6 +551,8 @@
             wide_ref[k, here, :] = hidden[:, k * 512 : (k + 1) * 512]
             wide_ref[4 + k, here, :] = slope[:, k * 512 : (k + 1) * 512]
 
+    load(4).wait()
+
     @pl.loop(0, MID_STEPS, unroll=UNROLL)
     def _(t):
         here = block_of(t)
@@ -555,11 +569,14 @@
         dpre_ref[here, :] = d_pre
         d_feed = (d_pre + d_dual).astype(BF)
         post_ref[here, :] = d_feed
-        dft_ref[:, here] = dot(pick_ref[...], d_feed, 0, 1).astype(BF)
+        dft_ref[:, :, here] = d_feed.T.reshape(batches, rows, block)
         norm_send[0] = norm_send[0] + jnp.concatenate([zero, over_tokens(d_out * n2), zero, over_tokens(d_out)], axis=0)
 
+    def in_slots(ref):
+        return jnp.concatenate([ref[owner_ref[j]] for j in range(batches)], axis=0)
+
     def weight_piece(k):
-        left = (dft_ref if k < groups else mbt_ref)[...]
+        left = in_slots(dft_ref if k < groups else mbt_ref)
         for device in range(heads):
             h = device * groups + k % groups
             held = wide_ref[4 * (k // groups) + h // 2, :, (h % 2) * PART : (h % 2 + 1) * PART]
@@ -586,7 +603,7 @@
         d_mid = norm_back(d_middle, n1, recip_ref[here, :], gain[0:1])
         dmid_ref[here, :] = d_mid
         d_branch = (d_mid + jnp.where(kept(t), dc_ref[here, :].astype(F32), 0.0)).astype(BF)
-        dbt_ref[:, here] = dot(pick_ref[...], d_branch, 0, 1).astype(BF)
+        dbt_ref[:, :, here] = d_branch.T.reshape(batches, rows, block)
         dat_ref[:, :, here] = dot(wo_ref[...], d_branch, 0, 1).astype(BF).reshape(NHEADS, DH, block)
         norm_send[0] = norm_send[0] + jnp.concatenate(
             [over_tokens(d_middle * n1), zero, over_tokens(d_middle), zero], axis=0
@@ -597,30 +614,28 @@
     norm_push(0)
     for k in range(groups, parts):
         weight_piece(k)
-    dwo = dot(dbt_ref[...], at_ref[...].reshape(D, SEQ_LEN), 1, 1).astype(BF)
+    dwo = dot(in_slots(dbt_ref), at_ref[...].reshape(D, SEQ_LEN), 1, 1).astype(BF)
     empty = jnp.zeros((D, DH), BF)
     for h in range(NHEADS):
         dwo_ref[h] = jnp.concatenate([empty, dwo[:, h * DH : (h + 1) * DH]], axis=1)
 
     half = parts // 2
-    todo = [[] for _ in range(NHEADS)]
+    todo = [[] for _ in range(NHEADS + 1)]
+    early, late = pieces[:half], pieces[half:]
     for n, chunk in enumerate(chunks):
         todo[n].append(chunk.hop0)
         if n + 1 < len(chunks):
             todo[n + 1].append(chunk.hop1)
-    early, late = pieces[:half], pieces[half:]
-    todo[0] += [p.hop1 for p in late] + [lambda: norm_pull(0), lambda: norm_push(1)]
-    todo[0] += [p.hop2 for p in early]
-    todo[2] += [lambda: norm_pull(1), lambda: norm_push(2)]
-    todo[2] += [p.hop3 for p in early]
-    todo[3] += [p.hop2 for p in late]
-    todo[4] += [p.hop4 for p in early] + [lambda: norm_pull(2), lambda: norm_push(3)]
-    todo[5] += [p.hop3 for p in late]
-    todo[6] += [lambda: norm_pull(3), lambda: norm_push(4)]
+    for k in range(4):
+        todo[2 * k] += [functools.partial(norm_pull, k), functools.partial(norm_push, k + 1)]
+    for t, hop, some in REDUCE_PLAN:
+        todo[t] += [getattr(p, hop) for p in (early, late)[some]]
 
     def backward_transfers(t):
         for act in todo[t]:
             act()
+
+    backward_transfers(-1)
 
     @pl.loop(0, NHEADS)
     def _(i):
@@ -719,6 +734,7 @@
         jax.ShapeDtypeStruct((NHEADS, 2, tokens, tokens // 2), BF),
     ]
     dma = pltpu.SemaphoreType.DMA
+    x_parts = sum(k < parts for k in X_FIRST)
     return pl.pallas_call(
         functools.partial(layer_kernel, batches, heads),
         in_specs=[smem, smem, vmem, vmem] + [far] * 5,
@@ -728,7 +744,6 @@
             pltpu.VMEM((tokens, D), BF),
             pltpu.VMEM(weights.shape, F32),
             pltpu.VMEM((tokens, D), F32),
-            pltpu.VMEM((tokens, D), BF),
             pltpu.VMEM((tokens, D), BF),
             pltpu.VMEM((tokens, D), F32),
             pltpu.VMEM((tokens, D), F32),
@@ -746,16 +761,16 @@
             pltpu.VMEM((NHEADS, DH, tokens), BF),
             pltpu.VMEM((2, D, FF), BF),
             pltpu.VMEM((D, D), BF),
-            pltpu.VMEM((D, tokens), BF),
-            pltpu.VMEM((D, tokens), BF),
-            pltpu.VMEM((D, tokens), BF),
+            pltpu.VMEM((batches, rows, tokens), BF),
+            pltpu.VMEM((batches, rows, tokens), BF),
+            pltpu.VMEM((batches, rows, tokens), BF),
             pltpu.VMEM((NHEADS, D, 128), BF),
             pltpu.VMEM((groups, 2, X, batches, rows, PART), BF),
             pltpu.VMEM((parts, X, Z, Y, rows, PART), BF),
-            pltpu.VMEM((parts, X - 1, Z, Y, rows, PART), BF),
-            pltpu.VMEM((parts, Y - 1, X, Z, rows, PART), BF),
-            pltpu.VMEM((parts, Z, Y, rows, PART), BF),
-            pltpu.VMEM((parts, X, Z, rows, PART), BF),
+            pltpu.VMEM((x_parts, X - 1, Z, Y, rows, PART), BF),
+            pltpu.VMEM((parts - x_parts, Y - 1, X, Z, rows, PART), BF),
+            pltpu.VMEM((x_parts, Z, Y, rows, PART), BF),
+            pltpu.VMEM((parts - x_parts, X, Z, rows, PART), BF),
             pltpu.VMEM((parts, X - 1, Z, rows, PART), BF),
             pltpu.VMEM((parts, Z, rows, PART), BF),
             pltpu.VMEM((parts, Z - 1, rows, PART), BF),

time: 113 us -> 110 us (0.973)
  Pallas kernels: 111 us -> 108 us
    pallas_call x1, Pallas kernels: 106 us -> 103 us  [layer_call(): pl.pallas_call(functools.partial(layer_kernel, batches, heads), in_specs=...]
where the time goes in v5:
time: 110 us; the launch traced here: 109 us
  Pallas kernels  108 us (98%)
    pallas_call x1, Pallas kernels, layer_call(): pl.pallas_call(functools.partial(layer_kernel, batches, heads), in_specs=...  103 us
    pallas_call x1, Pallas kernels, update_call(): pl.pallas_call(update_kernel, grid=(steps,), in_specs=[cut(a) for a in (p...  5.15 us

profile of v5, /device:TPU:0, one launch (start us, length us, event | category | flops | bytes accessed | tf_op | source)
XLA Modules:
  0.0 109.3 jit_solution(1176867917412908907)
XLA Ops:
  0.6 103.3 %layer.1 = (bf16[1024,512]{1,0:T(8,128)(2,1)}, f32[1024,512]{1,0:T(8,128)}, f32[1024,512]{1,0:T(8,128)}, f32[64,1536]{1,0:T(8,128)}, f32[4,512]{1,0:T(4,128)}, /*index=5*/bf16[8,2,1024,512]{3,2,1,0:T(8,128)(2,1)}) custom-call(s32[8]{0:T(128)} %owner_ref.1, s32[4]{0:T(128)} %lengths_ref.1, f32[2,512]{1,0:T(2,128)} %gain_ref.3, f32[2,512]{1,0:T(2,128)} %bias_ref.3, ...), custom_call_target="tpu_custom_call" | custom-call | tf_op jit(solution)/shard_map/layer/pallas_call | solution.py:738
  103.9 5.1 %update.1 = (bf16[1024,512]{1,0:T(8,128)(2,1)}, f32[1024,512]{1,0:T(8,128)}, f32[1024,512]{1,0:T(8,128)}, f32[64,1536]{1,0:T(8,128)}, f32[64,1536]{1,0:T(8,128)}...) custom-call(bf16[1024,512]{1,0:T(8,128)(2,1)} %get-tuple-element.14.post_in, ...), custom_call_target="tpu_custom_call" | custom-call | tf_op jit(solution)/shard_map/update/pallas_call | solution.py:826

commit v6 on v5

--- a/solution.py
+++ b/solution.py
@@ -539,7 +539,9 @@
                     k * groups + g, cc, xx, held[b] // Y, held[b] % Y
                 ]
 
-    @pl.loop(0, MID_STEPS, unroll=UNROLL)
+    load(4).wait()
+
+    @pl.loop(0, MID_STEPS)
     def _(t):
         here = block_of(t)
         pre = dot(post_ref[here, :], w12_ref[0], 1, 0)
@@ -550,13 +552,6 @@
         for k in range(4):
             wide_ref[k, here, :] = hidden[:, k * 512 : (k + 1) * 512]
             wide_ref[4 + k, here, :] = slope[:, k * 512 : (k + 1) * 512]
-
-    load(4).wait()
-
-    @pl.loop(0, MID_STEPS, unroll=UNROLL)
-    def _(t):
-        here = block_of(t)
-        hidden = jnp.concatenate([wide_ref[k, here, :] for k in range(4)], axis=1)
         feed = dot(hidden, w12_ref[1], 1, 1)
         out, n2, recip = norm_forward(dmid_ref[here, :] * gain[0:1] + bias[0:1] + feed, gain[1:2], bias[1:2])
         dual_ref[here, :] = dual_ref[here, :] + feed

time: 110 us -> 110 us (level)
  no operation moved by 1% of the time
where the time goes in v6:
time: 110 us; the launch traced here: 109 us
  Pallas kernels  108 us (98%)
    pallas_call x1, Pallas kernels, layer_call(): pl.pallas_call(functools.partial(layer_kernel, batches, heads), in_specs=...  103 us
    pallas_call x1, Pallas kernels, update_call(): pl.pallas_call(update_kernel, grid=(steps,), in_specs=[cut(a) for a in (p...  5.15 us

profile of v6, /device:TPU:0, one launch (start us, length us, event | category | flops | bytes accessed | tf_op | source)
XLA Modules:
  0.0 108.8 jit_solution(7393511452368678676)
XLA Ops:
  0.6 102.9 %layer.1 = (bf16[1024,512]{1,0:T(8,128)(2,1)}, f32[1024,512]{1,0:T(8,128)}, f32[1024,512]{1,0:T(8,128)}, f32[64,1536]{1,0:T(8,128)}, f32[4,512]{1,0:T(4,128)}, /*index=5*/bf16[8,2,1024,512]{3,2,1,0:T(8,128)(2,1)}) custom-call(s32[8]{0:T(128)} %owner_ref.1, s32[4]{0:T(128)} %lengths_ref.1, f32[2,512]{1,0:T(2,128)} %gain_ref.3, f32[2,512]{1,0:T(2,128)} %bias_ref.3, ...), custom_call_target="tpu_custom_call" | custom-call | tf_op jit(solution)/shard_map/layer/pallas_call | solution.py:733
  103.5 5.1 %update.1 = (bf16[1024,512]{1,0:T(8,128)(2,1)}, f32[1024,512]{1,0:T(8,128)}, f32[1024,512]{1,0:T(8,128)}, f32[64,1536]{1,0:T(8,128)}, f32[64,1536]{1,0:T(8,128)}...) custom-call(bf16[1024,512]{1,0:T(8,128)(2,1)} %get-tuple-element.14.post_in, ...), custom_call_target="tpu_custom_call" | custom-call | tf_op jit(solution)/shard_map/update/pallas_call | solution.py:821
